TPU v7x, 32 devices: a whole 2x2x4 slice. The times are simulated.
32 devices in a mesh: seq: 2 (over x), fsdp: 4 (over z), rep: 4 (over y, core).
Axes of the slice: x: 2, y: 2, z: 4, core: 2. Of those that a mesh axis runs over, the one named last changes fastest.
Arguments:
- tokens: bfloat16 [16, 1024, 1088], P(('fsdp', 'rep'), 'seq'), may hold values from -6 to 6
- segments: int32 [16, 1024], P(('fsdp', 'rep'), 'seq'), may hold values from 0 to 5, as said below
- grad_out: bfloat16 [16, 1024, 1088], P(('fsdp', 'rep'), 'seq'), may hold values from -6 to 6
- attn_gain: bfloat16 [2, 1088], P(None, 'fsdp'), may hold values from 0.099609375 to 1.8984375
- attn_shift: bfloat16 [2, 1088], P(None, 'fsdp'), may hold values from -3 to 3
- w_qkv: bfloat16 [2, 1088, 3264], P(None, 'fsdp'), may hold values from -0.1875 to 0.1875
- b_query: bfloat16 [2, 1088], P(None, 'fsdp'), may hold values from -3 to 3
- b_value: bfloat16 [2, 1088], P(None, 'fsdp'), may hold values from -3 to 3
- w_out: bfloat16 [2, 1088, 1088], P(None, 'fsdp'), may hold values from -0.5 to 0.5
- b_out: bfloat16 [2, 1088], P(None, 'fsdp'), may hold values from -3 to 3
- mlp_gain: bfloat16 [2, 1088], P(None, 'fsdp'), may hold values from 0.099609375 to 1.8984375
- mlp_shift: bfloat16 [2, 1088], P(None, 'fsdp'), may hold values from -3 to 3
- w_up: bfloat16 [2, 1088, 4352], P(None, 'fsdp'), may hold values from -0.1875 to 0.1875
- b_up: bfloat16 [2, 4352], P(None, 'fsdp'), may hold values from -3 to 3
- w_down: bfloat16 [2, 4352, 1088], P(None, 'fsdp'), may hold values from -0.09375 to 0.09375
- b_down: bfloat16 [2, 1088], P(None, 'fsdp'), may hold values from -3 to 3
Outputs:
- result: bfloat16 [16, 1024, 1088], P(('fsdp', 'rep'), 'seq')
- grad_tokens: bfloat16 [16, 1024, 1088], P(('fsdp', 'rep'), 'seq')
- grad_attn_gain: float32 [2, 1088], P(None, 'fsdp')
- grad_attn_shift: float32 [2, 1088], P(None, 'fsdp')
- grad_w_qkv: float32 [2, 1088, 3264], P(None, 'fsdp')
- grad_b_query: float32 [2, 1088], P(None, 'fsdp')
- grad_b_value: float32 [2, 1088], P(None, 'fsdp')
- grad_w_out: float32 [2, 1088, 1088], P(None, 'fsdp')
- grad_b_out: float32 [2, 1088], P(None, 'fsdp')
- grad_mlp_gain: float32 [2, 1088], P(None, 'fsdp')
- grad_mlp_shift: float32 [2, 1088], P(None, 'fsdp')
- grad_w_up: float32 [2, 1088, 4352], P(None, 'fsdp')
- grad_b_up: float32 [2, 4352], P(None, 'fsdp')
- grad_w_down: float32 [2, 4352, 1088], P(None, 'fsdp')
- grad_b_down: float32 [2, 1088], P(None, 'fsdp')
Inputs may be any that keep to these rules, and one draw needn't show every extreme that they name: `segments`: within a sequence segment numbers start at 0 and never fall; every document except the last of its sequence has 200 to 1000 tokens.
All inputs are finite; a program needn't handle non-finite values.
Results may differ from a plain program's by a relative error of at most 0.02.
Values may be sent and summed in bfloat16 or wider, within the bound.
A program may use at most 448 MiB of HBM per device.

v0:
```python
import math

import jax
import jax.numpy as jnp
from jax import lax
from jax.sharding import PartitionSpec as P

HEAD_DIM = 64


NORM_EPSILON = 1e-05
MASKED = -1e30


def layer_norm(inputs, gain, bias_term):
    center = inputs - jnp.mean(inputs, axis=-1, keepdims=True)
    spread = jnp.mean(center * center, axis=-1, keepdims=True)
    return center * lax.rsqrt(spread + NORM_EPSILON) * gain + bias_term


def gelu_tanh(inputs):
    return jax.nn.gelu(inputs, approximate=True)


def product(left, right):
    return jnp.dot(left, right, preferred_element_type=jnp.float32)


def inner_rows(left, right):
    return lax.dot_general(
        left, right, (((0,), (0,)), ((), ())), preferred_element_type=jnp.float32
    )


def outer_cols(left, right):
    return lax.dot_general(
        left, right, (((1,), (1,)), ((), ())), preferred_element_type=jnp.float32
    )


def column_sum(values_low):
    return jnp.sum(values_low.astype(jnp.float32), axis=0)


def visible_mask(seg_own, seg_all, offset):
    row_pos = offset + lax.iota(jnp.int32, seg_own.shape[0])
    col_pos = lax.iota(jnp.int32, seg_all.shape[0])
    return (seg_own[:, None] == seg_all[None, :]) & (row_pos[:, None] >= col_pos[None, :])


def head_scores(queries, keys_all, visible, head_count):
    query_heads = queries.reshape(queries.shape[0], head_count, HEAD_DIM)
    key_heads = keys_all.reshape(keys_all.shape[0], head_count, HEAD_DIM)
    scores = jnp.einsum("thd,shd->hts", query_heads, key_heads, preferred_element_type=jnp.float32)
    return jnp.where(visible[None], scores, MASKED)


def gather_layer(
    layer_index,
    attn_gain,
    attn_shift,
    w_qkv,
    b_query,
    b_value,
    w_out,
    b_out,
    mlp_gain,
    mlp_shift,
    w_up,
    b_up,
    w_down,
    b_down,
):
    return (
        lax.all_gather(attn_gain[layer_index], "fsdp", axis=0, tiled=True),
        lax.all_gather(attn_shift[layer_index], "fsdp", axis=0, tiled=True),
        lax.all_gather(w_qkv[layer_index], "fsdp", axis=0, tiled=True),
        lax.all_gather(b_query[layer_index], "fsdp", axis=0, tiled=True),
        lax.all_gather(b_value[layer_index], "fsdp", axis=0, tiled=True),
        lax.all_gather(w_out[layer_index], "fsdp", axis=0, tiled=True),
        lax.all_gather(b_out[layer_index], "fsdp", axis=0, tiled=True),
        lax.all_gather(mlp_gain[layer_index], "fsdp", axis=0, tiled=True),
        lax.all_gather(mlp_shift[layer_index], "fsdp", axis=0, tiled=True),
        lax.all_gather(w_up[layer_index], "fsdp", axis=0, tiled=True),
        lax.all_gather(b_up[layer_index], "fsdp", axis=0, tiled=True),
        lax.all_gather(w_down[layer_index], "fsdp", axis=0, tiled=True),
        lax.all_gather(b_down[layer_index], "fsdp", axis=0, tiled=True),
    )


def gather_again(
    layer_index,
    attn_gain,
    attn_shift,
    w_qkv,
    b_query,
    b_value,
    w_out,
    b_out,
    mlp_gain,
    mlp_shift,
    w_up,
    b_up,
    w_down,
    b_down,
):
    return (
        lax.all_gather(attn_gain[layer_index], "fsdp", axis=0, tiled=True),
        lax.all_gather(attn_shift[layer_index], "fsdp", axis=0, tiled=True),
        lax.all_gather(w_qkv[layer_index], "fsdp", axis=0, tiled=True),
        lax.all_gather(b_query[layer_index], "fsdp", axis=0, tiled=True),
        lax.all_gather(b_value[layer_index], "fsdp", axis=0, tiled=True),
        lax.all_gather(w_out[layer_index], "fsdp", axis=0, tiled=True),
        lax.all_gather(b_out[layer_index], "fsdp", axis=0, tiled=True),
        lax.all_gather(mlp_gain[layer_index], "fsdp", axis=0, tiled=True),
        lax.all_gather(mlp_shift[layer_index], "fsdp", axis=0, tiled=True),
        lax.all_gather(w_up[layer_index], "fsdp", axis=0, tiled=True),
        lax.all_gather(b_up[layer_index], "fsdp", axis=0, tiled=True),
        lax.all_gather(w_down[layer_index], "fsdp", axis=0, tiled=True),
        lax.all_gather(b_down[layer_index], "fsdp", axis=0, tiled=True),
    )


def forward_layer(resid, gathered, visible):
    (
        attn_gain,
        attn_shift,
        w_qkv,
        b_query,
        b_value,
        w_out,
        b_out,
        mlp_gain,
        mlp_shift,
        w_up,
        b_up,
        w_down,
        b_down,
    ) = gathered
    model_width = resid.shape[1]
    head_count = model_width // HEAD_DIM
    query_scale = 1.0 / math.sqrt(HEAD_DIM)
    normed_attn = layer_norm(
        resid, attn_gain.astype(jnp.float32), attn_shift.astype(jnp.float32)
    ).astype(jnp.bfloat16)
    proj_all = product(normed_attn, w_qkv)
    queries = ((proj_all[:, :model_width] + b_query.astype(jnp.float32)) * query_scale).astype(
        jnp.bfloat16
    )
    keys_own = proj_all[:, model_width : 2 * model_width].astype(jnp.bfloat16)
    values_own = (proj_all[:, 2 * model_width :] + b_value.astype(jnp.float32)).astype(jnp.bfloat16)
    keys_all, values_all = (
        lax.all_gather(keys_own, "seq", axis=0, tiled=True),
        lax.all_gather(values_own, "seq", axis=0, tiled=True),
    )
    scores = head_scores(queries, keys_all, visible, head_count)
    row_max = jnp.max(scores, axis=-1, keepdims=True)
    exponent = jnp.exp(scores - row_max)
    row_sum = jnp.sum(exponent, axis=-1, keepdims=True)
    weights_soft = (exponent / row_sum).astype(jnp.bfloat16)
    log_total = row_max + jnp.log(row_sum)
    value_heads = values_all.reshape(values_all.shape[0], head_count, HEAD_DIM)
    attended = jnp.einsum(
        "hts,shd->thd", weights_soft, value_heads, preferred_element_type=jnp.float32
    )
    attended = attended.reshape(resid.shape[0], model_width).astype(jnp.bfloat16)
    middle = resid + product(attended, w_out) + b_out.astype(jnp.float32)
    normed_mlp = layer_norm(
        middle, mlp_gain.astype(jnp.float32), mlp_shift.astype(jnp.float32)
    ).astype(jnp.bfloat16)
    pre_act = product(normed_mlp, w_up) + b_up.astype(jnp.float32)
    activated = gelu_tanh(pre_act).astype(jnp.bfloat16)
    output = middle + product(activated, w_down) + b_down.astype(jnp.float32)
    stored = (
        resid,
        normed_attn,
        queries,
        keys_all,
        values_all,
        log_total,
        attended,
        middle,
        normed_mlp,
        pre_act,
        activated,
    )
    return (output, stored)


def backward_layer(grad_next, stored, gathered, visible):
    (
        attn_gain,
        attn_shift,
        w_qkv,
        b_query,
        b_value,
        w_out,
        b_out,
        mlp_gain,
        mlp_shift,
        w_up,
        b_up,
        w_down,
        b_down,
    ) = gathered
    (
        resid,
        normed_attn,
        queries,
        keys_all,
        values_all,
        log_total,
        attended,
        middle,
        normed_mlp,
        pre_act,
        activated,
    ) = stored
    model_width = resid.shape[1]
    tok_rows = resid.shape[0]
    key_rows = keys_all.shape[0]
    head_count = model_width // HEAD_DIM
    query_scale = 1.0 / math.sqrt(HEAD_DIM)
    grad_mlp = grad_next.astype(jnp.bfloat16)
    grad_b_down = column_sum(grad_mlp)
    grad_w_down = inner_rows(activated, grad_mlp)
    grad_act = outer_cols(grad_mlp, w_down)
    gelu_value, gelu_pull = jax.vjp(gelu_tanh, pre_act)
    grad_pre = gelu_pull(grad_act)[0].astype(jnp.bfloat16)
    grad_b_up = column_sum(grad_pre)
    grad_w_up = inner_rows(normed_mlp, grad_pre)
    grad_nm = outer_cols(grad_pre, w_up)
    norm_value, norm_pull = jax.vjp(
        layer_norm, middle, mlp_gain.astype(jnp.float32), mlp_shift.astype(jnp.float32)
    )
    grad_middle, grad_mlp_gain, grad_mlp_shift = norm_pull(grad_nm)
    grad_middle = grad_middle + grad_next
    grad_branch = grad_middle.astype(jnp.bfloat16)
    grad_b_out = column_sum(grad_branch)
    grad_w_out = inner_rows(attended, grad_branch)
    grad_attended = outer_cols(grad_branch, w_out).astype(jnp.bfloat16)
    scores = head_scores(queries, keys_all, visible, head_count)
    weights_full = jnp.exp(scores - log_total)
    weights_soft = weights_full.astype(jnp.bfloat16)
    grad_heads = grad_attended.reshape(tok_rows, head_count, HEAD_DIM)
    query_heads = queries.reshape(tok_rows, head_count, HEAD_DIM)
    key_heads = keys_all.reshape(key_rows, head_count, HEAD_DIM)
    value_heads = values_all.reshape(key_rows, head_count, HEAD_DIM)
    grad_value_terms = jnp.einsum(
        "hts,thd->shd", weights_soft, grad_heads, preferred_element_type=jnp.float32
    )
    grad_probs = jnp.einsum(
        "thd,shd->hts", grad_heads, value_heads, preferred_element_type=jnp.float32
    )
    inner_sum = jnp.sum(weights_full * grad_probs, axis=-1, keepdims=True)
    grad_scores = (weights_full * (grad_probs - inner_sum)).astype(jnp.bfloat16)
    grad_queries = jnp.einsum(
        "hts,shd->thd", grad_scores, key_heads, preferred_element_type=jnp.float32
    )
    grad_queries = grad_queries.reshape(tok_rows, model_width).astype(jnp.bfloat16) * query_scale
    grad_key_terms = jnp.einsum(
        "hts,thd->shd", grad_scores, query_heads, preferred_element_type=jnp.float32
    )
    grad_keys, grad_values = (
        lax.psum_scatter(
            grad_key_terms.reshape(key_rows, model_width).astype(jnp.bfloat16),
            "seq",
            scatter_dimension=0,
            tiled=True,
        ).astype(jnp.float32),
        lax.psum_scatter(
            grad_value_terms.reshape(key_rows, model_width).astype(jnp.bfloat16),
            "seq",
            scatter_dimension=0,
            tiled=True,
        ).astype(jnp.float32),
    )
    grad_keys = grad_keys.astype(jnp.bfloat16)
    grad_values = grad_values.astype(jnp.bfloat16)
    grad_proj = jnp.concatenate([grad_queries, grad_keys, grad_values], axis=1)
    grad_b_query = column_sum(grad_queries)
    grad_b_value = column_sum(grad_values)
    grad_w_qkv = inner_rows(normed_attn, grad_proj)
    grad_na = outer_cols(grad_proj, w_qkv)
    first_value, first_pull = jax.vjp(
        layer_norm, resid, attn_gain.astype(jnp.float32), attn_shift.astype(jnp.float32)
    )
    grad_resid, grad_attn_gain, grad_attn_shift = first_pull(grad_na)
    grad_resid = grad_resid + grad_middle
    gradients = (
        grad_attn_gain,
        grad_attn_shift,
        grad_w_qkv,
        grad_b_query,
        grad_b_value,
        grad_w_out,
        grad_b_out,
        grad_mlp_gain,
        grad_mlp_shift,
        grad_w_up,
        grad_b_up,
        grad_w_down,
        grad_b_down,
    )
    return (grad_resid, gradients)


def reduce_grads(gradients):
    shares = (
        lax.psum_scatter(gradients[0], ("fsdp", "rep"), scatter_dimension=0, tiled=True),
        lax.psum_scatter(gradients[1], ("fsdp", "rep"), scatter_dimension=0, tiled=True),
        lax.psum_scatter(gradients[2], ("fsdp", "rep"), scatter_dimension=0, tiled=True),
        lax.psum_scatter(gradients[3], ("fsdp", "rep"), scatter_dimension=0, tiled=True),
        lax.psum_scatter(gradients[4], ("fsdp", "rep"), scatter_dimension=0, tiled=True),
        lax.psum_scatter(gradients[5], ("fsdp", "rep"), scatter_dimension=0, tiled=True),
        lax.psum_scatter(gradients[6], ("fsdp", "rep"), scatter_dimension=0, tiled=True),
        lax.psum_scatter(gradients[7], ("fsdp", "rep"), scatter_dimension=0, tiled=True),
        lax.psum_scatter(gradients[8], ("fsdp", "rep"), scatter_dimension=0, tiled=True),
        lax.psum_scatter(gradients[9], ("fsdp", "rep"), scatter_dimension=0, tiled=True),
        lax.psum_scatter(gradients[10], ("fsdp", "rep"), scatter_dimension=0, tiled=True),
        lax.psum_scatter(gradients[11], ("fsdp", "rep"), scatter_dimension=0, tiled=True),
        lax.psum_scatter(gradients[12], ("fsdp", "rep"), scatter_dimension=0, tiled=True),
    )
    shares = (
        lax.psum(shares[0].astype(jnp.bfloat16), "seq").astype(jnp.float32),
        lax.psum(shares[1].astype(jnp.bfloat16), "seq").astype(jnp.float32),
        lax.psum(shares[2].astype(jnp.bfloat16), "seq").astype(jnp.float32),
        lax.psum(shares[3].astype(jnp.bfloat16), "seq").astype(jnp.float32),
        lax.psum(shares[4].astype(jnp.bfloat16), "seq").astype(jnp.float32),
        lax.psum(shares[5].astype(jnp.bfloat16), "seq").astype(jnp.float32),
        lax.psum(shares[6].astype(jnp.bfloat16), "seq").astype(jnp.float32),
        lax.psum(shares[7].astype(jnp.bfloat16), "seq").astype(jnp.float32),
        lax.psum(shares[8].astype(jnp.bfloat16), "seq").astype(jnp.float32),
        lax.psum(shares[9].astype(jnp.bfloat16), "seq").astype(jnp.float32),
        lax.psum(shares[10].astype(jnp.bfloat16), "seq").astype(jnp.float32),
        lax.psum(shares[11].astype(jnp.bfloat16), "seq").astype(jnp.float32),
        lax.psum(shares[12].astype(jnp.bfloat16), "seq").astype(jnp.float32),
    )
    return (
        lax.all_gather(shares[0].astype(jnp.bfloat16), "rep", axis=0, tiled=True).astype(
            jnp.float32
        ),
        lax.all_gather(shares[1].astype(jnp.bfloat16), "rep", axis=0, tiled=True).astype(
            jnp.float32
        ),
        lax.all_gather(shares[2].astype(jnp.bfloat16), "rep", axis=0, tiled=True).astype(
            jnp.float32
        ),
        lax.all_gather(shares[3].astype(jnp.bfloat16), "rep", axis=0, tiled=True).astype(
            jnp.float32
        ),
        lax.all_gather(shares[4].astype(jnp.bfloat16), "rep", axis=0, tiled=True).astype(
            jnp.float32
        ),
        lax.all_gather(shares[5].astype(jnp.bfloat16), "rep", axis=0, tiled=True).astype(
            jnp.float32
        ),
        lax.all_gather(shares[6].astype(jnp.bfloat16), "rep", axis=0, tiled=True).astype(
            jnp.float32
        ),
        lax.all_gather(shares[7].astype(jnp.bfloat16), "rep", axis=0, tiled=True).astype(
            jnp.float32
        ),
        lax.all_gather(shares[8].astype(jnp.bfloat16), "rep", axis=0, tiled=True).astype(
            jnp.float32
        ),
        lax.all_gather(shares[9].astype(jnp.bfloat16), "rep", axis=0, tiled=True).astype(
            jnp.float32
        ),
        lax.all_gather(shares[10].astype(jnp.bfloat16), "rep", axis=0, tiled=True).astype(
            jnp.float32
        ),
        lax.all_gather(shares[11].astype(jnp.bfloat16), "rep", axis=0, tiled=True).astype(
            jnp.float32
        ),
        lax.all_gather(shares[12].astype(jnp.bfloat16), "rep", axis=0, tiled=True).astype(
            jnp.float32
        ),
    )


def on_device(
    tokens,
    segments,
    grad_out,
    attn_gain,
    attn_shift,
    w_qkv,
    b_query,
    b_value,
    w_out,
    b_out,
    mlp_gain,
    mlp_shift,
    w_up,
    b_up,
    w_down,
    b_down,
):
    seg_own = segments[0]
    seg_all = lax.all_gather(seg_own, "seq", axis=0, tiled=True)
    offset = lax.axis_index("seq") * seg_own.shape[0]
    visible = visible_mask(seg_own, seg_all, offset)
    layer_count = attn_gain.shape[0]
    resid = tokens[0].astype(jnp.float32)
    kept_weights = []
    stored_list = []
    for layer_index in range(layer_count):
        gathered = gather_layer(
            layer_index,
            attn_gain,
            attn_shift,
            w_qkv,
            b_query,
            b_value,
            w_out,
            b_out,
            mlp_gain,
            mlp_shift,
            w_up,
            b_up,
            w_down,
            b_down,
        )
        resid, stored = forward_layer(resid, gathered, visible)
        kept_weights.append(gathered)
        stored_list.append(stored)
    result = resid.astype(jnp.bfloat16)[None]
    grad_resid = grad_out[0].astype(jnp.float32)
    reduced = [None] * layer_count
    for layer_index in reversed(range(layer_count)):
        gathered = gather_again(
            layer_index,
            attn_gain,
            attn_shift,
            w_qkv,
            b_query,
            b_value,
            w_out,
            b_out,
            mlp_gain,
            mlp_shift,
            w_up,
            b_up,
            w_down,
            b_down,
        )
        grad_resid, gradients = backward_layer(
            grad_resid, stored_list[layer_index], gathered, visible
        )
        reduced[layer_index] = reduce_grads(gradients)
    stacked = tuple((jnp.stack([entry[member] for entry in reduced]) for member in range(13)))
    return (result, grad_resid.astype(jnp.bfloat16)[None]) + stacked


def solution(mesh):
    return jax.shard_map(
        on_device,
        mesh=mesh,
        in_specs=(
            P(("fsdp", "rep"), "seq", None),
            P(("fsdp", "rep"), "seq"),
            P(("fsdp", "rep"), "seq", None),
            P(None, "fsdp"),
            P(None, "fsdp"),
            P(None, "fsdp", None),
            P(None, "fsdp"),
            P(None, "fsdp"),
            P(None, "fsdp", None),
            P(None, "fsdp"),
            P(None, "fsdp"),
            P(None, "fsdp"),
            P(None, "fsdp", None),
            P(None, "fsdp"),
            P(None, "fsdp", None),
            P(None, "fsdp"),
        ),
        out_specs=(
            P(("fsdp", "rep"), "seq", None),
            P(("fsdp", "rep"), "seq", None),
            P(None, "fsdp"),
            P(None, "fsdp"),
            P(None, "fsdp", None),
            P(None, "fsdp"),
            P(None, "fsdp"),
            P(None, "fsdp", None),
            P(None, "fsdp"),
            P(None, "fsdp"),
            P(None, "fsdp"),
            P(None, "fsdp", None),
            P(None, "fsdp"),
            P(None, "fsdp", None),
            P(None, "fsdp"),
        ),
        check_vma=False,
    )
```

profile of v0, /device:TPU:25, one launch (start us, length us, event | category | flops | bytes accessed | tf_op | source)
XLA Modules:
  0.0 3008.1 jit_solution(1192678646422683233)
XLA Ops:
  32.1 24.5 all-reduce.68
  57.9 85.8 %all-gather.64.cloned.1.call-done = bf16[1,1088,3264]{2,1,0:T(8,128)(2,1)} async-done(((bf16[1,272,3264]{2,1,0:T(8,128)(2,1)}), bf16[1,1088,3264]{2,1,0:T(8,128)(2,1)}) %all-gather.64.cloned.1.call-update) | async-done | bytes 7102480 | tf_op jit(solution)/shard_map/all_gather | solution.py:77
  190.9 16.8 select_reduce_fusion.1
  227.7 16.7 fusion.120
  244.4 35.4 %all-gather.66.cloned.1.call-done = bf16[1,1088,1088]{2,1,0:T(8,128)(2,1)} async-done(((bf16[1,272,1088]{2,1,0:T(8,128)(2,1)}), bf16[1,1088,1088]{2,1,0:T(8,128)(2,1)}) %all-gather.66.cloned.1.call-update) | async-done | bytes 2367504 | tf_op jit(solution)/shard_map/all_gather | solution.py:80
  285.0 162.3 %all-gather.68.cloned.1.call-done = bf16[1,1088,4352]{2,1,0:T(8,128)(2,1)} async-done(((bf16[1,272,4352]{2,1,0:T(8,128)(2,1)}), bf16[1,1088,4352]{2,1,0:T(8,128)(2,1)}) %all-gather.68.cloned.1.call-update) | async-done | bytes 9469968 | tf_op jit(solution)/shard_map/all_gather | solution.py:84
  459.9 164.1 %all-gather.70.cloned.1.call-done = bf16[1,4352,1088]{2,1,0:T(8,128)(2,1)} async-done(((bf16[1,1088,1088]{2,1,0:T(8,128)(2,1)}), bf16[1,4352,1088]{2,1,0:T(8,128)(2,1)}) %all-gather.70.cloned.1.call-update) | async-done | bytes 9469968 | tf_op jit(solution)/shard_map/all_gather | solution.py:86
  637.6 117.0 %all-gather.72.cloned.1.call-done = bf16[1,1088,3264]{2,1,0:T(8,128)(2,1)} async-done(((bf16[1,272,3264]{2,1,0:T(8,128)(2,1)}), bf16[1,1088,3264]{2,1,0:T(8,128)(2,1)}) %all-gather.72.cloned.1.call-update) | async-done | bytes 7102480 | tf_op jit(solution)/shard_map/all_gather | solution.py:77
  772.4 30.0 all-gather.58.cloned.1.call-done
  802.4 17.0 select_reduce_fusion
  839.2 16.7 fusion.119
  855.9 35.4 %all-gather.74.cloned.1.call-done = bf16[1,1088,1088]{2,1,0:T(8,128)(2,1)} async-done(((bf16[1,272,1088]{2,1,0:T(8,128)(2,1)}), bf16[1,1088,1088]{2,1,0:T(8,128)(2,1)}) %all-gather.74.cloned.1.call-update) | async-done | bytes 2367504 | tf_op jit(solution)/shard_map/all_gather | solution.py:80
  896.1 163.0 %all-gather.76.cloned.1.call-done = bf16[1,1088,4352]{2,1,0:T(8,128)(2,1)} async-done(((bf16[1,272,4352]{2,1,0:T(8,128)(2,1)}), bf16[1,1088,4352]{2,1,0:T(8,128)(2,1)}) %all-gather.76.cloned.1.call-update) | async-done | bytes 9469968 | tf_op jit(solution)/shard_map/all_gather | solution.py:84
  1071.4 164.2 %all-gather.78.cloned.1.call-done = bf16[1,4352,1088]{2,1,0:T(8,128)(2,1)} async-done(((bf16[1,1088,1088]{2,1,0:T(8,128)(2,1)}), bf16[1,4352,1088]{2,1,0:T(8,128)(2,1)}) %all-gather.78.cloned.1.call-update) | async-done | bytes 9469968 | tf_op jit(solution)/shard_map/all_gather | solution.py:86
  1284.5 26.1 multiply_reduce_fusion.1
  1310.5 29.7 multiply_convert_fusion.1
  1365.7 20.1 reduce-scatter.19.cloned.1.call-done
  1432.1 17.5 fusion.113
  1449.7 26.5 multiply_reduce_fusion
  1476.2 29.7 multiply_convert_fusion
  1582.0 540.0 %fusion.155 = (f32[72,4352]{1,0:T(8,128)}, f32[72,4352]{1,0:T(8,128)S(1)}) fusion(f32[1088,4352]{1,0:T(8,128)} %fusion.151, f32[1088,4352]{1,0:T(8,128)} %fusion.150), kind=kCustom, calls=%all-reduce-scatter.7 | all-reduce-scatter fusion | flops 10027009 | bytes 40387072
  2182.6 444.3 %fusion.154 = (f32[72,3264]{1,0:T(8,128)}, f32[72,3264]{1,0:T(8,128)}, f32[80,1088]{1,0:T(8,128)}, f32[80,1088]{1,0:T(8,128)}) fusion(f32[1088,3264]{1,0:T(8,128)} %fusion.125, f32[1088,3264]{1,0:T(8,128)} %fusion.124, f32[1088,1088]{1,0:T(8,128)} %fusion.171, f32[1088,1088]{1,0:T(8,128)} %fusion.170), kind=kCustom, calls=%all-reduce-scatter.6 | all-reduce-scatter fusion | flops 10305538 | bytes 40456704
  2705.0 107.1 %all-reduce.75.cloned.1.call-done = (bf16[68,3264]{1,0:T(8,128)(2,1)}, bf16[68,3264]{1,0:T(8,128)(2,1)}, bf16[68,1088]{1,0:T(8,128)(2,1)}, bf16[68,1088]{1,0:T(8...) async-done(((bf16[68,3264]{1,0:T(8,128)(2,1)}, bf16[68,3264]{1,0:T(8,128)(2,1)}, ...) | async-done | bytes 3551248 | tf_op jit(solution)/shard_map/psum | solution.py:327
  2846.3 57.6 %all-reduce.66 = (bf16[1088]{0:T(1024)(128)(2,1)S(1)}, bf16[1088]{0:T(1024)(128)(2,1)S(1)}, bf16[1088]{0:T(1024)(128)(2,1)}, bf16[1088]{0:T(1024)(128)(2,1)}, bf...) all-reduce(f32[1088]{0:T(1024)S(1)} %copy-done.66, ...), channel_id=34, replica_groups=mesh['seq'=2,'fsdp'=4,'rep'=4] {'fsdp','rep'}, use_global_device_ids=true, to_apply=%region_30.31.clone | all-reduce | flops 26112 | bytes 156672
  (571 shorter events, 639.5 us)
Async XLA Ops:
  7.3 136.4 %all-gather.64.cloned.1.call-start = ((), (), s32[]{:S(2)}) async-start(), calls=%async_computation.18 | async-start | bytes 9052160 | tf_op jit(solution)/shard_map/all_gather | solution.py:77
  11.5 179.4 %all-gather.54.cloned.1.call-start = ((), (), s32[]{:S(2)}) async-start(), calls=%async_computation.7 | async-start | bytes 3342336 | tf_op jit(solution)/shard_map/all_gather | solution.py:153
  158.8 121.0 %all-gather.66.cloned.1.call-start = ((), (), s32[]{:S(2)}) async-start(), calls=%async_computation.19 | async-start | bytes 3133440 | tf_op jit(solution)/shard_map/all_gather | solution.py:80
  160.2 287.2 %all-gather.68.cloned.1.call-start = ((), (), s32[]{:S(2)}) async-start(), calls=%async_computation.20 | async-start | bytes 11837440 | tf_op jit(solution)/shard_map/all_gather | solution.py:84
  165.1 458.8 %all-gather.70.cloned.1.call-start = ((), (), s32[]{:S(2)}) async-start(), calls=%async_computation.21 | async-start | bytes 12533760 | tf_op jit(solution)/shard_map/all_gather | solution.py:86
  170.7 584.0 %all-gather.72.cloned.1.call-start = ((), (), s32[]{:S(2)}) async-start(), calls=%async_computation.22 | async-start | bytes 9052160 | tf_op jit(solution)/shard_map/all_gather | solution.py:77
  171.4 631.0 %all-gather.58.cloned.1.call-start = ((), (), s32[]{:S(2)}) async-start(), calls=%async_computation.9 | async-start | bytes 3342336 | tf_op jit(solution)/shard_map/all_gather | solution.py:153
  770.4 120.9 %all-gather.74.cloned.1.call-start = ((), (), s32[]{:S(2)}) async-start(), calls=%async_computation.23 | async-start | bytes 3133440 | tf_op jit(solution)/shard_map/all_gather | solution.py:80
  771.0 288.0 %all-gather.76.cloned.1.call-start = ((), (), s32[]{:S(2)}) async-start(), calls=%async_computation.24 | async-start | bytes 11837440 | tf_op jit(solution)/shard_map/all_gather | solution.py:84
  771.7 463.9 %all-gather.78.cloned.1.call-start = ((), (), s32[]{:S(2)}) async-start(), calls=%async_computation.25 | async-start | bytes 12533760 | tf_op jit(solution)/shard_map/all_gather | solution.py:86
  772.3 593.4 %reduce-scatter.21.cloned.1.call-start = ((), (), s32[]{:S(2)}) async-start(), calls=%async_computation.11 | async-start | bytes 3342336 | tf_op jit(solution)/shard_map/reduce_scatter | solution.py:271
  1282.8 103.0 %reduce-scatter.19.cloned.1.call-start = ((), (), s32[]{:S(2)}) async-start(), calls=%async_computation.10 | async-start | bytes 3342336 | tf_op jit(solution)/shard_map/reduce_scatter | solution.py:265
  1350.9 820.6 %reduce-scatter.25.cloned.1.call-start = ((), (), s32[]{:S(2)}) async-start(), calls=%async_computation.13 | async-start | bytes 3342336 | tf_op jit(solution)/shard_map/reduce_scatter | solution.py:271
  1449.7 721.8 %reduce-scatter.23.cloned.1.call-start = ((), (), s32[]{:S(2)}) async-start(), calls=%async_computation.12 | async-start | bytes 3342336 | tf_op jit(solution)/shard_map/reduce_scatter | solution.py:265
  1517.0 1183.5 %reduce-scatter.29.cloned.1.call-start = ((), (), s32[]{:S(2)}) async-start(), calls=%async_computation.16 | async-start | bytes 21307392 | tf_op jit(solution)/shard_map/reduce_scatter | solution.py:321
  1531.6 1171.1 %reduce-scatter.27.cloned.1.call-start = ((), (), s32[]{:S(2)}) async-start(), calls=%async_computation.14 | async-start | bytes 21307392 | tf_op jit(solution)/shard_map/reduce_scatter | solution.py:321
  1545.8 1266.2 %all-reduce.75.cloned.1.call-start = ((), (), s32[]{:S(2)}) async-start(), calls=%async_computation.30 | async-start | bytes 7593984 | tf_op jit(solution)/shard_map/psum | solution.py:327
  2129.9 501.9 %collective-permute-start.8 = (bf16[60,4352]{1,0:T(8,128)(2,1)}, bf16[60,4352]{1,0:T(8,128)(2,1)}, u32[]{:S(2)}, u32[]{:S(2)}) collective-permute-start(bf16[60,4352]{1,0:T(8,128)(2,1)} %slice.152), channel_id=1, source_target_pairs={{0,1},{1,2},{2,3},{3,4},{4,5},{5,6},{6,7},{7,8},{8,9},{9,10},{10,1... | collective-permute-start | bytes 1566728
  2704.9 268.6 %all-gather.82.cloned.1.call-start = ((), (), s32[]{:S(2)}) async-start(), calls=%async_computation.27 | async-start | bytes 2396160 | tf_op jit(solution)/shard_map/all_gather | solution.py:346
  2812.1 163.4 %all-gather.80.cloned.1.call-start = ((), (), s32[]{:S(2)}) async-start(), calls=%async_computation.26 | async-start | bytes 2396160 | tf_op jit(solution)/shard_map/all_gather | solution.py:346
  2812.8 170.6 %all-gather.86.cloned.1.call-start = ((), (), s32[]{:S(2)}) async-start(), calls=%async_computation.29 | async-start | bytes 3133440 | tf_op jit(solution)/shard_map/all_gather | solution.py:367
  2813.5 171.8 %all-gather.84.cloned.1.call-start = ((), (), s32[]{:S(2)}) async-start(), calls=%async_computation.28 | async-start | bytes 3133440 | tf_op jit(solution)/shard_map/all_gather | solution.py:367
  2814.3 180.0 %all-gather.62.cloned.1.call-start = ((), (), s32[]{:S(2)}) async-start(), calls=%async_computation.17 | async-start | bytes 3133440 | tf_op jit(solution)/shard_map/all_gather | solution.py:373
  2817.6 176.7 %all-gather.60.cloned.1.call-start = ((), (), s32[]{:S(2)}) async-start(), calls=%async_computation.15 | async-start | bytes 3133440 | tf_op jit(solution)/shard_map/all_gather | solution.py:373
  (126 other events, 6926.1 us)
Sparse Core Ops, SparseCore 0:
  11.6 132.0 all-gather.63
  155.1 35.7 all-gather.53
  193.0 34.5 all-gather.51
  229.1 50.6 all-gather.65
  281.8 165.5 all-gather.67
  449.3 174.6 all-gather.69
  625.6 129.0 all-gather.71
  766.8 35.6 all-gather.57
  804.5 34.5 all-gather.55
  840.6 50.6 all-gather.73
  893.4 165.5 all-gather.75
  1061.0 174.6 all-gather.77
  1283.0 34.2 reduce-scatter.20
  1351.0 34.7 reduce-scatter.18
  1449.8 33.2 reduce-scatter.24
  1517.1 33.2 reduce-scatter.22
  1554.5 354.5 reduce-scatter.28
  1913.8 262.8 reduce-scatter.26
  2705.1 106.9 all-reduce.74
  2813.5 22.1 all-gather.81
  2861.1 26.0 all-gather.85
  2888.9 25.1 all-gather.83
  2915.6 25.4 all-gather.61
  2942.7 31.6 all-gather.59
  (1 shorter events, 22.1 us)
where the time goes:
time: 3020 us; the launch traced here: 3010 us
  waiting for transfers between devices  1110 us (37%)
  blocking collectives  1110 us (37%)
  matrix products  441 us (15%)
  local copies, waits for them, and re-layouts  150 us (5%)
  other arithmetic  145 us (5%)
    unnamed x5, blocking collectives  1080 us
    all_gather x2, waiting for transfers between devices, gather_layer(): lax.all_gather(w_down[layer_index], 'fsdp', axis=0, tiled=True)  328 us
    all_gather x2, waiting for transfers between devices, gather_layer(): lax.all_gather(w_up[layer_index], 'fsdp', axis=0, tiled=True)  325 us
    all_gather x2, waiting for transfers between devices, gather_layer(): lax.all_gather(w_qkv[layer_index], 'fsdp', axis=0, tiled=True)  203 us
    unnamed x335, local copies, waits for them, and re-layouts  110 us
    psum x1, waiting for transfers between devices, reduce_grads(): lax.psum(shares[2].astype(jnp.bfloat16), 'seq').astype(jnp.float32)  107 us
    dot_general x8, matrix products, inner_rows(): lax.dot_general(left, right, (((0,), (0,)), ((), ())), preferred_element_...  89.1 us
    dot_general x8, matrix products, product(): return jnp.dot(left, right, preferred_element_type=jnp.float32)  75.7 us
  transfers between devices with their start and end apart: 35, of which 14 were waited for; matrix products, arithmetic and copies ran while one was open for 52% of the time, Pallas kernels for 0%

commit v1 on v0

--- a/solution.py
+++ b/solution.py
@@ -3,9 +3,12 @@
 import jax
 import jax.numpy as jnp
 from jax import lax
+from jax.experimental import pallas as pl
+from jax.experimental.pallas import tpu as pltpu
 from jax.sharding import PartitionSpec as P
 
 HEAD_DIM = 64
+MESH = pl.DeviceIdType.MESH
 
 
 NORM_EPSILON = 1e-05
@@ -121,7 +124,7 @@
     )
 
 
-def forward_layer(resid, gathered, visible):
+def forward_layer(resid, gathered, visible, pool):
     (
         attn_gain,
         attn_shift,
@@ -149,10 +152,7 @@
     )
     keys_own = proj_all[:, model_width : 2 * model_width].astype(jnp.bfloat16)
     values_own = (proj_all[:, 2 * model_width :] + b_value.astype(jnp.float32)).astype(jnp.bfloat16)
-    keys_all, values_all = (
-        lax.all_gather(keys_own, "seq", axis=0, tiled=True),
-        lax.all_gather(values_own, "seq", axis=0, tiled=True),
-    )
+    keys_all, values_all = pool.spread(keys_own), pool.spread(values_own)
     scores = head_scores(queries, keys_all, visible, head_count)
     row_max = jnp.max(scores, axis=-1, keepdims=True)
     exponent = jnp.exp(scores - row_max)
@@ -187,7 +187,7 @@
     return (output, stored)
 
 
-def backward_layer(grad_next, stored, gathered, visible):
+def backward_layer(grad_next, stored, gathered, visible, pool):
     (
         attn_gain,
         attn_shift,
@@ -261,20 +261,8 @@
     grad_key_terms = jnp.einsum(
         "hts,thd->shd", grad_scores, query_heads, preferred_element_type=jnp.float32
     )
-    grad_keys, grad_values = (
-        lax.psum_scatter(
-            grad_key_terms.reshape(key_rows, model_width).astype(jnp.bfloat16),
-            "seq",
-            scatter_dimension=0,
-            tiled=True,
-        ).astype(jnp.float32),
-        lax.psum_scatter(
-            grad_value_terms.reshape(key_rows, model_width).astype(jnp.bfloat16),
-            "seq",
-            scatter_dimension=0,
-            tiled=True,
-        ).astype(jnp.float32),
-    )
+    grad_keys = pool.collect(grad_key_terms.reshape(key_rows, model_width).astype(jnp.bfloat16))
+    grad_values = pool.collect(grad_value_terms.reshape(key_rows, model_width).astype(jnp.bfloat16))
     grad_keys = grad_keys.astype(jnp.bfloat16)
     grad_values = grad_values.astype(jnp.bfloat16)
     grad_proj = jnp.concatenate([grad_queries, grad_keys, grad_values], axis=1)
@@ -377,6 +365,619 @@
             jnp.float32
         ),
     )
+
+
+class Halves:
+    def spread(self, rows):
+        return lax.all_gather(rows, "seq", axis=0, tiled=True)
+
+    def collect(self, rows):
+        return lax.psum_scatter(rows, "seq", scatter_dimension=0, tiled=True)
+
+
+class Cores:
+    swap = [(0, 1), (1, 0), (2, 3), (3, 2)]
+
+    def spread(self, rows):
+        other = lax.ppermute(rows, "rep", self.swap)
+        return jnp.concatenate([rows, other], axis=0)
+
+    def collect(self, rows):
+        half = rows.shape[0] // 2
+        other = lax.ppermute(rows[half:], "rep", self.swap)
+        return rows[:half] + other
+
+
+def to_cores(rows):
+    half = rows.shape[0] // 2
+    spots = [(x, y, c) for x in range(2) for y in range(2) for c in range(2)]
+    first = [(x * 4 + y * 2 + c, c * 4 + y * 2 + x) for x, y, c in spots]
+    second = [(x * 4 + y * 2 + c, c * 4 + y * 2 + 1 - x) for x, y, c in spots]
+    return jnp.concatenate(
+        [
+            lax.ppermute(rows[:half], ("seq", "rep"), first),
+            lax.ppermute(rows[half:], ("seq", "rep"), second),
+        ],
+        axis=0,
+    )
+
+
+def from_cores(rows):
+    half = rows.shape[0] // 2
+    spots = [(x, y, c) for x in range(2) for y in range(2) for c in range(2)]
+    first = [(c * 4 + y * 2 + x, x * 4 + y * 2 + c) for x, y, c in spots]
+    second = [(c * 4 + y * 2 + 1 - x, x * 4 + y * 2 + c) for x, y, c in spots]
+    return jnp.concatenate(
+        [
+            lax.ppermute(rows[:half], ("seq", "rep"), first),
+            lax.ppermute(rows[half:], ("seq", "rep"), second),
+        ],
+        axis=0,
+    )
+
+
+ZN = 4
+
+
+def neighbours():
+    x, z, r = lax.axis_index("seq"), lax.axis_index("fsdp"), lax.axis_index("rep")
+    y, c = r // 2, r % 2
+    across = (1 - x, z, r)
+    beside = (x, z, (1 - y) * 2 + c)
+    twin = (x, z, y * 2 + (1 - c))
+    up = (x, (z + 1) % ZN, r)
+    down = (x, (z + ZN - 1) % ZN, r)
+    return x, y, z, c, across, beside, twin, up, down
+
+
+def greet(z, across, beside, twin, up, down):
+    barrier = pltpu.get_barrier_semaphore()
+
+    def tell(device):
+        pl.semaphore_signal(barrier, inc=1, device_id=device, device_id_type=MESH)
+
+    for device in (across, beside, twin):
+        tell(device)
+
+    @pl.when(z < ZN - 1)
+    def _():
+        tell(up)
+
+    @pl.when(z > 0)
+    def _():
+        tell(down)
+
+    pl.semaphore_wait(barrier, 3 + (z + ZN - 1) // ZN + (2 * ZN - 2 - z) // ZN)
+
+
+ZA, ZR, GX, GY, GD1, GD2, GC = range(7)
+
+
+def gather_body(units, ins, outs, holds, load_sem, store_sem, send_sem, recv_sem):
+    x, y, z, c, across, beside, twin, up, down = neighbours()
+    greet(z, across, beside, twin, up, down)
+
+    def owned(u, px, py, half=None):
+        k = ins[units[u][1]].shape[1] // 8
+        base = (c * 4 + px * 2 + py) * k
+        if half is None:
+            return pl.ds(base, k)
+        return pl.ds(base + half * (k // 2), k // 2)
+
+    def rest(u):
+        n = ins[units[u][1]].shape[1]
+        return pl.ds(n // 8 * 8, n % 8)
+
+    def slab(u, core):
+        k = ins[units[u][1]].shape[1] // 8
+        return pl.ds(core * 4 * k, 4 * k)
+
+    def move(u, zz, rows, device, kind, source=None, send_kind=None):
+        layer, m = units[u]
+        target = outs[m].at[layer, zz, rows]
+        return pltpu.make_async_remote_copy(
+            src_ref=target if source is None else source,
+            dst_ref=target,
+            send_sem=send_sem.at[u, zz, kind if send_kind is None else send_kind],
+            recv_sem=recv_sem.at[u, zz, kind],
+            device_id=device,
+            device_id_type=MESH,
+        )
+
+    def load(u):
+        layer, m = units[u]
+        return pltpu.make_async_copy(ins[m].at[layer], holds[m].at[layer], load_sem.at[u])
+
+    def store(u):
+        layer, m = units[u]
+        return pltpu.make_async_copy(holds[m].at[layer], outs[m].at[layer, z], store_sem.at[u])
+
+    def own_sends(u, act):
+        layer, m = units[u]
+        mine, left_over = owned(u, x, y), rest(u)
+
+        @pl.when(z < ZN - 1)
+        def _():
+            act(move(u, z, mine, up, ZA, ins[m].at[layer, mine], 0))
+            act(move(u, z, left_over, up, ZR, ins[m].at[layer, left_over], 1))
+
+        @pl.when(z > 0)
+        def _():
+            act(move(u, z, mine, down, ZA, ins[m].at[layer, mine], 2))
+            act(move(u, z, left_over, down, ZR, ins[m].at[layer, left_over], 3))
+
+    def both(s, act):
+        @pl.when(z >= s)
+        def _():
+            act(z - s, 0)
+
+        @pl.when(z + s <= ZN - 1)
+        def _():
+            act(z + s, 1)
+
+    def onward(u, zz, d, act):
+        mine, left_over = owned(u, x, y), rest(u)
+        if d == 0:
+
+            @pl.when(z < ZN - 1)
+            def _():
+                act(move(u, zz, mine, up, ZA))
+                act(move(u, zz, left_over, up, ZR))
+
+        else:
+
+            @pl.when(z > 0)
+            def _():
+                act(move(u, zz, mine, down, ZA))
+                act(move(u, zz, left_over, down, ZR))
+
+    def line_step(u, s):
+        def act(zz, d):
+            mine, left_over = owned(u, x, y), rest(u)
+            move(u, zz, mine, across, ZA).wait_recv()
+            move(u, zz, left_over, across, ZR).wait_recv()
+            onward(u, zz, d, lambda copy: copy.start())
+            move(u, zz, mine, across, GX).start()
+            move(u, zz, mine, beside, GY).start()
+
+        both(s, act)
+
+    def plane_step(u, s):
+        def act(zz, d):
+            move(u, zz, owned(u, 1 - x, y), across, GX).wait_recv()
+            move(u, zz, owned(u, 1 - x, y, 0), beside, GD1).start()
+            move(u, zz, owned(u, x, 1 - y), beside, GY).wait_recv()
+            move(u, zz, owned(u, x, 1 - y, 1), across, GD2).start()
+
+        both(s, act)
+
+    def corner_step(u, s):
+        def act(zz, d):
+            move(u, zz, owned(u, 1 - x, 1 - y, 0), beside, GD1).wait_recv()
+            move(u, zz, owned(u, 1 - x, 1 - y, 1), across, GD2).wait_recv()
+            move(u, zz, slab(u, c), twin, GC).start()
+
+        both(s, act)
+
+    def finish(u):
+        store(u).wait()
+        own_sends(u, lambda copy: copy.wait_send())
+        for s in (1, 2, 3):
+
+            def act(zz, d):
+                mine = owned(u, x, y)
+                move(u, zz, slab(u, 1 - c), twin, GC).wait_recv()
+                onward(u, zz, d, lambda copy: copy.wait_send())
+                move(u, zz, mine, across, GX).wait_send()
+                move(u, zz, mine, beside, GY).wait_send()
+                move(u, zz, owned(u, 1 - x, y, 0), beside, GD1).wait_send()
+                move(u, zz, owned(u, x, 1 - y, 1), across, GD2).wait_send()
+                move(u, zz, slab(u, c), twin, GC).wait_send()
+
+            both(s, act)
+
+    count = len(units)
+
+    def at(step, u, s):
+        if 0 <= u < count:
+            step(u, s)
+
+    for u in range(count):
+        load(u).start()
+    for u in range(2):
+        own_sends(u, lambda copy: copy.start())
+    for t in range(count + 5):
+        if t + 2 < count:
+            own_sends(t + 2, lambda copy: copy.start())
+        for s in (1, 2, 3):
+            at(line_step, t + 1 - s, s)
+        for s in (1, 2, 3):
+            at(plane_step, t - s, s)
+        for s in (1, 2, 3):
+            at(corner_step, t - 1 - s, s)
+        if t < count:
+            load(t).wait()
+            store(t).start()
+    for u in range(count):
+        finish(u)
+
+
+def gather_weights(shards):
+    layers, m_count = shards[0].shape[0], len(shards)
+    units = [(layer, m) for layer in range(layers) for m in range(m_count)]
+
+    def body(*refs):
+        gather_body(
+            units, refs[:m_count], refs[m_count : 2 * m_count], refs[2 * m_count : 3 * m_count], *refs[3 * m_count :]
+        )
+
+    return pl.pallas_call(
+        body,
+        out_shape=[jax.ShapeDtypeStruct((layers, ZN) + w.shape[1:], w.dtype) for w in shards],
+        in_specs=[pl.BlockSpec(memory_space=pl.ANY)] * m_count,
+        out_specs=[pl.BlockSpec(memory_space=pl.ANY)] * m_count,
+        scratch_shapes=[pltpu.VMEM(w.shape, w.dtype) for w in shards]
+        + [
+            pltpu.SemaphoreType.DMA((len(units),)),
+            pltpu.SemaphoreType.DMA((len(units),)),
+            pltpu.SemaphoreType.DMA((len(units), ZN, 7)),
+            pltpu.SemaphoreType.DMA((len(units), ZN, 7)),
+        ],
+        compiler_params=pltpu.CompilerParams(
+            collective_id=0, has_side_effects=True, vmem_limit_bytes=40 << 20
+        ),
+        name="gather_weights",
+    )(*shards)
+
+
+PAIRS = ((0, 1), (3, 2))
+RC, R1, R2, RL, RR, RX, RY, RD1, RD2, RCC, R1B = 0, 4, 8, 12, 16, 20, 21, 22, 23, 24, 25
+
+
+def reduce_body(ks, grads, outs, own, twin_in, first_in, second_in, low_in, high_in, load_sem, store_sem, send_sem, recv_sem):
+    x, y, z, c, across, beside, twin, up, down = neighbours()
+    greet(z, across, beside, twin, up, down)
+    units = [(m, h) for h in range(2) for m in range(len(grads))]
+    p = x * 2 + y
+
+    def move(source, target, m, kind, device):
+        return pltpu.make_async_remote_copy(
+            src_ref=source,
+            dst_ref=target,
+            send_sem=send_sem.at[m, kind],
+            recv_sem=recv_sem.at[m, kind],
+            device_id=device,
+            device_id_type=MESH,
+        )
+
+    def to_twin(m, d):
+        k = ks[m]
+        return move(grads[m].at[d, pl.ds((1 - c) * 4 * k, 4 * k)], twin_in[m].at[d], m, RC + d, twin)
+
+    def load(m, d):
+        k = ks[m]
+        return pltpu.make_async_copy(grads[m].at[d, pl.ds(c * 4 * k, 4 * k)], own[m].at[d], load_sem.at[m, d])
+
+    def add(m, d, at, extra, extra_at, n):
+        def step(i, carry):
+            own[m][d, at + i] = own[m][d, at + i] + extra[d, extra_at + i]
+            return carry
+
+        lax.fori_loop(0, n, step, 0)
+
+    def first_moves(u):
+        m, h = units[u]
+        k = ks[m]
+        a, b = PAIRS[h]
+        return [
+            move(own[m].at[a, pl.ds((1 - x) * 2 * k, 2 * k)], first_in[m].at[a], m, R1 + a, across),
+            move(own[m].at[b, pl.ds((1 - y) * k, k)], first_in[m].at[b, pl.ds(0, k)], m, R1 + b, beside),
+            move(own[m].at[b, pl.ds((3 - y) * k, k)], first_in[m].at[b, pl.ds(k, k)], m, R1B + h, beside),
+        ]
+
+    def second_moves(u):
+        m, h = units[u]
+        k = ks[m]
+        a, b = PAIRS[h]
+        return [
+            move(own[m].at[a, pl.ds((x * 2 + 1 - y) * k, k)], second_in[m].at[a], m, R2 + a, beside),
+            move(own[m].at[b, pl.ds(((1 - x) * 2 + y) * k, k)], second_in[m].at[b], m, R2 + b, across),
+        ]
+
+    def with_twin(u):
+        m, h = units[u]
+        for d in PAIRS[h]:
+            to_twin(m, d).wait_recv()
+            load(m, d).wait()
+            add(m, d, 0, twin_in[m], 0, 4 * ks[m])
+        for copy in first_moves(u):
+            copy.start()
+
+    def with_first(u):
+        m, h = units[u]
+        k = ks[m]
+        a, b = PAIRS[h]
+        for copy in first_moves(u):
+            copy.wait_recv()
+        add(m, a, x * 2 * k, first_in[m], 0, 2 * k)
+        add(m, b, y * k, first_in[m], 0, k)
+        add(m, b, (2 + y) * k, first_in[m], k, k)
+        for copy in second_moves(u):
+            copy.start()
+
+    def with_second(u):
+        m, h = units[u]
+        for copy in second_moves(u):
+            copy.wait_recv()
+        for d in PAIRS[h]:
+            add(m, d, p * ks[m], second_in[m], 0, ks[m])
+
+    def piece(m, d):
+        return own[m].at[d, pl.ds(p * ks[m], ks[m])]
+
+    def to_down(m, d):
+        return move(piece(m, d), high_in[m].at[d], m, RR + d, down)
+
+    def to_up(m, d):
+        return move(piece(m, d), low_in[m].at[d], m, RL + d, up)
+
+    def rows_of(m, px, py, low=0, n=None):
+        k = ks[m]
+        return outs[m].at[pl.ds((c * 4 + px * 2 + py) * k + low, k if n is None else n)]
+
+    def share_across(m):
+        return move(piece(m, z), rows_of(m, x, y), m, RX, across)
+
+    def share_beside(m):
+        return move(piece(m, z), rows_of(m, x, y), m, RY, beside)
+
+    def store(m):
+        return pltpu.make_async_copy(piece(m, z), rows_of(m, x, y), store_sem.at[m])
+
+    def arrived_across(m):
+        return move(rows_of(m, 1 - x, y), rows_of(m, 1 - x, y), m, RX, across)
+
+    def arrived_beside(m):
+        return move(rows_of(m, x, 1 - y), rows_of(m, x, 1 - y), m, RY, beside)
+
+    def corner(m, px, py, part):
+        k = ks[m]
+        low, n = (0, max(k // 2, 1)) if part == 0 else (k // 2, k - k // 2)
+        rows = rows_of(m, px, py, low, n)
+        return move(rows, rows, m, RD1 if part == 0 else RD2, beside if part == 0 else across)
+
+    def to_core(m, core):
+        rows = outs[m].at[pl.ds(core * 4 * ks[m], 4 * ks[m])]
+        return move(rows, rows, m, RCC, twin)
+
+    def line_step(u, s):
+        m, h = units[u]
+        for zz in range(ZN):
+            downward = [d for d in PAIRS[h] if d < zz] if zz == ZN - 1 - s else []
+            upward = [d for d in PAIRS[h] if d > zz] if zz == s else []
+            last = [d for d in PAIRS[h] if d == zz] if s == ZN - 1 else []
+            if not (downward or upward or last):
+                continue
+
+            @pl.when(z == zz)
+            def _():
+                for d in downward:
+                    if zz < ZN - 1:
+                        to_down(m, d).wait_recv()
+                        add(m, d, p * ks[m], high_in[m], 0, ks[m])
+                    to_down(m, d).start()
+                for d in upward:
+                    if zz > 0:
+                        to_up(m, d).wait_recv()
+                        add(m, d, p * ks[m], low_in[m], 0, ks[m])
+                    to_up(m, d).start()
+                for d in last:
+                    if zz > 0:
+                        to_up(m, d).wait_recv()
+                        add(m, d, p * ks[m], low_in[m], 0, ks[m])
+                    if zz < ZN - 1:
+                        to_down(m, d).wait_recv()
+                        add(m, d, p * ks[m], high_in[m], 0, ks[m])
+                    share_across(m).start()
+                    share_beside(m).start()
+                    store(m).start()
+
+    def where_mine(u, act):
+        m, h = units[u]
+
+        @pl.when((z >= min(PAIRS[h])) & (z <= max(PAIRS[h])))
+        def _():
+            act(m)
+
+    def corner_step(u):
+        def act(m):
+            arrived_across(m).wait_recv()
+            corner(m, 1 - x, y, 0).start()
+            arrived_beside(m).wait_recv()
+            if ks[m] > 1:
+                corner(m, x, 1 - y, 1).start()
+
+        where_mine(u, act)
+
+    def core_step(u):
+        def act(m):
+            store(m).wait()
+            corner(m, 1 - x, 1 - y, 0).wait_recv()
+            if ks[m] > 1:
+                corner(m, 1 - x, 1 - y, 1).wait_recv()
+            to_core(m, c).start()
+
+        where_mine(u, act)
+
+    def finish(u):
+        m, h = units[u]
+        for d in PAIRS[h]:
+            to_twin(m, d).wait_send()
+        for copy in first_moves(u) + second_moves(u):
+            copy.wait_send()
+        for zz in range(ZN):
+
+            @pl.when(z == zz)
+            def _():
+                for d in PAIRS[h]:
+                    if d < zz:
+                        to_down(m, d).wait_send()
+                    if d > zz:
+                        to_up(m, d).wait_send()
+
+        def act(m):
+            to_core(m, 1 - c).wait_recv()
+            share_across(m).wait_send()
+            share_beside(m).wait_send()
+            corner(m, 1 - x, y, 0).wait_send()
+            if ks[m] > 1:
+                corner(m, x, 1 - y, 1).wait_send()
+            to_core(m, c).wait_send()
+
+        where_mine(u, act)
+
+    count = len(units)
+
+    def at(step, u, *s):
+        if 0 <= u < count:
+            step(u, *s)
+
+    for u in range(count):
+        m, h = units[u]
+        for d in PAIRS[h]:
+            to_twin(m, d).start()
+            load(m, d).start()
+    for t in range(count + 8):
+        at(with_twin, t)
+        at(with_first, t - 1)
+        at(with_second, t - 2)
+        for s in range(ZN):
+            at(line_step, t - 2 - s, s)
+        at(corner_step, t - 6)
+        at(core_step, t - 7)
+    for u in range(count):
+        finish(u)
+
+
+def reduce_pieces(grads, ks):
+    m_count = len(grads)
+
+    def body(*refs):
+        groups = [refs[i * m_count : (i + 1) * m_count] for i in range(8)]
+        reduce_body(ks, *groups, *refs[8 * m_count :])
+
+    def buffers(rows):
+        return [pltpu.VMEM((ZN, rows * k) + g.shape[2:], g.dtype) for g, k in zip(grads, ks)]
+
+    return pl.pallas_call(
+        body,
+        out_shape=[jax.ShapeDtypeStruct((8 * k,) + g.shape[2:], g.dtype) for g, k in zip(grads, ks)],
+        in_specs=[pl.BlockSpec(memory_space=pl.ANY)] * m_count,
+        out_specs=[pl.BlockSpec(memory_space=pl.ANY)] * m_count,
+        scratch_shapes=buffers(4)
+        + buffers(4)
+        + buffers(2)
+        + buffers(1)
+        + buffers(1)
+        + buffers(1)
+        + [
+            pltpu.SemaphoreType.DMA((m_count, ZN)),
+            pltpu.SemaphoreType.DMA((m_count,)),
+            pltpu.SemaphoreType.DMA((m_count, 27)),
+            pltpu.SemaphoreType.DMA((m_count, 27)),
+        ],
+        compiler_params=pltpu.CompilerParams(
+            collective_id=1, has_side_effects=True, vmem_limit_bytes=60 << 20
+        ),
+        name="reduce_grads",
+    )(*grads)
+
+
+VECTORS = (0, 1, 3, 4, 6, 7, 8, 12, 10)
+MATRICES = (2, 5, 9, 11)
+WIDE = 13312
+
+
+def gather_all(params):
+    layers = params[0].shape[0]
+    shards = [params[i].reshape(layers, -1, 16, params[i].shape[2]) for i in MATRICES]
+    full = gather_weights(shards)
+    vectors = jnp.concatenate([params[i].reshape(layers, -1, params[0].shape[1]) for i in VECTORS], axis=1)
+    vectors = lax.all_gather(vectors, "fsdp", axis=2)
+    gathered = []
+    for layer in range(layers):
+        entry = [None] * 13
+        for at, i in enumerate(MATRICES):
+            entry[i] = full[at][layer].reshape(-1, params[i].shape[2])
+        row = 0
+        for i in VECTORS:
+            rows = params[i].shape[1] // params[0].shape[1]
+            entry[i] = jnp.moveaxis(vectors[layer, row : row + rows], 0, 1).reshape(-1)
+            row += rows
+        gathered.append(tuple(entry))
+    return gathered
+
+
+def reduce_layer(gradients):
+    low = [g.astype(jnp.bfloat16) for g in gradients]
+    mats = [low[i].reshape(ZN, -1, 16, low[i].shape[1]) for i in MATRICES]
+    rest = [jnp.swapaxes(g[:, g.shape[1] // 8 * 8 :], 1, 2).reshape(ZN, 16, -1) for g in mats]
+    vectors = jnp.concatenate([low[i].reshape(ZN, -1) for i in VECTORS], axis=1)
+    width = WIDE - sum(r.shape[2] for r in rest)
+    vectors = jnp.pad(vectors, ((0, 0), (0, 16 * width - vectors.shape[1]))).reshape(ZN, 16, width)
+    wide = jnp.concatenate(rest + [vectors], axis=2)
+    wide = jnp.swapaxes(wide.reshape(ZN, 16, 8, WIDE // 8), 1, 2)
+    ks = [g.shape[1] // 8 for g in mats] + [1]
+    sums = reduce_pieces(mats + [wide], ks)
+    tail = jnp.swapaxes(sums[-1], 0, 1).reshape(16, WIDE)
+    result = [None] * 13
+    col = 0
+    for at, i in enumerate(MATRICES):
+        columns = low[i].shape[1]
+        n = mats[at].shape[1] % 8
+        extra = jnp.swapaxes(tail[:, col : col + n * columns].reshape(16, n, columns), 0, 1)
+        col += n * columns
+        result[i] = jnp.concatenate([sums[at].reshape(-1, columns), extra.reshape(-1, columns)], axis=0)
+    flat = tail[:, col:].reshape(-1)
+    col = 0
+    for i in VECTORS:
+        n = low[i].shape[0] // ZN
+        result[i] = flat[col : col + n]
+        col += n
+    return tuple(r.astype(jnp.float32) for r in result)
+
+
+def on_cores(tokens, segments, grad_out, *params):
+    rows = tokens.shape[1]
+    own_x, grad_x = to_cores(tokens[0]), to_cores(grad_out[0])
+    seg_own = to_cores(segments[0])
+    core = lax.rem(lax.axis_index("rep"), 2)
+    pool = Cores()
+    places = jnp.concatenate(
+        [
+            core * rows + lax.iota(jnp.int32, rows // 2),
+            (3 - 2 * core) * (rows // 2) + lax.iota(jnp.int32, rows // 2),
+        ]
+    )
+    seg_all, places_all = pool.spread(seg_own), pool.spread(places)
+    visible = (seg_own[:, None] == seg_all[None, :]) & (places[:, None] >= places_all[None, :])
+    gathered = gather_all(params)
+    layer_count = params[0].shape[0]
+    resid = own_x.astype(jnp.float32)
+    stored_list = []
+    for layer_index in range(layer_count):
+        resid, stored = forward_layer(resid, gathered[layer_index], visible, pool)
+        stored_list.append(stored)
+    result = from_cores(resid.astype(jnp.bfloat16))[None]
+    grad_resid = grad_x.astype(jnp.float32)
+    reduced = [None] * layer_count
+    for layer_index in reversed(range(layer_count)):
+        grad_resid, gradients = backward_layer(
+            grad_resid, stored_list[layer_index], gathered[layer_index], visible, pool
+        )
+        reduced[layer_index] = reduce_layer(gradients)
+    stacked = tuple((jnp.stack([entry[member] for entry in reduced]) for member in range(13)))
+    return (result, from_cores(grad_resid.astype(jnp.bfloat16))[None]) + stacked
 
 
 def on_device(
@@ -422,7 +1023,7 @@
             w_down,
             b_down,
         )
-        resid, stored = forward_layer(resid, gathered, visible)
+        resid, stored = forward_layer(resid, gathered, visible, Halves())
         kept_weights.append(gathered)
         stored_list.append(stored)
     result = resid.astype(jnp.bfloat16)[None]
@@ -446,7 +1047,7 @@
             b_down,
         )
         grad_resid, gradients = backward_layer(
-            grad_resid, stored_list[layer_index], gathered, visible
+            grad_resid, stored_list[layer_index], gathered, visible, Halves()
         )
         reduced[layer_index] = reduce_grads(gradients)
     stacked = tuple((jnp.stack([entry[member] for entry in reduced]) for member in range(13)))
@@ -454,8 +1055,9 @@
 
 
 def solution(mesh):
+    fits = (mesh.shape["seq"], mesh.shape["fsdp"], mesh.shape["rep"]) == (2, ZN, 4)
     return jax.shard_map(
-        on_device,
+        on_cores if fits else on_device,
         mesh=mesh,
         in_specs=(
             P(("fsdp", "rep"), "seq", None),

time: 3020 us -> 1390 us (0.46)
  waiting for transfers between devices: 1110 us -> 1.18 us
  blocking collectives: 1110 us -> 13.1 us
  Pallas kernels: 0 us -> 605 us
  matrix products: 441 us -> 396 us
    unnamed x5 -> x0, blocking collectives: 1080 us -> none
    all_gather x18 -> x0, waiting for transfers between devices: 981 us -> none  [the longest x2 328 us: gather_layer(): lax.all_gather(w_down[layer_index], 'fsdp', axis=0, tiled=True)]
    pallas_call x0 -> x3, Pallas kernels: none -> 605 us  [the longest x2 396 us: reduce_pieces(): pl.pallas_call(body, out_shape=[jax.ShapeDtypeStruct((8 * k,) + g.shape[2...]
    psum x1 -> x0, waiting for transfers between devices: 107 us -> none  [reduce_grads(): lax.psum(shares[2].astype(jnp.bfloat16), 'seq').astype(jnp.float32)]
    unnamed x335 -> x317, local copies, waits for them, and re-layouts: 110 us -> 46.2 us
    slice x13 -> x21, local copies, waits for them, and re-layouts: 15.9 us -> 65.3 us  [the longest x4 36.7 us: gather_all(): entry[i] = full[at][layer].reshape(-1, params[i].shape[2])]
  transfers between devices with their start and end apart: 35 -> 20, of which waited for: 14 -> 1; matrix products, arithmetic and copies ran while one was open for 52% -> 22% of each run, Pallas kernels for 0% -> 15%
where the time goes in v1:
time: 1390 us; the launch traced here: 1370 us
  Pallas kernels  605 us (44%)
  matrix products  396 us (28%)
  local copies, waits for them, and re-layouts  179 us (13%)
  other arithmetic  152 us (11%)
  starting transfers between devices  22.7 us (2%)
    pallas_call x2, Pallas kernels, reduce_pieces(): pl.pallas_call(body, out_shape=[jax.ShapeDtypeStruct((8 * k,) + g.shape[2...  396 us
    pallas_call x1, Pallas kernels, gather_weights(): pl.pallas_call(body, out_shape=[jax.ShapeDtypeStruct((layers, ZN) + w.sha...  209 us
    dot_general x8, matrix products, outer_cols(): lax.dot_general(left, right, (((1,), (1,)), ((), ())), preferred_element_...  70.3 us
    dot_general x8, matrix products, inner_rows(): lax.dot_general(left, right, (((0,), (0,)), ((), ())), preferred_element_...  63.7 us
    dot_general x8, matrix products, product(): return jnp.dot(left, right, preferred_element_type=jnp.float32)  62.6 us
    convert_element_type x2, other arithmetic, backward_layer(): grad_scores = (weights_full * (grad_probs - inner_sum)).astype(jnp.bfloat16)  59.4 us
    dot_general x2, matrix products, backward_layer(): jnp.einsum('thd,shd->hts', grad_heads, value_heads, preferred_element_typ...  53.1 us
    unnamed x317, local copies, waits for them, and re-layouts  46.2 us
  transfers between devices with their start and end apart: 20, of which 1 were waited for; matrix products, arithmetic and copies ran while one was open for 22% of the time, Pallas kernels for 15%

profile of v1, /device:TPU:25, one launch (start us, length us, event | category | flops | bytes accessed | tf_op | source)
XLA Modules:
  0.0 1372.6 jit_solution(3127847521331540115)
XLA Ops:
  10.6 13.1 all-gather
  36.6 209.1 %gather_weights.1 = (bf16[2,4,17,16,3264]{4,3,2,1,0:T(8,128)(2,1)}, bf16[2,4,17,16,1088]{4,3,2,1,0:T(8,128)(2,1)}, bf16[2,4,17,16,4352]{4,3,2,1,0:T(8,128)(2,1)}, bf16[2,4,68,16,1088]{4,3,2,1,0:T(8,128)(2,1)}) custom-call(bf16[2,17,16,3264]{3,2,1,0:T(8,128)(2,1)S(1)} %bitcast.258, bf16[2,17,16,1088]{3,2,1,0:T(8,128)(2,1)S(1)} %bitcast.259, ...), custom_call_target="tpu_custom_call" | custom-call | tf_op jit(solution)/shard_map/gather_weights/pallas_call | solution.py:614
  272.5 14.6 %fusion.102 = (bf16[1,4,17,16,4352]{4,3,2,1,0:T(8,128)(2,1)}, bf16[1,4,17,16,4352]{4,3,2,1,0:T(8,128)(2,1)}) fusion(bf16[2,4,17,16,4352]{4,3,2,1,0:T(8,128)(2,1)} %get-tuple-element.31), kind=kLoop, calls=%fused_computation.234 | loop fusion | bytes 37879808 | tf_op jit(solution)/shard_map/slice | solution.py:911
  342.3 14.3 %select_reduce_fusion.1 = (f32[17,512]{1,0:T(8,128)S(1)}, f32[17,512,1024]{2,1,0:T(8,128)}) fusion(pred[512,1024]{1,0:T(8,128)(4,1)S(1)} %compare_and_fusion, bf16[512,17,64]{0,2,1:T(8,128)(2,1)S(1)} %bitcast.286, bf16[1024,17,64]{0,2,1:T(8,128)(2,1)S(1)} %bitcast.278), kind=kOutput, calls=%fused_computation.13 | convolution fusion | flops 1158667776 | bytes 39553024 | tf_op jit(solution)/shard_map/thd,shd->hts/dot_general | solution.py:57
  356.6 15.6 %fusion = f32[17,512]{1,0:T(8,128)S(1)} fusion(f32[17,512,1024]{2,1,0:T(8,128)} %get-tuple-element.146, f32[17,512]{1,0:T(8,128)S(1)} %get-tuple-element.145, pred[512,1024]{1,0:T(8,128)(4,1)S(1)} %compare_and_fusion), kind=kLoop, calls=%fused_computation.10 | loop fusion | flops 26729984 | bytes 36245504 | tf_op jit(solution)/shard_map/reduce_sum | solution.py:159
  374.2 17.0 %fusion.57 = bf16[17,64,512]{2,1,0:T(8,128)(2,1)S(1)} fusion(bf16[1024,17,64]{0,2,1:T(8,128)(2,1)S(1)} %bitcast.282, f32[17,512,1024]{2,1,0:T(8,128)} %get-tuple-element.146, f32[17,512]{1,0:T(8,128)S(1)} %fusion, f32[17,512]{1,0:T(8,128)S(1)} %get-tuple-element.145, pred[512,1024]{1,0:T(8,128)(4,1)S(1)} %compare_and_fusion), kind=kOutput, calls=%fused_computation.129 | convolution fusion | flops 1177059328 | bytes 39587840 | tf_op jit(solution)/shard_map/hts,shd->thd/dot_general | solution.py:163
  433.1 14.2 %select_reduce_fusion = (f32[17,512]{1,0:T(8,128)S(1)}, f32[17,512,1024]{2,1,0:T(8,128)}) fusion(pred[512,1024]{1,0:T(8,128)(4,1)S(1)} %compare_and_fusion, bf16[512,17,64]{0,2,1:T(8,128)(2,1)S(1)} %bitcast.288, bf16[1024,17,64]{0,2,1:T(8,128)(2,1)S(1)} %bitcast.280), kind=kOutput, calls=%fused_computation.12 | convolution fusion | flops 1158667776 | bytes 39553024 | tf_op jit(solution)/shard_map/thd,shd->hts/dot_general | solution.py:57
  447.4 15.6 %fusion.1 = f32[17,512]{1,0:T(8,128)S(1)} fusion(f32[17,512,1024]{2,1,0:T(8,128)} %get-tuple-element.152, f32[17,512]{1,0:T(8,128)S(1)} %get-tuple-element.151, pred[512,1024]{1,0:T(8,128)(4,1)S(1)} %compare_and_fusion), kind=kLoop, calls=%fused_computation.11 | loop fusion | flops 26729984 | bytes 36245504 | tf_op jit(solution)/shard_map/reduce_sum | solution.py:159
  464.6 17.6 %fusion.56 = bf16[17,64,512]{2,1,0:T(8,128)(2,1)} fusion(bf16[1024,17,64]{0,2,1:T(8,128)(2,1)S(1)} %bitcast.284, f32[17,512,1024]{2,1,0:T(8,128)} %get-tuple-element.152, f32[17,512]{1,0:T(8,128)S(1)} %fusion.1, f32[17,512]{1,0:T(8,128)S(1)} %get-tuple-element.151, pred[512,1024]{1,0:T(8,128)(4,1)S(1)} %compare_and_fusion), kind=kOutput, calls=%fused_computation.128 | convolution fusion | flops 1177059328 | bytes 39587840 | tf_op jit(solution)/shard_map/hts,shd->thd/dot_general | solution.py:163
  494.7 15.9 %fusion.94 = (bf16[4352]{0:T(1024)(128)(2,1)}, bf16[512,4352]{1,0:T(8,128)(2,1)}) fusion(f32[512,4352]{1,0:T(8,128)} %fusion.88, f32[4352]{0:T(1024)S(1)} %copy-done.78, bf16[512,1088]{0,1:T(8,128)(2,1)} %get-tuple-element.102, bf16[4352,1088]{1,0:T(8,128)(2,1)} %bitcast.296), kind=kOutput, calls=%fused_computation.228 | convolution fusion | flops 4897632256 | bytes 23979520 | tf_op jit(solution)/shard_map/dot_general | solution.py:39
  525.3 17.1 %convert_bitcast_fusion.2 = bf16[1024,17,64]{0,2,1:T(8,128)(2,1)} fusion(bf16[512,17,64]{0,2,1:T(8,128)(2,1)} %bitcast.325, f32[17,512,1024]{2,1,0:T(8,128)} %get-tuple-element.152, f32[17,512]{1,0:T(8,128)S(1)} %log_add_fusion, pred[512,1024]{1,0:T(8,128)(4,1)S(1)} %compare_and_fusion), kind=kOutput, calls=%fused_computation.113 | convolution fusion | flops 1168703488 | bytes 39553024 | tf_op jit(solution)/shard_map/hts,thd->shd/dot_general | solution.py:249
  542.5 26.5 %multiply_reduce_fusion.1 = (f32[17,512]{1,0:T(8,128)S(1)}, f32[17,512,1024]{2,1,0:T(8,128)}) fusion(f32[17,512,1024]{2,1,0:T(8,128)} %get-tuple-element.152, f32[17,512]{1,0:T(8,128)S(1)} %log_add_fusion, pred[512,1024]{1,0:T(8,128)(4,1)S(1)} %compare_and_fusion, bf16[512,17,64]{0,2,1:T(8,128)(2,1)} %bitcast.326, bf16[1024,17,64]{0,2,1:T(8,128)(2,1)} %bitcast.285), kind=kOutput, calls=%fused_computation.3 | convolution fusion | flops 1176493568 | bytes 75239424 | tf_op jit(solution)/shard_map/thd,shd->hts/dot_general | solution.py:252
  569.0 29.6 %multiply_convert_fusion.1 = bf16[17,512,1024]{2,1,0:T(8,128)(2,1)} fusion(f32[17,512,1024]{2,1,0:T(8,128)} %get-tuple-element.157, f32[17,512,1024]{2,1,0:T(8,128)} %get-tuple-element.152, f32[17,512]{1,0:T(8,128)S(1)} %get-tuple-element.156, f32[17,512]{1,0:T(8,128)S(1)} %log_add_fusion, pred[512,1024]{1,0:T(8,128)(4,1)S(1)} %compare_and_fusion), kind=kLoop, calls=%fused_computation.2 | loop fusion | flops 44564480 | bytes 89722880 | tf_op jit(solution)/shard_map/convert_element_type | solution.py:256
  609.6 13.3 fusion.123
  645.9 13.0 fusion.38
  671.6 14.3 %copy.107 = bf16[4352,1088]{1,0:T(8,128)(2,1)} copy(bf16[4352,1088]{0,1:T(8,128)(2,1)} %convolution_convert_fusion) | data formatting | bytes 18939904 | tf_op jit(solution)/shard_map/convert_element_type | solution.py:922
  719.7 16.6 %fusion.125 = (bf16[4352]{0:T(1024)(128)(2,1)}, bf16[512,4352]{1,0:T(8,128)(2,1)}) fusion(f32[512,4352]{1,0:T(8,128)} %fusion.86, f32[4352]{0:T(1024)S(1)} %copy-done.77, bf16[4352,1088]{1,0:T(8,128)(2,1)} %bitcast.295, f32[512,1088]{0,1:T(8,128)} %get-tuple-element.58), kind=kOutput, calls=%fused_computation.257 | convolution fusion | flops 4898189312 | bytes 25093632 | tf_op jit(solution)/shard_map/dot_general | solution.py:39
  751.4 17.3 %convert_bitcast_fusion = bf16[1024,17,64]{0,2,1:T(8,128)(2,1)} fusion(bf16[512,17,64]{0,2,1:T(8,128)(2,1)} %bitcast.327, f32[17,512,1024]{2,1,0:T(8,128)} %get-tuple-element.146, f32[17,512]{1,0:T(8,128)S(1)} %copy-done.51, pred[512,1024]{1,0:T(8,128)(4,1)S(1)} %compare_and_fusion), kind=kOutput, calls=%fused_computation.107 | convolution fusion | flops 1168703488 | bytes 39553024 | tf_op jit(solution)/shard_map/hts,thd->shd/dot_general | solution.py:249
  768.7 26.6 %multiply_reduce_fusion = (f32[17,512]{1,0:T(8,128)S(1)}, f32[17,512,1024]{2,1,0:T(8,128)}) fusion(f32[17,512,1024]{2,1,0:T(8,128)} %get-tuple-element.146, f32[17,512]{1,0:T(8,128)S(1)} %copy-done.51, pred[512,1024]{1,0:T(8,128)(4,1)S(1)} %compare_and_fusion, bf16[512,17,64]{0,2,1:T(8,128)(2,1)} %bitcast.328, bf16[1024,17,64]{0,2,1:T(8,128)(2,1)} %bitcast.283), kind=kOutput, calls=%fused_computation.1 | convolution fusion | flops 1176493568 | bytes 75239424 | tf_op jit(solution)/shard_map/thd,shd->hts/dot_general | solution.py:252
  795.3 29.8 %multiply_convert_fusion = bf16[17,512,1024]{2,1,0:T(8,128)(2,1)} fusion(f32[17,512,1024]{2,1,0:T(8,128)} %get-tuple-element.161, f32[17,512,1024]{2,1,0:T(8,128)} %get-tuple-element.146, f32[17,512]{1,0:T(8,128)S(1)} %get-tuple-element.160, f32[17,512]{1,0:T(8,128)S(1)} %copy-done.51, pred[512,1024]{1,0:T(8,128)(4,1)S(1)} %compare_and_fusion), kind=kLoop, calls=%fused_computation | loop fusion | flops 44564480 | bytes 89722880 | tf_op jit(solution)/shard_map/convert_element_type | solution.py:256
  836.1 13.3 fusion.124
  886.5 199.4 %reduce_grads.3 = (bf16[16,16,3264]{2,1,0:T(8,128)(2,1)}, bf16[16,16,1088]{2,1,0:T(8,128)(2,1)}, bf16[16,16,4352]{2,1,0:T(8,128)(2,1)}, bf16[64,16,1088]{2,1,0:T(8,128)(2,1)}, bf16[8,16,1664]{2,1,0:T(8,128)(2,1)}) custom-call(bf16[4,17,16,3264]{3,2,1,0:T(8,128)(2,1)} %bitcast.299, bf16[4,17,16,1088]{3,2,1,0:T(8,128)(2,1)} %bitcast.316, ...), custom_call_target="tpu_custom_call" | custom-call | tf_op jit(solution)/shard_map/reduce_grads/pallas_call | solution.py:872
  1092.3 13.9 %copy.101 = bf16[4352,1088]{1,0:T(8,128)(2,1)} copy(bf16[4352,1088]{0,1:T(8,128)(2,1)} %convolution_convert_fusion.1) | data formatting | bytes 18939904 | tf_op jit(solution)/shard_map/convert_element_type | solution.py:922
  1140.5 196.8 %reduce_grads.2 = (bf16[16,16,3264]{2,1,0:T(8,128)(2,1)}, bf16[16,16,1088]{2,1,0:T(8,128)(2,1)}, bf16[16,16,4352]{2,1,0:T(8,128)(2,1)}, bf16[64,16,1088]{2,1,0:T(8,128)(2,1)}, bf16[8,16,1664]{2,1,0:T(8,128)(2,1)}) custom-call(bf16[4,17,16,3264]{3,2,1,0:T(8,128)(2,1)} %bitcast.301, bf16[4,17,16,1088]{3,2,1,0:T(8,128)(2,1)} %bitcast.314, ...), custom_call_target="tpu_custom_call" | custom-call | tf_op jit(solution)/shard_map/reduce_grads/pallas_call | solution.py:872
  (573 shorter events, 395.2 us)
Async XLA Ops:
  3.1 327.4 %collective-permute-start.1 = (bf16[256,1088]{0,1:T(8,128)(2,1)}, bf16[256,1088]{0,1:T(8,128)(2,1)S(1)}, u32[]{:S(2)}, u32[]{:S(2)}) collective-permute-start(bf16[256,1088]{0,1:T(8,128)(2,1)} %get-tuple-element.100), channel_id=1, source_target_pairs={{0,1},{1,17},{2,3},{3,19},{16,0},{17,16},{18,2},{19,18},{4,5},{5,2... | collective-permute-start | bytes 1671176 | tf_op jit(solution)/shard_map/ppermute | solution.py:399
  4.4 326.2 %collective-permute-start = (bf16[256,1088]{0,1:T(8,128)(2,1)}, bf16[256,1088]{0,1:T(8,128)(2,1)S(1)}, u32[]{:S(2)}, u32[]{:S(2)}) collective-permute-start(bf16[256,1088]{0,1:T(8,128)(2,1)} %get-tuple-element.99), channel_id=1, source_target_pairs={{0,0},{1,16},{2,2},{3,18},{16,1},{17,17},{18,3},{19,19},{4,4},{5,2... | collective-permute-start | bytes 1671176 | tf_op jit(solution)/shard_map/ppermute | solution.py:398
  7.4 322.0 %collective-permute-start.6 = (s32[512]{0:T(512)S(1)}, s32[512]{0:T(512)S(1)}, u32[]{:S(2)}, u32[]{:S(2)}) collective-permute-start(s32[512]{0:T(512)S(1)} %pad_add_fusion.2), channel_id=1, source_target_pairs={{0,1},{1,0},{2,3},{3,2},{4,5},{5,4},{6,7},{7,6},{8,9},{9,8},{10,11... | collective-permute-start | bytes 6152 | tf_op jit(solution)/shard_map/ppermute | solution.py:382
  7.5 317.9 %collective-permute-start.3 = (s32[256]{0:T(256)S(1)}, s32[256]{0:T(256)S(1)}, u32[]{:S(2)}, u32[]{:S(2)}) collective-permute-start(s32[256]{0:T(256)S(1)} %bitcast.368), channel_id=1, source_target_pairs={{0,0},{1,16},{2,2},{3,18},{16,1},{17,17},{18,3},{19,19},{4,4},{5,2... | collective-permute-start | bytes 3080 | tf_op jit(solution)/shard_map/ppermute | solution.py:398
  10.1 316.7 %collective-permute-start.4 = (s32[256]{0:T(256)S(1)}, s32[256]{0:T(256)S(1)}, u32[]{:S(2)}, u32[]{:S(2)}) collective-permute-start(s32[256]{0:T(256)S(1)} %bitcast.367), channel_id=1, source_target_pairs={{0,1},{1,17},{2,3},{3,19},{16,0},{17,16},{18,2},{19,18},{4,5},{5,2... | collective-permute-start | bytes 3080 | tf_op jit(solution)/shard_map/ppermute | solution.py:399
  314.9 99.9 %copy-start.105 = (f32[1088]{0:T(1024)}, f32[1088]{0:T(1024)S(1)}, u32[]{:S(2)}) copy-start(f32[1088]{0:T(1024)S(1)} %reshape.899) | copy-start | bytes 13060
  325.4 100.6 %collective-permute-start.13 = (bf16[256,1088]{0,1:T(8,128)(2,1)}, bf16[256,1088]{0,1:T(8,128)(2,1)S(1)}, u32[]{:S(2)}, u32[]{:S(2)}) collective-permute-start(bf16[256,1088]{0,1:T(8,128)(2,1)} %get-tuple-element.95), channel_id=1, source_target_pairs={{0,1},{1,17},{2,3},{3,19},{16,0},{17,16},{18,2},{19,18},{4,5},{5,2... | collective-permute-start | bytes 1671176 | tf_op jit(solution)/shard_map/ppermute | solution.py:399
  326.7 14.4 %collective-permute-start.12 = (bf16[256,1088]{0,1:T(8,128)(2,1)}, bf16[256,1088]{0,1:T(8,128)(2,1)S(1)}, u32[]{:S(2)}, u32[]{:S(2)}) collective-permute-start(bf16[256,1088]{0,1:T(8,128)(2,1)} %get-tuple-element.96), channel_id=1, source_target_pairs={{0,0},{1,16},{2,2},{3,18},{16,1},{17,17},{18,3},{19,19},{4,4},{5,2... | collective-permute-start | bytes 1671176 | tf_op jit(solution)/shard_map/ppermute | solution.py:398
  329.3 1.2 collective-permute-start.5
  338.7 3.4 collective-permute-start.7
  340.8 31.5 %collective-permute-start.2 = (bf16[512,1088]{0,1:T(8,128)(2,1)}, bf16[512,1088]{0,1:T(8,128)(2,1)}, u32[]{:S(2)}, u32[]{:S(2)}) collective-permute-start(bf16[512,1088]{0,1:T(8,128)(2,1)} %get-tuple-element.82), channel_id=1, source_target_pairs={{0,1},{1,0},{2,3},{3,2},{4,5},{5,4},{6,7},{7,6},{8,9},{9,8},{10,11... | collective-permute-start | bytes 3342344 | tf_op jit(solution)/shard_map/ppermute | solution.py:382
  425.7 5.5 collective-permute-start.9
  430.3 32.7 %collective-permute-start.8 = (bf16[512,1088]{0,1:T(8,128)(2,1)S(1)}, bf16[512,1088]{0,1:T(8,128)(2,1)}, u32[]{:S(2)}, u32[]{:S(2)}) collective-permute-start(bf16[512,1088]{0,1:T(8,128)(2,1)S(1)} %get-tuple-element.80), channel_id=1, source_target_pairs={{0,1},{1,0},{2,3},{3,2},{4,5},{5,4},{6,7},{7,6},{8,9},{9,8},{10,11... | collective-permute-start | bytes 3342344 | tf_op jit(solution)/shard_map/ppermute | solution.py:382
  661.4 37.2 %collective-permute-start.11 = (bf16[256,1088]{0,1:T(8,128)(2,1)}, bf16[256,1088]{0,1:T(8,128)(2,1)}, u32[]{:S(2)}, u32[]{:S(2)}) collective-permute-start(bf16[256,1088]{0,1:T(8,128)(2,1)} %get-tuple-element.98), channel_id=1, source_target_pairs={{1,0},{17,1},{3,2},{19,3},{0,16},{16,17},{2,18},{18,19},{5,4},{21,... | collective-permute-start | bytes 1671176 | tf_op jit(solution)/shard_map/ppermute | solution.py:413
  661.6 37.0 %collective-permute-start.10 = (bf16[256,1088]{0,1:T(8,128)(2,1)}, bf16[256,1088]{0,1:T(8,128)(2,1)}, u32[]{:S(2)}, u32[]{:S(2)}) collective-permute-start(bf16[256,1088]{0,1:T(8,128)(2,1)} %get-tuple-element.97), channel_id=1, source_target_pairs={{0,0},{16,1},{2,2},{18,3},{1,16},{17,17},{3,18},{19,19},{4,4},{20,... | collective-permute-start | bytes 1671176 | tf_op jit(solution)/shard_map/ppermute | solution.py:412
  666.2 34.7 %collective-permute-start.15 = (bf16[512,1088]{0,1:T(8,128)(2,1)}, bf16[512,1088]{0,1:T(8,128)(2,1)}, u32[]{:S(2)}, u32[]{:S(2)}) collective-permute-start(bf16[512,1088]{0,1:T(8,128)(2,1)} %bitcast.50), channel_id=1, source_target_pairs={{0,1},{1,0},{2,3},{3,2},{4,5},{5,4},{6,7},{7,6},{8,9},{9,8},{10,11... | collective-permute-start | bytes 3342344 | tf_op jit(solution)/shard_map/ppermute | solution.py:387
  671.6 31.6 %collective-permute-start.14 = (bf16[512,1088]{0,1:T(8,128)(2,1)}, bf16[512,1088]{0,1:T(8,128)(2,1)}, u32[]{:S(2)}, u32[]{:S(2)}) collective-permute-start(bf16[512,1088]{0,1:T(8,128)(2,1)} %bitcast.47), channel_id=1, source_target_pairs={{0,1},{1,0},{2,3},{3,2},{4,5},{5,4},{6,7},{7,6},{8,9},{9,8},{10,11... | collective-permute-start | bytes 3342344 | tf_op jit(solution)/shard_map/ppermute | solution.py:387
  886.5 201.9 %copy-start.35 = (bf16[1024,17,64]{0,2,1:T(8,128)(2,1)S(1)}, bf16[1024,17,64]{0,2,1:T(8,128)(2,1)}, u32[]{:S(2)}) copy-start(bf16[1024,17,64]{0,2,1:T(8,128)(2,1)} %convert_bitcast_fusion) | copy-start | bytes 6684676
  1089.7 27.1 %collective-permute-start.17 = (bf16[512,1088]{0,1:T(8,128)(2,1)}, bf16[512,1088]{0,1:T(8,128)(2,1)}, u32[]{:S(2)}, u32[]{:S(2)}) collective-permute-start(bf16[512,1088]{0,1:T(8,128)(2,1)} %bitcast.59), channel_id=1, source_target_pairs={{0,1},{1,0},{2,3},{3,2},{4,5},{5,4},{6,7},{7,6},{8,9},{9,8},{10,11... | collective-permute-start | bytes 3342344 | tf_op jit(solution)/shard_map/ppermute | solution.py:387
  1092.2 26.4 %collective-permute-start.16 = (bf16[512,1088]{0,1:T(8,128)(2,1)}, bf16[512,1088]{0,1:T(8,128)(2,1)}, u32[]{:S(2)}, u32[]{:S(2)}) collective-permute-start(bf16[512,1088]{0,1:T(8,128)(2,1)} %bitcast.56), channel_id=1, source_target_pairs={{0,1},{1,0},{2,3},{3,2},{4,5},{5,4},{6,7},{7,6},{8,9},{9,8},{10,11... | collective-permute-start | bytes 3342344 | tf_op jit(solution)/shard_map/ppermute | solution.py:387
  1140.5 199.9 %copy-start.6 = (f32[512,1088]{0,1:T(8,128)S(1)}, f32[512,1088]{0,1:T(8,128)}, u32[]{:S(2)}) copy-start(f32[512,1088]{0,1:T(8,128)} %get-tuple-element.58) | copy-start | bytes 6684676
  1140.5 199.9 %copy-start.84 = (f32[512]{0:T(512)S(1)}, f32[512]{0:T(512)}, u32[]{:S(2)}) copy-start(f32[512]{0:T(512)} %copy-done.83) | copy-start | bytes 6148
  1344.7 25.3 %collective-permute-start.19 = (bf16[256,1088]{0,1:T(8,128)(2,1)}, bf16[256,1088]{0,1:T(8,128)(2,1)}, u32[]{:S(2)}, u32[]{:S(2)}) collective-permute-start(bf16[256,1088]{0,1:T(8,128)(2,1)} %get-tuple-element.94), channel_id=1, source_target_pairs={{1,0},{17,1},{3,2},{19,3},{0,16},{16,17},{2,18},{18,19},{5,4},{21,... | collective-permute-start | bytes 1671176 | tf_op jit(solution)/shard_map/ppermute | solution.py:413
  1344.8 25.2 %collective-permute-start.18 = (bf16[256,1088]{0,1:T(8,128)(2,1)}, bf16[256,1088]{0,1:T(8,128)(2,1)}, u32[]{:S(2)}, u32[]{:S(2)}) collective-permute-start(bf16[256,1088]{0,1:T(8,128)(2,1)} %get-tuple-element.93), channel_id=1, source_target_pairs={{0,0},{16,1},{2,2},{18,3},{1,16},{17,17},{3,18},{19,19},{4,4},{20,... | collective-permute-start | bytes 1671176 | tf_op jit(solution)/shard_map/ppermute | solution.py:412
  (142 other events, 1746.8 us)

commit v2 on v1

--- a/solution.py
+++ b/solution.py
@@ -1,3 +1,4 @@
+import functools
 import math
 
 import jax
@@ -375,33 +376,6 @@
         return lax.psum_scatter(rows, "seq", scatter_dimension=0, tiled=True)
 
 
-class Cores:
-    swap = [(0, 1), (1, 0), (2, 3), (3, 2)]
-
-    def spread(self, rows):
-        other = lax.ppermute(rows, "rep", self.swap)
-        return jnp.concatenate([rows, other], axis=0)
-
-    def collect(self, rows):
-        half = rows.shape[0] // 2
-        other = lax.ppermute(rows[half:], "rep", self.swap)
-        return rows[:half] + other
-
-
-def to_cores(rows):
-    half = rows.shape[0] // 2
-    spots = [(x, y, c) for x in range(2) for y in range(2) for c in range(2)]
-    first = [(x * 4 + y * 2 + c, c * 4 + y * 2 + x) for x, y, c in spots]
-    second = [(x * 4 + y * 2 + c, c * 4 + y * 2 + 1 - x) for x, y, c in spots]
-    return jnp.concatenate(
-        [
-            lax.ppermute(rows[:half], ("seq", "rep"), first),
-            lax.ppermute(rows[half:], ("seq", "rep"), second),
-        ],
-        axis=0,
-    )
-
-
 def from_cores(rows):
     half = rows.shape[0] // 2
     spots = [(x, y, c) for x in range(2) for y in range(2) for c in range(2)]
@@ -430,7 +404,7 @@
     return x, y, z, c, across, beside, twin, up, down
 
 
-def greet(z, across, beside, twin, up, down):
+def greet(z, c, x, across, beside, twin, diag, up, down):
     barrier = pltpu.get_barrier_semaphore()
 
     def tell(device):
@@ -438,6 +412,11 @@
 
     for device in (across, beside, twin):
         tell(device)
+    if diag is not None:
+
+        @pl.when(c != x)
+        def _():
+            tell(diag)
 
     @pl.when(z < ZN - 1)
     def _():
@@ -447,64 +426,175 @@
     def _():
         tell(down)
 
-    pl.semaphore_wait(barrier, 3 + (z + ZN - 1) // ZN + (2 * ZN - 2 - z) // ZN)
+    extra = 0 if diag is None else (x + c) % 2
+    pl.semaphore_wait(barrier, 3 + extra + (z + ZN - 1) // ZN + (2 * ZN - 2 - z) // ZN)
+
+
+GELU_A = math.sqrt(2.0 / math.pi)
+GELU_B = 0.044715
+QUERY_SCALE = 1.0 / math.sqrt(HEAD_DIM)
+HEAD_ROWS = 24
+PACE = 2
+
+
+NT = (((1,), (1,)), ((), ()))
+TN = (((0,), (0,)), ((), ()))
+BLOCK = 256
+RANGES = (((0, 256), (256, 1024)), ((0, 768), (256, 512)))
+VMEM_LIMIT = 60 << 20
+
+
+def dot_nt(left, right):
+    return lax.dot_general(left, right, NT, preferred_element_type=jnp.float32)
+
+
+def dot_tn(left, right):
+    return lax.dot_general(left, right, TN, preferred_element_type=jnp.float32)
+
+
+def tiles(width, tile, act):
+    whole = width // tile
+
+    def step(i, carry):
+        act(pl.multiple_of(i * tile, tile), tile)
+        return carry
+
+    lax.fori_loop(0, whole, step, 0)
+    if width % tile:
+        act(whole * tile, width % tile)
+
+
+def tiles_between(low, high, tile, act):
+    def step(i, carry):
+        act(pl.multiple_of(i * tile, tile), tile)
+        return carry
+
+    if low // tile < high // tile:
+        lax.fori_loop(low // tile, high // tile, step, 0)
+    if high % tile:
+        act(high // tile * tile, high % tile)
+
+
+def norm_parts(rows):
+    center = rows - jnp.mean(rows, axis=1, keepdims=True)
+    scale = lax.rsqrt(jnp.mean(center * center, axis=1, keepdims=True) + NORM_EPSILON)
+    return center * scale, scale
+
+
+def norm_into(source, gain, shift, target):
+    def act(start, size):
+        rows = pl.ds(start, size)
+        unit, _ = norm_parts(source[rows, :])
+        target[rows, :] = (unit * gain + shift).astype(target.dtype)
+
+    tiles(source.shape[0], 64, act)
+
+
+def norm_back(source, grad, extra, gain, target, gain_grad, shift_grad, low=None):
+    gain_grad[...] = jnp.zeros_like(gain_grad)
+    shift_grad[...] = jnp.zeros_like(shift_grad)
+
+    def act(start, size):
+        rows = pl.ds(start, size)
+        unit, scale = norm_parts(source[rows, :])
+        g = grad[rows, :]
+        q = g * gain
+        mean_q = jnp.mean(q, axis=1, keepdims=True)
+        mean_qn = jnp.mean(q * unit, axis=1, keepdims=True)
+        out = extra[rows, :] + (q - mean_q - unit * mean_qn) * scale
+        target[rows, :] = out
+        if low is not None:
+            low[rows, :] = out.astype(low.dtype)
+        gain_grad[...] += jnp.sum(g * unit, axis=0, keepdims=True)
+        shift_grad[...] += jnp.sum(g, axis=0, keepdims=True)
+
+    tiles(source.shape[0], 64, act)
+
+
+def whole(count):
+    return [pl.BlockSpec(memory_space=pltpu.VMEM)] * count
+
+
+def anywhere(count):
+    return [pl.BlockSpec(memory_space=pl.ANY)] * count
+
+
+def shaped(shape, dtype=jnp.float32):
+    return jax.ShapeDtypeStruct(shape, dtype)
+
+
+def params():
+    return pltpu.CompilerParams(vmem_limit_bytes=VMEM_LIMIT)
+
+
+def of_head(values, j):
+    if values.shape[1] == HEAD_DIM:
+        return values
+    lane = lax.broadcasted_iota(jnp.int32, values.shape, 1)
+    return jnp.where(lane // HEAD_DIM == j, values, jnp.zeros_like(values))
 
 
 ZA, ZR, GX, GY, GD1, GD2, GC = range(7)
-
-
-def gather_body(units, ins, outs, holds, load_sem, store_sem, send_sem, recv_sem):
-    x, y, z, c, across, beside, twin, up, down = neighbours()
-    greet(z, across, beside, twin, up, down)
+ROW = dict(attn_gain=0, attn_shift=1, b_query=2, b_value=3, b_out=4, mlp_gain=5, mlp_shift=6, b_down=7)
+SAVED = ("x", "normed_attn", "q", "keys", "values", "attended", "lse", "middle", "normed_mlp", "slope", "activated")
+
+
+def advance(steps, count):
+    for _ in range(count):
+        if next(steps, None) is None:
+            return
+
+
+def weight_moves(ins, outs, send_sem, recv_sem, place):
+    x, y, z, c, across, beside, twin, up, down = place
+    m_count = len(ins) - 1
+    layers = ins[0].shape[0]
+    units = [(layer, m) for layer in range(layers) for m in range(m_count + 1)]
+    index = {unit: i for i, unit in enumerate(units)}
+
+    def depth(u):
+        return ins[u[1]].shape[1] // 8
 
     def owned(u, px, py, half=None):
-        k = ins[units[u][1]].shape[1] // 8
+        k = depth(u)
         base = (c * 4 + px * 2 + py) * k
         if half is None:
             return pl.ds(base, k)
         return pl.ds(base + half * (k // 2), k // 2)
 
     def rest(u):
-        n = ins[units[u][1]].shape[1]
+        n = ins[u[1]].shape[1]
         return pl.ds(n // 8 * 8, n % 8)
 
     def slab(u, core):
-        k = ins[units[u][1]].shape[1] // 8
-        return pl.ds(core * 4 * k, 4 * k)
+        return pl.ds(core * 4 * depth(u), 4 * depth(u))
 
     def move(u, zz, rows, device, kind, source=None, send_kind=None):
-        layer, m = units[u]
-        target = outs[m].at[layer, zz, rows]
+        target = outs[u[1]].at[u[0], zz, rows]
         return pltpu.make_async_remote_copy(
             src_ref=target if source is None else source,
             dst_ref=target,
-            send_sem=send_sem.at[u, zz, kind if send_kind is None else send_kind],
-            recv_sem=recv_sem.at[u, zz, kind],
+            send_sem=send_sem.at[index[u], zz, kind if send_kind is None else send_kind],
+            recv_sem=recv_sem.at[index[u], zz, kind],
             device_id=device,
             device_id_type=MESH,
         )
 
-    def load(u):
-        layer, m = units[u]
-        return pltpu.make_async_copy(ins[m].at[layer], holds[m].at[layer], load_sem.at[u])
-
-    def store(u):
-        layer, m = units[u]
-        return pltpu.make_async_copy(holds[m].at[layer], outs[m].at[layer, z], store_sem.at[u])
-
     def own_sends(u, act):
-        layer, m = units[u]
-        mine, left_over = owned(u, x, y), rest(u)
+        source = ins[u[1]].at[u[0]]
+
+        def along(device, first):
+            if depth(u):
+                act(move(u, z, owned(u, x, y), device, ZA, source.at[owned(u, x, y)], first))
+            act(move(u, z, rest(u), device, ZR, source.at[rest(u)], first + 1))
 
         @pl.when(z < ZN - 1)
         def _():
-            act(move(u, z, mine, up, ZA, ins[m].at[layer, mine], 0))
-            act(move(u, z, left_over, up, ZR, ins[m].at[layer, left_over], 1))
+            along(up, 0)
 
         @pl.when(z > 0)
         def _():
-            act(move(u, z, mine, down, ZA, ins[m].at[layer, mine], 2))
-            act(move(u, z, left_over, down, ZR, ins[m].at[layer, left_over], 3))
+            along(down, 2)
 
     def both(s, act):
         @pl.when(z >= s)
@@ -516,29 +606,32 @@
             act(z + s, 1)
 
     def onward(u, zz, d, act):
-        mine, left_over = owned(u, x, y), rest(u)
+        def along(device):
+            if depth(u):
+                act(move(u, zz, owned(u, x, y), device, ZA))
+            act(move(u, zz, rest(u), device, ZR))
+
         if d == 0:
 
             @pl.when(z < ZN - 1)
             def _():
-                act(move(u, zz, mine, up, ZA))
-                act(move(u, zz, left_over, up, ZR))
+                along(up)
 
         else:
 
             @pl.when(z > 0)
             def _():
-                act(move(u, zz, mine, down, ZA))
-                act(move(u, zz, left_over, down, ZR))
+                along(down)
 
     def line_step(u, s):
         def act(zz, d):
-            mine, left_over = owned(u, x, y), rest(u)
-            move(u, zz, mine, across, ZA).wait_recv()
-            move(u, zz, left_over, across, ZR).wait_recv()
+            if depth(u):
+                move(u, zz, owned(u, x, y), across, ZA).wait_recv()
+            move(u, zz, rest(u), across, ZR).wait_recv()
             onward(u, zz, d, lambda copy: copy.start())
-            move(u, zz, mine, across, GX).start()
-            move(u, zz, mine, beside, GY).start()
+            if depth(u):
+                move(u, zz, owned(u, x, y), across, GX).start()
+                move(u, zz, owned(u, x, y), beside, GY).start()
 
         both(s, act)
 
@@ -559,75 +652,737 @@
 
         both(s, act)
 
+    def arrive(u):
+        for s in range(1, ZN):
+            both(s, lambda zz, d: move(u, zz, slab(u, 1 - c), twin, GC).wait_recv())
+
     def finish(u):
-        store(u).wait()
         own_sends(u, lambda copy: copy.wait_send())
-        for s in (1, 2, 3):
+        for s in range(1, ZN):
 
             def act(zz, d):
-                mine = owned(u, x, y)
-                move(u, zz, slab(u, 1 - c), twin, GC).wait_recv()
                 onward(u, zz, d, lambda copy: copy.wait_send())
-                move(u, zz, mine, across, GX).wait_send()
-                move(u, zz, mine, beside, GY).wait_send()
-                move(u, zz, owned(u, 1 - x, y, 0), beside, GD1).wait_send()
-                move(u, zz, owned(u, x, 1 - y, 1), across, GD2).wait_send()
-                move(u, zz, slab(u, c), twin, GC).wait_send()
+                if depth(u):
+                    move(u, zz, owned(u, x, y), across, GX).wait_send()
+                    move(u, zz, owned(u, x, y), beside, GY).wait_send()
+                    move(u, zz, owned(u, 1 - x, y, 0), beside, GD1).wait_send()
+                    move(u, zz, owned(u, x, 1 - y, 1), across, GD2).wait_send()
+                    move(u, zz, slab(u, c), twin, GC).wait_send()
 
             both(s, act)
 
-    count = len(units)
-
-    def at(step, u, s):
-        if 0 <= u < count:
-            step(u, s)
-
-    for u in range(count):
-        load(u).start()
-    for u in range(2):
-        own_sends(u, lambda copy: copy.start())
-    for t in range(count + 5):
-        if t + 2 < count:
-            own_sends(t + 2, lambda copy: copy.start())
-        for s in (1, 2, 3):
-            at(line_step, t + 1 - s, s)
-        for s in (1, 2, 3):
-            at(plane_step, t - s, s)
-        for s in (1, 2, 3):
-            at(corner_step, t - 1 - s, s)
-        if t < count:
-            load(t).wait()
-            store(t).start()
-    for u in range(count):
-        finish(u)
-
-
-def gather_weights(shards):
-    layers, m_count = shards[0].shape[0], len(shards)
-    units = [(layer, m) for layer in range(layers) for m in range(m_count)]
-
-    def body(*refs):
-        gather_body(
-            units, refs[:m_count], refs[m_count : 2 * m_count], refs[2 * m_count : 3 * m_count], *refs[3 * m_count :]
+    matrices = [u for u in units if u[1] < m_count]
+    vectors = [u for u in units if u[1] == m_count]
+    count = len(matrices)
+
+    def steps():
+        for u in vectors + matrices[:2]:
+            own_sends(u, lambda copy: copy.start())
+        for s in range(1, ZN):
+            for u in vectors:
+                line_step(u, s)
+        yield ("vectors",)
+        for t in range(count + 4):
+            if t + 2 < count:
+                own_sends(matrices[t + 2], lambda copy: copy.start())
+            for s in range(1, ZN):
+                if 0 <= t + 1 - s < count:
+                    line_step(matrices[t + 1 - s], s)
+                    yield ("line",)
+            for s in range(1, ZN):
+                if 0 <= t - s < count:
+                    plane_step(matrices[t - s], s)
+                    yield ("plane",)
+            for s in range(1, ZN):
+                if 0 <= t - 1 - s < count:
+                    corner_step(matrices[t - 1 - s], s)
+                    yield ("here", matrices[t - 1 - s]) if s == ZN - 1 else ("corner",)
+
+    return steps, arrive, lambda: [finish(u) for u in units]
+
+
+def attend(core, q, keys, values, mask, attended, lse, first, last):
+    def slab(start, size, head):
+        cols = pl.ds(start, size)
+        for variant in range(2):
+
+            @pl.when(core == variant)
+            def _():
+                for row, high in RANGES[variant]:
+                    rows = slice(row, row + BLOCK)
+                    qs = q[rows, cols]
+                    ks, vs = keys[:high, cols], values[:high, cols]
+                    parts = []
+                    for j in range(size // HEAD_DIM):
+                        s = dot_nt(ks, of_head(qs, j)) + mask[:high, rows]
+                        top = jnp.max(s, axis=0, keepdims=True)
+                        e = jnp.exp(s - top)
+                        total = jnp.sum(e, axis=0, keepdims=True)
+                        lse[pl.ds(head + j, 1), rows] = top + jnp.log(total)
+                        out = dot_tn(vs, e.astype(jnp.bfloat16)) * (1.0 / total)
+                        parts.append(out[j * HEAD_DIM : (j + 1) * HEAD_DIM])
+                    out = jnp.concatenate(parts, axis=0) if len(parts) > 1 else parts[0]
+                    attended[rows, cols] = out.T.astype(jnp.bfloat16)
+
+    over_slabs(q.shape[1], slab, first, last)
+
+
+def over_slabs(width, slab, first, last):
+    pair = 2 * HEAD_DIM
+    full = width // pair
+
+    def step(i, carry):
+        slab(pl.multiple_of(i * pair, pair), pair, i * 2)
+        return carry
+
+    if first < min(last, full):
+        lax.fori_loop(first, min(last, full), step, 0)
+    if last > full and width % pair:
+        slab(full * pair, HEAD_DIM, full * 2)
+
+
+def forward_body(
+    tokens, grads, segs, vectors, w_qkv, w_out, w_up, w_down,
+    full_qkv, full_out, full_up, full_down, full_vectors, result, grads_here, mask_out, rows_out, *rest_refs,
+):
+    layers = w_qkv.shape[0]
+    saved = [dict(zip(SAVED, rest_refs[i * len(SAVED) : (i + 1) * len(SAVED)])) for i in range(layers)]
+    (
+        wq, wo, wu, wd, xs, tok, na, nm, q, keys, values, mask, att, middle, slope, act_buf, lse,
+        vecs, rows, b_up, b_proj, seg_nat, seg_row,
+        send_sem, recv_sem, load_sem, save_sem, kv_send, kv_recv, in_send, in_recv, in_local, free_sem,
+    ) = rest_refs[layers * len(SAVED) :]
+    place = neighbours()
+    x, y, z, c, across, beside, twin, up, down = place
+    diag = (1 - x, z, y * 2 + (1 - c))
+    here = c == x
+    greet(z, c, x, across, beside, twin, diag, up, down)
+    width = xs.shape[1]
+    half = BLOCK
+    parts = [w_qkv, w_out, w_up, w_down]
+    fulls = [full_qkv, full_out, full_up, full_down]
+    buffers = [wq, wo, wu, wd]
+    steps, arrive, finish = weight_moves(parts + [vectors], fulls + [full_vectors], send_sem, recv_sem, place)
+
+    def in_move(i, source, target, device):
+        return pltpu.make_async_remote_copy(
+            src_ref=source, dst_ref=target, send_sem=in_send.at[i], recv_sem=in_recv.at[i],
+            device_id=device, device_id_type=MESH,
         )
 
+    top, low = pl.ds(0, half), pl.ds(half, half)
+
+    def in_copies(i, source, target):
+        stay = pltpu.make_async_copy(source.at[top], target.at[top], in_local.at[i])
+        return (
+            stay,
+            in_move(2 * i + 1, source.at[low], target.at[low], twin),
+            in_move(2 * i, source.at[top], target.at[top], diag),
+            in_move(2 * i + 1, source.at[low], target.at[low], across),
+        )
+
+    tok_copies = in_copies(0, tokens, tok)
+    grad_copies = in_copies(1, grads, grads_here)
+    seg_stay = pltpu.make_async_copy(segs, seg_nat.at[x], in_local.at[2])
+    seg_twin = in_move(4, segs, seg_nat.at[x], twin)
+    seg_across = in_move(4, segs, seg_nat.at[x], across)
+    seg_diag = pltpu.make_async_remote_copy(
+        src_ref=segs, dst_ref=seg_nat.at[x], send_sem=in_send.at[5], recv_sem=in_recv.at[5],
+        device_id=diag, device_id_type=MESH,
+    )
+
+    @pl.when(here)
+    def _():
+        for copy in (seg_stay, seg_twin, tok_copies[0], tok_copies[1], grad_copies[0], grad_copies[1]):
+            copy.start()
+
+    @pl.when(jnp.logical_not(here))
+    def _():
+        for copy in (seg_across, seg_diag, tok_copies[2], tok_copies[3], grad_copies[2], grad_copies[3]):
+            copy.start()
+
+    def wait_in(copies):
+        @pl.when(here)
+        def _():
+            copies[0].wait()
+            copies[1].wait_recv()
+
+        @pl.when(jnp.logical_not(here))
+        def _():
+            copies[2].wait_recv()
+            copies[3].wait_recv()
+
+    def wait_segs():
+        @pl.when(here)
+        def _():
+            seg_stay.wait()
+            seg_across.wait_recv()
+
+        @pl.when(jnp.logical_not(here))
+        def _():
+            seg_twin.wait_recv()
+            seg_diag.wait_recv()
+
+    def finish_in():
+        @pl.when(here)
+        def _():
+            grad_copies[0].wait()
+            grad_copies[1].wait_recv()
+            for copy in (seg_twin, tok_copies[1], grad_copies[1]):
+                copy.wait_send()
+
+        @pl.when(jnp.logical_not(here))
+        def _():
+            grad_copies[2].wait_recv()
+            grad_copies[3].wait_recv()
+            for copy in (seg_across, seg_diag, tok_copies[2], tok_copies[3], grad_copies[2], grad_copies[3]):
+                copy.wait_send()
+
+    comm = steps()
+    seen = set()
+    loaded = {}
+    done_with = set()
+
+    def tick(count=1):
+        for _ in range(count):
+            label = next(comm, None)
+            if label is None:
+                return False
+            seen.add(label)
+            if label[0] == "here":
+                fetch_ready()
+        return True
+
+    def loads(u):
+        layer, m = u
+        n = parts[m].shape[1]
+        copies = [pltpu.make_async_copy(parts[m].at[layer], buffers[m].at[pl.ds(z * n, n)], load_sem.at[m, 0])]
+        for s in range(1, ZN):
+            zz = (z + s) % ZN
+            copies.append(
+                pltpu.make_async_copy(fulls[m].at[layer, zz], buffers[m].at[pl.ds(zz * n, n)], load_sem.at[m, s])
+            )
+        return copies
+
+    def fetch_ready(upto=None):
+        for layer in range(layers):
+            for m in range(len(parts)):
+                u = (layer, m)
+                if u in loaded or ("here", u) not in seen:
+                    continue
+                if layer and (layer - 1, m) not in done_with:
+                    continue
+                following = (layer, m + 1) if m + 1 < len(parts) else (layer + 1, 0)
+                if u != upto and following[0] < layers and ("here", following) not in seen:
+                    continue
+                arrive(u)
+                for copy in loads(u):
+                    copy.start()
+                loaded[u] = True
+
+    def need(u):
+        while ("here", u) not in seen:
+            if not tick():
+                break
+        fetch_ready(u)
+        for copy in loads(u):
+            copy.wait()
+
+    pending = []
+
+    def save(layer, name, buffer):
+        copy = pltpu.make_async_copy(buffer, saved[layer][name], save_sem.at[layer, SAVED.index(name)])
+        copy.start()
+        pending.append(copy)
+
+    def settle():
+        while pending:
+            pending.pop().wait()
+
+    def row(layer, name):
+        return rows[layer, pl.ds(ROW[name], 1), :]
+
+    def make_mask():
+        wait_segs()
+        joined = jnp.concatenate([seg_nat[0], seg_nat[1]], axis=1).astype(jnp.float32)
+        seg_row[...] = jnp.broadcast_to(joined, seg_row.shape)
+        column = seg_row[...].T[:, :1]
+        for block in range(2):
+            base = ((2 * c) if block == 0 else (3 - 2 * c)) * BLOCK
+            own = seg_row[0:1, pl.ds(pl.multiple_of(base, BLOCK), BLOCK)]
+            spot = lax.broadcasted_iota(jnp.int32, (mask.shape[0], BLOCK), 0)
+            mine = lax.broadcasted_iota(jnp.int32, (mask.shape[0], BLOCK), 1) + base
+            ok = (column == own) & (spot <= mine)
+            mask[:, block * BLOCK : (block + 1) * BLOCK] = jnp.where(ok, 0.0, MASKED).astype(jnp.float32)
+        copy = pltpu.make_async_copy(mask, mask_out, save_sem.at[0, len(SAVED)])
+        copy.start()
+        pending.append(copy)
+
+    def make_rows(layer):
+        copies = [
+            pltpu.make_async_copy(vectors.at[layer, 0], vecs.at[z], load_sem.at[4, 0])
+        ] + [
+            pltpu.make_async_copy(full_vectors.at[layer, (z + s) % ZN, 0], vecs.at[(z + s) % ZN], load_sem.at[4, s])
+            for s in range(1, ZN)
+        ]
+        for copy in copies:
+            copy.start()
+        for copy in copies:
+            copy.wait()
+        share = vecs.shape[2]
+        b_proj[layer, 0:1, :] = jnp.zeros((1, b_proj.shape[2]), jnp.float32)
+        for zz in range(ZN):
+            block = vecs[zz].astype(jnp.float32)
+            rows[layer, 0:8, zz * share : (zz + 1) * share] = block[0:8]
+            for name, at in (("b_query", 0), ("b_value", 2 * width)):
+                b_proj[layer, 0:1, at + zz * share : at + (zz + 1) * share] = block[ROW[name] : ROW[name] + 1]
+            for j in range(ZN):
+                at = (zz * ZN + j) * share
+                b_up[layer, 0:1, at : at + share] = block[8 + j : 9 + j]
+
+    def swap_moves(layer):
+        moves = []
+        for i, ref in enumerate((keys, values)):
+            for block in range(2):
+                at = ((2 * c) if block == 0 else (3 - 2 * c)) * BLOCK
+                spot = ref.at[pl.ds(pl.multiple_of(at, BLOCK), BLOCK)]
+                moves.append(
+                    pltpu.make_async_remote_copy(
+                        src_ref=spot, dst_ref=spot, send_sem=kv_send.at[layer, i, block],
+                        recv_sem=kv_recv.at[layer, i, block], device_id=twin, device_id_type=MESH,
+                    )
+                )
+        return moves
+
+    def swap_waits(layer):
+        moves = []
+        for i, ref in enumerate((keys, values)):
+            for block in range(2):
+                at = ((2 - 2 * c) if block == 0 else (1 + 2 * c)) * BLOCK
+                spot = ref.at[pl.ds(pl.multiple_of(at, BLOCK), BLOCK)]
+                moves.append(
+                    pltpu.make_async_remote_copy(
+                        src_ref=spot, dst_ref=spot, send_sem=kv_send.at[layer, i, block],
+                        recv_sem=kv_recv.at[layer, i, block], device_id=twin, device_id_type=MESH,
+                    )
+                )
+        return moves
+
+    def matrix(buffer, cols):
+        return buffer[:, :, cols].reshape(-1, cols.size)
+
+    def compute(layer):
+        if layer == 0:
+            make_rows(0)
+            make_rows(1)
+            for i in range(layers):
+                copy = pltpu.make_async_copy(rows.at[i], rows_out.at[i], save_sem.at[i, len(SAVED) + 1])
+                copy.start()
+                pending.append(copy)
+            wait_in(tok_copies)
+            xs[...] = tok[...].astype(jnp.float32)
+            make_mask()
+        else:
+            settle()
+        save(layer, "x", xs)
+        norm_into(xs, row(layer, "attn_gain"), row(layer, "attn_shift"), na)
+        save(layer, "normed_attn", na)
+        yield
+        need((layer, 0))
+        total = wq.shape[2]
+
+        for low_at in range(0, total, 4 * BLOCK):
+            high_at = min(low_at + 4 * BLOCK, total)
+            tiles_between(low_at, high_at, BLOCK, lambda start, size: project_tile(layer, start, size))
+            yield
+        done_with.add((layer, 0))
+        q[...] = slope[:, :width]
+        if layer:
+            pl.semaphore_wait(free_sem, 1)
+        for block in range(2):
+            at = ((2 * c) if block == 0 else (3 - 2 * c)) * BLOCK
+            spot = pl.ds(pl.multiple_of(at, BLOCK), BLOCK)
+            source = slice(block * BLOCK, (block + 1) * BLOCK)
+            keys[spot, :] = slope[source, width : 2 * width]
+            values[spot, :] = slope[source, 2 * width : 3 * width]
+        for copy in swap_moves(layer):
+            copy.start()
+        save(layer, "q", q)
+        yield
+        for copy in swap_waits(layer):
+            copy.wait_recv()
+        save(layer, "keys", keys)
+        save(layer, "values", values)
+        for first in range(0, width // (2 * HEAD_DIM) + 1, 4):
+            attend(c, q, keys, values, mask, att, lse, first, min(first + 4, width // (2 * HEAD_DIM) + 1))
+            yield
+        save(layer, "attended", att)
+        save(layer, "lse", lse)
+        if layer + 1 < layers:
+            settle()
+            for copy in swap_moves(layer):
+                copy.wait_send()
+            pl.semaphore_signal(free_sem, inc=1, device_id=twin, device_id_type=MESH)
+        need((layer, 1))
+
+        def out_step(start, size):
+            cols = pl.ds(start, size)
+            middle[:, cols] = xs[:, cols] + product(att[...], matrix(wo, cols)) + rows[layer, pl.ds(ROW["b_out"], 1), cols]
+
+        tiles_between(0, width, BLOCK, out_step)
+        done_with.add((layer, 1))
+        save(layer, "middle", middle)
+        yield
+        norm_into(middle, row(layer, "mlp_gain"), row(layer, "mlp_shift"), nm)
+        save(layer, "normed_mlp", nm)
+        yield
+        need((layer, 2))
+        settle()
+
+        def up_step(start, size):
+            cols = pl.ds(start, size)
+            u = product(nm[...], matrix(wu, cols)) + b_up[layer, 0:1, cols]
+            square = u * u
+            t = jnp.tanh(u * (GELU_A + (GELU_A * GELU_B) * square))
+            half_up = 0.5 + 0.5 * t
+            act_buf[:, cols] = (u * half_up).astype(jnp.bfloat16)
+            slope[:, cols] = (
+                half_up + (0.5 * u) * (1.0 - t * t) * (GELU_A + (3.0 * GELU_A * GELU_B) * square)
+            ).astype(jnp.bfloat16)
+
+        ff = wu.shape[2]
+        for low_at in range(0, ff, 6 * BLOCK):
+            tiles_between(low_at, min(low_at + 6 * BLOCK, ff), BLOCK, up_step)
+            yield
+        done_with.add((layer, 2))
+        save(layer, "slope", slope)
+        save(layer, "activated", act_buf)
+        need((layer, 3))
+
+        def down_step(start, size):
+            cols = pl.ds(start, size)
+            xs[:, cols] = middle[:, cols] + product(act_buf[...], matrix(wd, cols)) + rows[layer, pl.ds(ROW["b_down"], 1), cols]
+
+        for low_at in range(0, width, 2 * BLOCK):
+            tiles_between(low_at, min(low_at + 2 * BLOCK, width), BLOCK, down_step)
+            yield
+        done_with.add((layer, 3))
+
+    def project_tile(layer, start, size):
+        cols = pl.ds(start, size)
+        out = product(na[...], matrix(wq, cols))
+        slope[:, cols] = ((out + b_proj[layer, 0:1, cols]) * scale_of(start, size)).astype(jnp.bfloat16)
+
+    def scale_of(start, size):
+        lane = lax.broadcasted_iota(jnp.int32, (1, size), 1) + start
+        return jnp.where(lane < width, QUERY_SCALE, 1.0).astype(jnp.float32)
+
+    tick()
+    for layer in range(layers):
+        for _ in compute(layer):
+            tick(PACE)
+    while tick():
+        pass
+    settle()
+    tok[...] = xs[...].astype(jnp.bfloat16)
+    out = pltpu.make_async_copy(tok, result, save_sem.at[0, 0])
+    out.start()
+    for copy in swap_moves(layers - 1):
+        copy.wait_send()
+    finish_in()
+    finish()
+    out.wait()
+
+
+def forward(tokens, grads, segs, vectors, weights):
+    rows, width = tokens.shape
+    low = jnp.bfloat16
+    layers = vectors.shape[0]
+    ff = weights[2].shape[3]
+    units = layers * (len(weights) + 1)
+    shapes = dict(
+        x=((rows, width), jnp.float32),
+        normed_attn=((rows, width), low),
+        q=((rows, width), low),
+        keys=((2 * rows, width), low),
+        values=((2 * rows, width), low),
+        attended=((rows, width), low),
+        lse=((HEAD_ROWS, rows), jnp.float32),
+        middle=((rows, width), jnp.float32),
+        normed_mlp=((rows, width), low),
+        slope=((rows, ff), low),
+        activated=((rows, ff), low),
+    )
+    out_shape = (
+        [shaped((layers, ZN) + w.shape[1:], low) for w in weights]
+        + [
+            shaped((layers, ZN) + vectors.shape[1:], low),
+            shaped((rows, width), low),
+            shaped((rows, width), low),
+            shaped((2 * rows, rows)),
+            shaped((layers, 16, width)),
+        ]
+        + [shaped(*shapes[name]) for _ in range(layers) for name in SAVED]
+    )
+    dma = pltpu.SemaphoreType.DMA
+    scratch = [pltpu.VMEM((ZN * w.shape[1],) + w.shape[2:], low) for w in weights] + [
+        pltpu.VMEM((rows, width), jnp.float32),
+        pltpu.VMEM((rows, width), low),
+        pltpu.VMEM((rows, width), low),
+        pltpu.VMEM((rows, width), low),
+        pltpu.VMEM((rows, width), low),
+        pltpu.VMEM((2 * rows, width), low),
+        pltpu.VMEM((2 * rows, width), low),
+        pltpu.VMEM((2 * rows, rows), jnp.float32),
+        pltpu.VMEM((rows, width), low),
+        pltpu.VMEM((rows, width), jnp.float32),
+        pltpu.VMEM((rows, ff), low),
+        pltpu.VMEM((rows, ff), low),
+        pltpu.VMEM((HEAD_ROWS, rows), jnp.float32),
+        pltpu.VMEM((ZN,) + vectors.shape[2:], low),
+        pltpu.VMEM((layers, 16, width), jnp.float32),
+        pltpu.VMEM((layers, 8, ff), jnp.float32),
+        pltpu.VMEM((layers, 8, 3 * width), jnp.float32),
+        pltpu.VMEM((2, 1, rows), jnp.int32),
+        pltpu.VMEM((8, 2 * rows), jnp.float32),
+        dma((units, ZN, 7)),
+        dma((units, ZN, 7)),
+        dma((len(weights) + 1, ZN)),
+        dma((layers, len(SAVED) + 2)),
+        dma((layers, 2, 2)),
+        dma((layers, 2, 2)),
+        dma((6,)),
+        dma((6,)),
+        dma((3,)),
+        pltpu.SemaphoreType.REGULAR,
+    ]
+    outs = pl.pallas_call(
+        forward_body,
+        out_shape=out_shape,
+        in_specs=anywhere(4 + len(weights)),
+        out_specs=anywhere(len(out_shape)),
+        scratch_shapes=scratch,
+        compiler_params=pltpu.CompilerParams(collective_id=0, has_side_effects=True, vmem_limit_bytes=VMEM_LIMIT),
+        name="forward",
+    )(tokens, grads, segs, vectors, *weights)
+    count = len(weights)
+    fulls, rest = outs[:count], outs[count + 5 :]
+    _, result, grads_here, mask, vector_rows = outs[count : count + 5]
+    saved = [dict(zip(SAVED, rest[i * len(SAVED) : (i + 1) * len(SAVED)])) for i in range(layers)]
+    return fulls, result, grads_here, mask, vector_rows, saved
+
+
+def bring(layer, own, full, buffer, sems, i):
+    z = lax.axis_index("fsdp")
+    n = own.shape[1]
+    return [pltpu.make_async_copy(own.at[layer], buffer.at[pl.ds(z * n, n)], sems.at[i, 0])] + [
+        pltpu.make_async_copy(
+            full.at[layer, (z + s) % ZN], buffer.at[pl.ds((z + s) % ZN * n, n)], sems.at[i, s]
+        )
+        for s in range(1, ZN)
+    ]
+
+
+def begin(copies):
+    for copy in copies:
+        copy.start()
+
+
+def end(copies):
+    for copy in copies:
+        copy.wait()
+
+
+def some_rows(buffer, start, size):
+    return buffer[pl.ds(start // 16, size // 16)].reshape(size, buffer.shape[2])
+
+
+def mlp_back_body(
+    layer, dx, middle, gain, slope, down_own, down_full, up_own, up_full, out_own, out_full,
+    g_mlp, g_pre, g_middle, g_branch, g_attended, gb_down, gb_up, g_gain, g_shift, gb_out,
+    w_down, w_up, w_out, g_norm, sems,
+):
+    copies = [
+        bring(layer, down_own, down_full, w_down, sems, 0),
+        bring(layer, up_own, up_full, w_up, sems, 1),
+        bring(layer, out_own, out_full, w_out, sems, 2),
+    ]
+    for copy in copies:
+        begin(copy)
+    g_mlp[...] = dx[...].astype(jnp.bfloat16)
+    gb_down[...] = jnp.sum(g_mlp[...].astype(jnp.float32), axis=0, keepdims=True)
+    end(copies[0])
+
+    def down_step(start, size):
+        cols = pl.ds(start, size)
+        g = (dot_nt(g_mlp[...], some_rows(w_down, start, size)) * slope[:, cols].astype(jnp.float32)).astype(jnp.bfloat16)
+        g_pre[:, cols] = g
+        gb_up[:, cols] = jnp.sum(g.astype(jnp.float32), axis=0, keepdims=True)
+
+    tiles(g_pre.shape[1], BLOCK, down_step)
+    end(copies[1])
+
+    def up_step(start, size):
+        cols = pl.ds(start, size)
+        g_norm[:, cols] = dot_nt(g_pre[...], some_rows(w_up, start, size))
+
+    tiles(dx.shape[1], BLOCK, up_step)
+    norm_back(middle, g_norm, dx, gain[...], g_middle, g_gain, g_shift, g_branch)
+    gb_out[...] = jnp.sum(g_branch[...].astype(jnp.float32), axis=0, keepdims=True)
+    end(copies[2])
+
+    def out_step(start, size):
+        cols = pl.ds(start, size)
+        g_attended[:, cols] = dot_nt(g_branch[...], some_rows(w_out, start, size)).astype(jnp.bfloat16)
+
+    tiles(dx.shape[1], BLOCK, out_step)
+
+
+def mlp_back(layer, dx, middle, slope, gain, owns, fulls):
+    rows, width = dx.shape
+    ff = slope.shape[1]
+    low = jnp.bfloat16
     return pl.pallas_call(
-        body,
-        out_shape=[jax.ShapeDtypeStruct((layers, ZN) + w.shape[1:], w.dtype) for w in shards],
-        in_specs=[pl.BlockSpec(memory_space=pl.ANY)] * m_count,
-        out_specs=[pl.BlockSpec(memory_space=pl.ANY)] * m_count,
-        scratch_shapes=[pltpu.VMEM(w.shape, w.dtype) for w in shards]
-        + [
-            pltpu.SemaphoreType.DMA((len(units),)),
-            pltpu.SemaphoreType.DMA((len(units),)),
-            pltpu.SemaphoreType.DMA((len(units), ZN, 7)),
-            pltpu.SemaphoreType.DMA((len(units), ZN, 7)),
+        functools.partial(mlp_back_body, layer),
+        out_shape=[
+            shaped((rows, width), low),
+            shaped((rows, ff), low),
+            shaped((rows, width)),
+            shaped((rows, width), low),
+            shaped((rows, width), low),
+            shaped((1, width)),
+            shaped((1, ff)),
+            shaped((1, width)),
+            shaped((1, width)),
+            shaped((1, width)),
         ],
-        compiler_params=pltpu.CompilerParams(
-            collective_id=0, has_side_effects=True, vmem_limit_bytes=40 << 20
-        ),
-        name="gather_weights",
-    )(*shards)
+        in_specs=whole(4) + anywhere(6),
+        out_specs=whole(10),
+        scratch_shapes=[
+            pltpu.VMEM((ff // 16, 16, width), low),
+            pltpu.VMEM((width // 16, 16, ff), low),
+            pltpu.VMEM((width // 16, 16, width), low),
+            pltpu.VMEM((rows, width), jnp.float32),
+            pltpu.SemaphoreType.DMA((3, ZN)),
+        ],
+        compiler_params=params(),
+        name="mlp_back",
+    )(dx, middle, gain, slope, owns[3], fulls[3], owns[2], fulls[2], owns[1], fulls[1])
+
+
+def attend_back_body(
+    q, g_attended, attended, lse, mask, keys, values, g_q, g_own, g_other, inner, g_k, g_v
+):
+    core = lax.rem(lax.axis_index("rep"), 2)
+    width = q.shape[1]
+    head = lax.broadcasted_iota(jnp.int32, (HEAD_ROWS, width), 0)
+    lane = lax.broadcasted_iota(jnp.int32, (HEAD_ROWS, width), 1)
+    pick = (lane // HEAD_DIM == head).astype(jnp.float32).astype(jnp.bfloat16)
+    both = g_attended[...].astype(jnp.float32) * attended[...].astype(jnp.float32)
+    high = both.astype(jnp.bfloat16)
+    rest = (both - high.astype(jnp.float32)).astype(jnp.bfloat16)
+    inner[...] = dot_nt(pick, high) + dot_nt(pick, rest)
+    def act(start, size, head):
+        cols = pl.ds(start, size)
+        g_k[...] = jnp.zeros_like(g_k)
+        g_v[...] = jnp.zeros_like(g_v)
+        lanes = slice(0, size)
+        for variant in range(2):
+
+            @pl.when(core == variant)
+            def _():
+                for row, high in RANGES[variant]:
+                    rows = slice(row, row + BLOCK)
+                    qs, gs = q[rows, cols], g_attended[rows, cols]
+                    ks, vs = keys[:high, cols], values[:high, cols]
+                    parts = []
+                    for j in range(size // HEAD_DIM):
+                        q_j, g_j = of_head(qs, j), of_head(gs, j)
+                        s = dot_nt(ks, q_j) + mask[:high, rows]
+                        p = jnp.exp(s - lse[pl.ds(head + j, 1), rows])
+                        g_p = dot_nt(vs, g_j)
+                        g_s = (p * (g_p - inner[pl.ds(head + j, 1), rows])).astype(jnp.bfloat16)
+                        g_v[:high, lanes] += product(p.astype(jnp.bfloat16), g_j)
+                        g_k[:high, lanes] += product(g_s, q_j)
+                        parts.append(dot_tn(ks, g_s)[j * HEAD_DIM : (j + 1) * HEAD_DIM])
+                    out = jnp.concatenate(parts, axis=0) if len(parts) > 1 else parts[0]
+                    g_q[rows, cols] = out.T.astype(jnp.bfloat16) * QUERY_SCALE
+
+        for block in range(2):
+            rows = slice(block * BLOCK, (block + 1) * BLOCK)
+            for target, who in ((g_own, core), (g_other, 1 - core)):
+                at = ((2 * who) if block == 0 else (3 - 2 * who)) * BLOCK
+                spot = pl.ds(pl.multiple_of(at, BLOCK), BLOCK)
+                target[0, rows, cols] = g_k[spot, lanes].astype(jnp.bfloat16)
+                target[1, rows, cols] = g_v[spot, lanes].astype(jnp.bfloat16)
+
+    over_slabs(width, act, 0, width // (2 * HEAD_DIM) + 1)
+
+
+def attend_back(q, g_attended, attended, lse, mask, keys, values):
+    rows, width = q.shape
+    low = jnp.bfloat16
+    return pl.pallas_call(
+        attend_back_body,
+        out_shape=[shaped((rows, width), low), shaped((2, rows, width), low), shaped((2, rows, width), low)],
+        in_specs=whole(7),
+        out_specs=whole(3),
+        scratch_shapes=[
+            pltpu.VMEM((HEAD_ROWS, rows), jnp.float32),
+            pltpu.VMEM((2 * rows, 2 * HEAD_DIM), jnp.float32),
+            pltpu.VMEM((2 * rows, 2 * HEAD_DIM), jnp.float32),
+        ],
+        compiler_params=params(),
+        name="attend_back",
+    )(q, g_attended, attended, lse, mask, keys, values)
+
+
+def project_back_body(
+    layer, x, g_middle, gain, g_q, g_own, g_got, w_own, w_full, g_x, g_proj, gb_q, gb_v, g_gain, g_shift, w, g_norm, sem
+):
+    width = x.shape[1]
+    load = bring(layer, w_own, w_full, w, sem, 0)
+    begin(load)
+    g_k = g_own[0] + g_got[0]
+    g_v = g_own[1] + g_got[1]
+    gb_q[...] = jnp.sum(g_q[...].astype(jnp.float32), axis=0, keepdims=True)
+    gb_v[...] = jnp.sum(g_v.astype(jnp.float32), axis=0, keepdims=True)
+    g_proj[:, :width] = g_q[...]
+    g_proj[:, width : 2 * width] = g_k
+    g_proj[:, 2 * width :] = g_v
+    end(load)
+
+    def step(start, size):
+        cols = pl.ds(start, size)
+        g_norm[:, cols] = dot_nt(g_proj[...], some_rows(w, start, size))
+
+    tiles(width, BLOCK, step)
+    norm_back(x, g_norm, g_middle, gain[...], g_x, g_gain, g_shift)
+
+
+def project_back(layer, x, g_middle, g_q, g_own, g_got, gain, own, full):
+    rows, width = x.shape
+    low = jnp.bfloat16
+    return pl.pallas_call(
+        functools.partial(project_back_body, layer),
+        out_shape=[
+            shaped((rows, width)),
+            shaped((rows, 3 * width), low),
+            shaped((1, width)),
+            shaped((1, width)),
+            shaped((1, width)),
+            shaped((1, width)),
+        ],
+        in_specs=whole(6) + anywhere(2),
+        out_specs=whole(6),
+        scratch_shapes=[
+            pltpu.VMEM((width // 16, 16, 3 * width), low),
+            pltpu.VMEM((rows, width), jnp.float32),
+            pltpu.SemaphoreType.DMA((1, ZN)),
+        ],
+        compiler_params=params(),
+        name="project_back",
+    )(x, g_middle, gain, g_q, g_own, g_got, own, full)
 
 
 PAIRS = ((0, 1), (3, 2))
@@ -636,7 +1391,7 @@
 
 def reduce_body(ks, grads, outs, own, twin_in, first_in, second_in, low_in, high_in, load_sem, store_sem, send_sem, recv_sem):
     x, y, z, c, across, beside, twin, up, down = neighbours()
-    greet(z, across, beside, twin, up, down)
+    greet(z, c, x, across, beside, twin, None, up, down)
     units = [(m, h) for h in range(2) for m in range(len(grads))]
     p = x * 2 + y
 
@@ -896,26 +1651,6 @@
 VECTORS = (0, 1, 3, 4, 6, 7, 8, 12, 10)
 MATRICES = (2, 5, 9, 11)
 WIDE = 13312
-
-
-def gather_all(params):
-    layers = params[0].shape[0]
-    shards = [params[i].reshape(layers, -1, 16, params[i].shape[2]) for i in MATRICES]
-    full = gather_weights(shards)
-    vectors = jnp.concatenate([params[i].reshape(layers, -1, params[0].shape[1]) for i in VECTORS], axis=1)
-    vectors = lax.all_gather(vectors, "fsdp", axis=2)
-    gathered = []
-    for layer in range(layers):
-        entry = [None] * 13
-        for at, i in enumerate(MATRICES):
-            entry[i] = full[at][layer].reshape(-1, params[i].shape[2])
-        row = 0
-        for i in VECTORS:
-            rows = params[i].shape[1] // params[0].shape[1]
-            entry[i] = jnp.moveaxis(vectors[layer, row : row + rows], 0, 1).reshape(-1)
-            row += rows
-        gathered.append(tuple(entry))
-    return gathered
 
 
 def reduce_layer(gradients):
@@ -947,37 +1682,53 @@
     return tuple(r.astype(jnp.float32) for r in result)
 
 
+def swap_cores(rows):
+    return lax.ppermute(rows, "rep", [(0, 1), (1, 0), (2, 3), (3, 2)])
+
+
 def on_cores(tokens, segments, grad_out, *params):
-    rows = tokens.shape[1]
-    own_x, grad_x = to_cores(tokens[0]), to_cores(grad_out[0])
-    seg_own = to_cores(segments[0])
-    core = lax.rem(lax.axis_index("rep"), 2)
-    pool = Cores()
-    places = jnp.concatenate(
-        [
-            core * rows + lax.iota(jnp.int32, rows // 2),
-            (3 - 2 * core) * (rows // 2) + lax.iota(jnp.int32, rows // 2),
-        ]
-    )
-    seg_all, places_all = pool.spread(seg_own), pool.spread(places)
-    visible = (seg_own[:, None] == seg_all[None, :]) & (places[:, None] >= places_all[None, :])
-    gathered = gather_all(params)
-    layer_count = params[0].shape[0]
-    resid = own_x.astype(jnp.float32)
-    stored_list = []
-    for layer_index in range(layer_count):
-        resid, stored = forward_layer(resid, gathered[layer_index], visible, pool)
-        stored_list.append(stored)
-    result = from_cores(resid.astype(jnp.bfloat16))[None]
-    grad_resid = grad_x.astype(jnp.float32)
-    reduced = [None] * layer_count
-    for layer_index in reversed(range(layer_count)):
-        grad_resid, gradients = backward_layer(
-            grad_resid, stored_list[layer_index], gathered[layer_index], visible, pool
+    rows, width = tokens.shape[1:]
+    layers = params[0].shape[0]
+    weights = [params[i].reshape(layers, -1, 16, params[i].shape[2]) for i in MATRICES]
+    vectors = jnp.concatenate([params[i].reshape(layers, -1, params[0].shape[1]) for i in VECTORS], axis=1)
+    vectors = jnp.pad(vectors, ((0, 0), (0, 16 - vectors.shape[1]), (0, 0)))[:, None]
+    fulls, result, grads_here, mask, vector_rows, saved = forward(
+        tokens[0], grad_out[0], segments, vectors, weights
+    )
+    result = from_cores(result)[None]
+    grad = grads_here.astype(jnp.float32)
+    reduced = [None] * layers
+    for layer in reversed(range(layers)):
+        kept = saved[layer]
+        attn_gain, mlp_gain = vector_rows[layer, 0:1], vector_rows[layer, 5:6]
+        g_mlp, g_pre, g_middle, g_branch, g_attended, gb_down, gb_up, gm_gain, gm_shift, gb_out = mlp_back(
+            layer, grad, kept["middle"], kept["slope"], mlp_gain, weights, fulls
         )
-        reduced[layer_index] = reduce_layer(gradients)
+        g_q, g_own, g_other = attend_back(
+            kept["q"], g_attended, kept["attended"], kept["lse"], mask, kept["keys"], kept["values"]
+        )
+        g_got = swap_cores(g_other)
+        grad, g_proj, gb_q, gb_v, ga_gain, ga_shift = project_back(
+            layer, kept["x"], g_middle, g_q, g_own, g_got, attn_gain, weights[0], fulls[0]
+        )
+        gradients = (
+            ga_gain[0],
+            ga_shift[0],
+            inner_rows(kept["normed_attn"], g_proj),
+            gb_q[0],
+            gb_v[0],
+            inner_rows(kept["attended"], g_branch),
+            gb_out[0],
+            gm_gain[0],
+            gm_shift[0],
+            inner_rows(kept["normed_mlp"], g_pre),
+            gb_up[0],
+            inner_rows(kept["activated"], g_mlp),
+            gb_down[0],
+        )
+        reduced[layer] = reduce_layer(gradients)
     stacked = tuple((jnp.stack([entry[member] for entry in reduced]) for member in range(13)))
-    return (result, from_cores(grad_resid.astype(jnp.bfloat16))[None]) + stacked
+    return (result, from_cores(grad.astype(jnp.bfloat16))[None]) + stacked
 
 
 def on_device(

time: 1390 us -> 1060 us (0.76)
  matrix products: 396 us -> 53.8 us
  Pallas kernels: 605 us -> 820 us
  other arithmetic: 152 us -> 37.4 us
  local copies, waits for them, and re-layouts: 179 us -> 111 us
    dot_general x28 -> x0, matrix products: 332 us -> none  [the longest x8 70.3 us: outer_cols(): lax.dot_general(left, right, (((1,), (1,)), ((), ())), preferred_element_...]
    pallas_call x1 -> x7, Pallas kernels: 209 us -> 430 us  [the longest x1 279 us: forward(): pl.pallas_call(forward_body, out_shape=out_shape, in_specs=anywhere(4 + l...]
    convert_element_type x7 -> x12, other arithmetic: 66.6 us -> 7.05 us  [the longest x10 5.36 us: reduce_layer(): low = [g.astype(jnp.bfloat16) for g in gradients]]
    slice x15 -> x2, local copies, waits for them, and re-layouts: 61.1 us -> 2.07 us  [from_cores(): rows[half:]]
    reduce_sum x19 -> x0, other arithmetic: 49.4 us -> none  [the longest x2 31.2 us: forward_layer(): row_sum = jnp.sum(exponent, axis=-1, keepdims=True)]
    unnamed x317 -> x90, local copies, waits for them, and re-layouts: 46.2 us -> 17.2 us
    convert_element_type x10 -> x20, local copies, waits for them, and re-layouts: 30 us -> 30 us  [reduce_layer(): low = [g.astype(jnp.bfloat16) for g in gradients]]
  transfers between devices with their start and end apart: 20 -> 6, of which waited for: 1 -> 0; matrix products, arithmetic and copies ran while one was open for 22% -> 12% of each run, Pallas kernels for 15% -> 6%
where the time goes in v2:
time: 1060 us; the launch traced here: 1040 us
  Pallas kernels  820 us (77%)
  local copies, waits for them, and re-layouts  111 us (10%)
  matrix products  53.8 us (5%)
  other arithmetic  37.4 us (4%)
  starting transfers between devices  12.1 us (1%)
    pallas_call x2, Pallas kernels, reduce_pieces(): pl.pallas_call(body, out_shape=[jax.ShapeDtypeStruct((8 * k,) + g.shape[2...  391 us
    pallas_call x1, Pallas kernels, forward(): pl.pallas_call(forward_body, out_shape=out_shape, in_specs=anywhere(4 + l...  279 us
    pallas_call x2, Pallas kernels, mlp_back(): pl.pallas_call(functools.partial(mlp_back_body, layer), out_shape=[shaped...  65.3 us
    dot_general x8, matrix products, inner_rows(): lax.dot_general(left, right, (((0,), (0,)), ((), ())), preferred_element_...  53.8 us
    pallas_call x2, Pallas kernels, attend_back(): pl.pallas_call(attend_back_body, out_shape=[shaped((rows, width), low), s...  49.5 us
    pallas_call x2, Pallas kernels, project_back(): pl.pallas_call(functools.partial(project_back_body, layer), out_shape=[sh...  35.9 us
    convert_element_type x20, local copies, waits for them, and re-layouts, reduce_layer(): low = [g.astype(jnp.bfloat16) for g in gradients]  30 us
    another operation x13, other arithmetic, on_cores(): jnp.stack([entry[member] for entry in reduced])  25.7 us
  transfers between devices with their start and end apart: 6, of which 0 were waited for; matrix products, arithmetic and copies ran while one was open for 12% of the time, Pallas kernels for 6%

profile of v2, /device:TPU:25, one launch (start us, length us, event | category | flops | bytes accessed | tf_op | source)
XLA Modules:
  0.0 1036.5 jit_solution(6373070196302753945)
XLA Ops:
  11.5 279.1 %forward.1 = (bf16[2,4,17,16,3264]{4,3,2,1,0:T(8,128)(2,1)}, bf16[2,4,17,16,1088]{4,3,2,1,0:T(8,128)(2,1)}, bf16[2,4,17,16,4352]{4,3,2,1,0:T(8,128)(2,1)}, bf16[...) custom-call(bf16[512,1088]{1,0:T(8,128)(2,1)} %bitcast.162, ...), custom_call_target="tpu_custom_call" | custom-call | tf_op jit(solution)/shard_map/forward/pallas_call | solution.py:1159
  299.8 32.6 %mlp_back.2 = (bf16[512,1088]{1,0:T(8,128)(2,1)}, bf16[512,4352]{1,0:T(8,128)(2,1)}, f32[512,1088]{1,0:T(8,128)}, bf16[512,1088]{1,0:T(8,128)(2,1)}, bf16[512,10...) custom-call(f32[512,1088]{1,0:T(8,128)} %convert_element_type.243.dx, ...), custom_call_target="tpu_custom_call" | custom-call | tf_op jit(solution)/shard_map/mlp_back/pallas_call | solution.py:1245
  332.4 24.7 %attend_back.2 = (bf16[512,1088]{1,0:T(8,128)(2,1)}, bf16[2,512,1088]{2,1,0:T(8,128)(2,1)}, bf16[2,512,1088]{2,1,0:T(8,128)(2,1)}) custom-call(bf16[512,1088]{1,0:T(8,128)(2,1)} %get-tuple-element.104.q, bf16[512,1088]{1,0:T(8,128)(2,1)} %get-tuple-element.105.g_attended, bf16[512,1088]{1,0:T(8,128)(2,1)} %get-tuple-element.106.attended, ...), custom_call_target="tpu_custom_call" | custom-call | tf_op jit(solution)/shard_map/attend_back/pallas_call | solution.py:1325
  357.1 4.6 copy.81
  361.8 5.3 collective-permute-start.2
  367.6 9.7 convolution_convert_fusion
  377.3 14.0 %copy.93 = bf16[4352,1088]{1,0:T(8,128)(2,1)} copy(bf16[4352,1088]{0,1:T(8,128)(2,1)} %convolution_convert_fusion) | data formatting | bytes 18939904 | tf_op jit(solution)/shard_map/convert_element_type | solution.py:1657
  392.4 8.3 convolution_convert_fusion.1
  411.0 4.2 copy.82.g_got
  415.2 18.1 %project_back.2 = (f32[512,1088]{1,0:T(8,128)}, bf16[512,3264]{1,0:T(8,128)(2,1)}, f32[1,1088]{1,0:T(1,128)}, f32[1,1088]{1,0:T(1,128)}, f32[1,1088]{1,0:T(1,128)}, /*index=5*/f32[1,1088]{1,0:T(1,128)}) custom-call(f32[512,1088]{1,0:T(8,128)} %get-tuple-element.95.x, f32[512,1088]{1,0:T(8,128)} %get-tuple-element.103.g_middle, ...), custom_call_target="tpu_custom_call" | custom-call | tf_op jit(solution)/shard_map/project_back/pallas_call | solution.py:1366
  435.3 6.0 convolution_convert_fusion.4
  446.3 194.5 %reduce_grads.3 = (bf16[16,16,3264]{2,1,0:T(8,128)(2,1)}, bf16[16,16,1088]{2,1,0:T(8,128)(2,1)}, bf16[16,16,4352]{2,1,0:T(8,128)(2,1)}, bf16[64,16,1088]{2,1,0:T(8,128)(2,1)}, bf16[8,16,1664]{2,1,0:T(8,128)(2,1)}) custom-call(bf16[4,17,16,3264]{3,2,1,0:T(8,128)(2,1)} %bitcast.155, bf16[4,17,16,1088]{3,2,1,0:T(8,128)(2,1)} %bitcast.167, ...), custom_call_target="tpu_custom_call" | custom-call | tf_op jit(solution)/shard_map/reduce_grads/pallas_call | solution.py:1627
  644.5 32.7 %mlp_back.3 = (bf16[512,1088]{1,0:T(8,128)(2,1)}, bf16[512,4352]{1,0:T(8,128)(2,1)}, f32[512,1088]{1,0:T(8,128)}, bf16[512,1088]{1,0:T(8,128)(2,1)}, bf16[512,10...) custom-call(f32[512,1088]{1,0:T(8,128)} %get-tuple-element.115.dx, ...), custom_call_target="tpu_custom_call" | custom-call | tf_op jit(solution)/shard_map/mlp_back/pallas_call | solution.py:1245
  685.6 24.7 %attend_back.3 = (bf16[512,1088]{1,0:T(8,128)(2,1)}, bf16[2,512,1088]{2,1,0:T(8,128)(2,1)}, bf16[2,512,1088]{2,1,0:T(8,128)(2,1)}) custom-call(bf16[512,1088]{1,0:T(8,128)(2,1)} %get-tuple-element.119.q, bf16[512,1088]{1,0:T(8,128)(2,1)} %get-tuple-element.120.g_attended, bf16[512,1088]{1,0:T(8,128)(2,1)} %get-tuple-element.121.attended, ...), custom_call_target="tpu_custom_call" | custom-call | tf_op jit(solution)/shard_map/attend_back/pallas_call | solution.py:1325
  715.0 11.5 %convolution_convert_fusion.2 = bf16[4352,1088]{0,1:T(8,128)(2,1)} fusion(bf16[512,4352]{1,0:T(8,128)(2,1)} %get-tuple-element.134, bf16[512,1088]{1,0:T(8,128)(2,1)} %get-tuple-element.135), kind=kOutput, calls=%fused_computation.2 | convolution fusion | flops 4853350400 | bytes 15040512 | tf_op jit(solution)/shard_map/dot_general | solution.py:34
  726.4 13.9 %copy.87 = bf16[4352,1088]{1,0:T(8,128)(2,1)} copy(bf16[4352,1088]{0,1:T(8,128)(2,1)} %convolution_convert_fusion.2) | data formatting | bytes 18939904 | tf_op jit(solution)/shard_map/convert_element_type | solution.py:1657
  751.0 7.8 convolution_convert_fusion.3
  758.8 3.7 copy-done.1
  763.3 4.3 copy.84.g_got
  767.7 17.8 %project_back.3 = (f32[512,1088]{1,0:T(8,128)}, bf16[512,3264]{1,0:T(8,128)(2,1)}, f32[1,1088]{1,0:T(1,128)}, f32[1,1088]{1,0:T(1,128)}, f32[1,1088]{1,0:T(1,128)}, /*index=5*/f32[1,1088]{1,0:T(1,128)}) custom-call(f32[512,1088]{1,0:T(8,128)} %get-tuple-element.94.x, f32[512,1088]{1,0:T(8,128)} %get-tuple-element.118.g_middle, ...), custom_call_target="tpu_custom_call" | custom-call | tf_op jit(solution)/shard_map/project_back/pallas_call | solution.py:1366
  787.5 6.0 convolution_convert_fusion.5
  799.9 196.2 %reduce_grads.2 = (bf16[16,16,3264]{2,1,0:T(8,128)(2,1)}, bf16[16,16,1088]{2,1,0:T(8,128)(2,1)}, bf16[16,16,4352]{2,1,0:T(8,128)(2,1)}, bf16[64,16,1088]{2,1,0:T(8,128)(2,1)}, bf16[8,16,1664]{2,1,0:T(8,128)(2,1)}) custom-call(bf16[4,17,16,3264]{3,2,1,0:T(8,128)(2,1)} %bitcast.157, bf16[4,17,16,1088]{3,2,1,0:T(8,128)(2,1)} %bitcast.165, ...), custom_call_target="tpu_custom_call" | custom-call | tf_op jit(solution)/shard_map/reduce_grads/pallas_call | solution.py:1627
  1021.1 5.1 maximum_convert_fusion.1
  1026.3 4.4 maximum_convert_fusion
  (218 shorter events, 105.8 us)
Async XLA Ops:
  293.0 115.7 %collective-permute-start.1 = (bf16[256,1088]{0,1:T(8,128)(2,1)}, bf16[256,1088]{0,1:T(8,128)(2,1)}, u32[]{:S(2)}, u32[]{:S(2)}) collective-permute-start(bf16[256,1088]{0,1:T(8,128)(2,1)} %copy.80), channel_id=1, source_target_pairs={{1,0},{17,1},{3,2},{19,3},{0,16},{16,17},{2,18},{18,19},{5,4},{21,... | collective-permute-start | bytes 1671176 | tf_op jit(solution)/shard_map/ppermute | solution.py:387
  294.8 114.0 %collective-permute-start = (bf16[256,1088]{0,1:T(8,128)(2,1)}, bf16[256,1088]{0,1:T(8,128)(2,1)}, u32[]{:S(2)}, u32[]{:S(2)}) collective-permute-start(bf16[256,1088]{0,1:T(8,128)(2,1)} %copy.79), channel_id=1, source_target_pairs={{0,0},{16,1},{2,2},{18,3},{1,16},{17,17},{3,18},{19,19},{4,4},{20,... | collective-permute-start | bytes 1671176 | tf_op jit(solution)/shard_map/ppermute | solution.py:386
  357.1 10.5 %copy-start.40 = (bf16[512,1088]{1,0:T(8,128)(2,1)S(1)}, bf16[512,1088]{1,0:T(8,128)(2,1)}, u32[]{:S(2)}) copy-start(bf16[512,1088]{1,0:T(8,128)(2,1)} %get-tuple-element.152) | copy-start | bytes 3342340
  361.8 49.3 %collective-permute-start.2 = (bf16[2,512,1088]{1,2,0:T(8,128)(2,1)}, bf16[2,512,1088]{1,2,0:T(8,128)(2,1)}, u32[]{:S(2)}, u32[]{:S(2)}) collective-permute-start(bf16[2,512,1088]{1,2,0:T(8,128)(2,1)} %copy.81), channel_id=1, source_target_pairs={{0,1},{1,0},{2,3},{3,2},{4,5},{5,4},{6,7},{7,6},{8,9},{9,8},{10,11... | collective-permute-start | bytes 6684680 | tf_op jit(solution)/shard_map/ppermute | solution.py:1686
  377.3 15.1 %copy-start.38 = (bf16[512,1088]{1,0:T(8,128)(2,1)S(1)}, bf16[512,1088]{1,0:T(8,128)(2,1)}, u32[]{:S(2)}) copy-start(bf16[512,1088]{1,0:T(8,128)(2,1)} %get-tuple-element.149) | copy-start | bytes 3342340
  415.2 20.1 %copy-start.37 = (bf16[512,1088]{1,0:T(8,128)(2,1)S(1)}, bf16[512,1088]{1,0:T(8,128)(2,1)}, u32[]{:S(2)}) copy-start(bf16[512,1088]{1,0:T(8,128)(2,1)} %get-tuple-element.146) | copy-start | bytes 3342340
  644.5 36.0 %copy-start.15 = (bf16[512,1088]{1,0:T(8,128)(2,1)S(1)}, bf16[512,1088]{1,0:T(8,128)(2,1)}, u32[]{:S(2)}) copy-start(bf16[512,1088]{1,0:T(8,128)(2,1)} %get-tuple-element.121.attended) | copy-start | bytes 3342340
  713.7 49.6 %collective-permute-start.3 = (bf16[2,512,1088]{1,2,0:T(8,128)(2,1)S(1)}, bf16[2,512,1088]{1,2,0:T(8,128)(2,1)}, u32[]{:S(2)}, u32[]{:S(2)}) collective-permute-start(bf16[2,512,1088]{1,2,0:T(8,128)(2,1)S(1)} %copy.83), channel_id=1, source_target_pairs={{0,1},{1,0},{2,3},{3,2},{4,5},{5,4},{6,7},{7,6},{8,9},{9,8},{10,11... | collective-permute-start | bytes 6684680 | tf_op jit(solution)/shard_map/ppermute | solution.py:1686
  767.7 19.7 %copy-start.24 = (bf16[4,272]{1,0:T(4,128)(2,1)S(1)}, bf16[4,272]{1,0:T(4,128)(2,1)}, u32[]{:S(2)}) copy-start(bf16[4,272]{1,0:T(4,128)(2,1)} %convert_element_type.262) | copy-start | bytes 6532
  767.7 19.8 %copy-start.36 = (bf16[512,1088]{1,0:T(8,128)(2,1)S(1)}, bf16[512,1088]{1,0:T(8,128)(2,1)}, u32[]{:S(2)}) copy-start(bf16[512,1088]{1,0:T(8,128)(2,1)} %get-tuple-element.129) | copy-start | bytes 3342340
  799.9 198.7 %copy-start.8 = (f32[512,1088]{1,0:T(8,128)S(1)}, f32[512,1088]{1,0:T(8,128)}, u32[]{:S(2)}) copy-start(f32[512,1088]{1,0:T(8,128)} %get-tuple-element.128) | copy-start | bytes 6684676
  998.7 11.5 %copy-start.31 = (bf16[1,272]{1,0:T(2,128)(2,1)S(1)}, bf16[1,272]{1,0:T(2,128)(2,1)}, u32[]{:S(2)}) copy-start(bf16[1,272]{1,0:T(2,128)(2,1)} %stack.187) | copy-start | bytes 1636
  998.7 12.7 %copy-start.30 = (bf16[1,272]{1,0:T(2,128)(2,1)S(1)}, bf16[1,272]{1,0:T(2,128)(2,1)}, u32[]{:S(2)}) copy-start(bf16[1,272]{1,0:T(2,128)(2,1)} %stack.183) | copy-start | bytes 1636
  998.7 14.0 %copy-start.29 = (bf16[1,272]{1,0:T(2,128)(2,1)S(1)}, bf16[1,272]{1,0:T(2,128)(2,1)}, u32[]{:S(2)}) copy-start(bf16[1,272]{1,0:T(2,128)(2,1)} %stack.179) | copy-start | bytes 1636
  998.8 15.2 %copy-start.28 = (bf16[1,272]{1,0:T(2,128)(2,1)S(1)}, bf16[1,272]{1,0:T(2,128)(2,1)}, u32[]{:S(2)}) copy-start(bf16[1,272]{1,0:T(2,128)(2,1)} %stack.173) | copy-start | bytes 1636
  998.8 16.5 %copy-start.27 = (bf16[1,272]{1,0:T(2,128)(2,1)S(1)}, bf16[1,272]{1,0:T(2,128)(2,1)}, u32[]{:S(2)}) copy-start(bf16[1,272]{1,0:T(2,128)(2,1)} %stack.169) | copy-start | bytes 1636
  998.8 17.7 %copy-start.25 = (bf16[1,272]{1,0:T(2,128)(2,1)S(1)}, bf16[1,272]{1,0:T(2,128)(2,1)}, u32[]{:S(2)}) copy-start(bf16[1,272]{1,0:T(2,128)(2,1)} %stack.163) | copy-start | bytes 1636
  998.8 18.3 %copy-start.26 = (bf16[1,272]{1,0:T(2,128)(2,1)S(1)}, bf16[1,272]{1,0:T(2,128)(2,1)}, u32[]{:S(2)}) copy-start(bf16[1,272]{1,0:T(2,128)(2,1)} %stack.159) | copy-start | bytes 1636
  998.8 19.6 %copy-start.19 = (bf16[16,16,1088]{2,1,0:T(8,128)(2,1)S(1)}, bf16[16,16,1088]{2,1,0:T(8,128)(2,1)}, u32[]{:S(2)}) copy-start(bf16[16,16,1088]{2,1,0:T(8,128)(2,1)} %get-tuple-element.166) | copy-start | bytes 1671172
  1000.0 21.2 %copy-start.21 = (bf16[1,16,4352]{2,1,0:T(8,128)(2,1)S(1)}, bf16[1,16,4352]{2,1,0:T(8,128)(2,1)}, u32[]{:S(2)}) copy-start(bf16[1,16,4352]{2,1,0:T(8,128)(2,1)} %get-tuple-element.208) | copy-start | bytes 417796
  1001.0 20.1 %copy-start.9 = (bf16[16,16,4352]{2,1,0:T(8,128)(2,1)S(1)}, bf16[16,16,4352]{2,1,0:T(8,128)(2,1)}, u32[]{:S(2)}) copy-start(bf16[16,16,4352]{2,1,0:T(8,128)(2,1)} %get-tuple-element.168) | copy-start | bytes 6684676
  1001.0 33.0 %collective-permute-start.5 = (bf16[256,1088]{0,1:T(8,128)(2,1)}, bf16[256,1088]{0,1:T(8,128)(2,1)}, u32[]{:S(2)}, u32[]{:S(2)}) collective-permute-start(bf16[256,1088]{0,1:T(8,128)(2,1)} %copy.86), channel_id=1, source_target_pairs={{1,0},{17,1},{3,2},{19,3},{0,16},{16,17},{2,18},{18,19},{5,4},{21,... | collective-permute-start | bytes 1671176 | tf_op jit(solution)/shard_map/ppermute | solution.py:387
  1001.1 32.9 %collective-permute-start.4 = (bf16[256,1088]{0,1:T(8,128)(2,1)}, bf16[256,1088]{0,1:T(8,128)(2,1)}, u32[]{:S(2)}, u32[]{:S(2)}) collective-permute-start(bf16[256,1088]{0,1:T(8,128)(2,1)} %copy.85), channel_id=1, source_target_pairs={{0,0},{16,1},{2,2},{18,3},{1,16},{17,17},{3,18},{19,19},{4,4},{20,... | collective-permute-start | bytes 1671176 | tf_op jit(solution)/shard_map/ppermute | solution.py:386
  1008.1 13.0 %copy-start.10 = (bf16[16,16,4352]{2,1,0:T(8,128)(2,1)S(1)}, bf16[16,16,4352]{2,1,0:T(8,128)(2,1)}, u32[]{:S(2)}) copy-start(bf16[16,16,4352]{2,1,0:T(8,128)(2,1)} %get-tuple-element.167) | copy-start | bytes 6684676
  (23 other events, 153.3 us)

commit v3 on v2

--- a/solution.py
+++ b/solution.py
@@ -435,6 +435,8 @@
 QUERY_SCALE = 1.0 / math.sqrt(HEAD_DIM)
 HEAD_ROWS = 24
 PACE = 2
+REDUCE_PACE = 6
+SKEW = 2
 
 
 NT = (((1,), (1,)), ((), ()))
@@ -750,7 +752,7 @@
     (
         wq, wo, wu, wd, xs, tok, na, nm, q, keys, values, mask, att, middle, slope, act_buf, lse,
         vecs, rows, b_up, b_proj, seg_nat, seg_row,
-        send_sem, recv_sem, load_sem, save_sem, kv_send, kv_recv, in_send, in_recv, in_local, free_sem,
+        send_sem, recv_sem, load_sem, own_sem, save_sem, kv_send, kv_recv, in_send, in_recv, in_local, free_sem,
     ) = rest_refs[layers * len(SAVED) :]
     place = neighbours()
     x, y, z, c, across, beside, twin, up, down = place
@@ -876,9 +878,16 @@
                 if u != upto and following[0] < layers and ("here", following) not in seen:
                     continue
                 arrive(u)
+                if layer:
+                    own_rows((layer - 1, m)).wait()
                 for copy in loads(u):
                     copy.start()
                 loaded[u] = True
+
+    def own_rows(u):
+        layer, m = u
+        n = parts[m].shape[1]
+        return pltpu.make_async_copy(buffers[m].at[pl.ds(z * n, n)], fulls[m].at[layer, z], own_sem.at[layer, m])
 
     def need(u):
         while ("here", u) not in seen:
@@ -887,6 +896,7 @@
         fetch_ready(u)
         for copy in loads(u):
             copy.wait()
+        own_rows(u).start()
 
     pending = []
 
@@ -1091,6 +1101,8 @@
         copy.wait_send()
     finish_in()
     finish()
+    for m in range(len(parts)):
+        own_rows((layers - 1, m)).wait()
     out.wait()
 
 
@@ -1148,6 +1160,7 @@
         dma((units, ZN, 7)),
         dma((units, ZN, 7)),
         dma((len(weights) + 1, ZN)),
+        dma((layers, len(weights))),
         dma((layers, len(SAVED) + 2)),
         dma((layers, 2, 2)),
         dma((layers, 2, 2)),
@@ -1172,17 +1185,6 @@
     return fulls, result, grads_here, mask, vector_rows, saved
 
 
-def bring(layer, own, full, buffer, sems, i):
-    z = lax.axis_index("fsdp")
-    n = own.shape[1]
-    return [pltpu.make_async_copy(own.at[layer], buffer.at[pl.ds(z * n, n)], sems.at[i, 0])] + [
-        pltpu.make_async_copy(
-            full.at[layer, (z + s) % ZN], buffer.at[pl.ds((z + s) % ZN * n, n)], sems.at[i, s]
-        )
-        for s in range(1, ZN)
-    ]
-
-
 def begin(copies):
     for copy in copies:
         copy.start()
@@ -1193,497 +1195,737 @@
         copy.wait()
 
 
-def some_rows(buffer, start, size):
-    return buffer[pl.ds(start // 16, size // 16)].reshape(size, buffer.shape[2])
-
-
-def mlp_back_body(
-    layer, dx, middle, gain, slope, down_own, down_full, up_own, up_full, out_own, out_full,
-    g_mlp, g_pre, g_middle, g_branch, g_attended, gb_down, gb_up, g_gain, g_shift, gb_out,
-    w_down, w_up, w_out, g_norm, sems,
-):
-    copies = [
-        bring(layer, down_own, down_full, w_down, sems, 0),
-        bring(layer, up_own, up_full, w_up, sems, 1),
-        bring(layer, out_own, out_full, w_out, sems, 2),
+ORDER = (0, 1, 3, 2)
+RC, R1, R2, RZ, RX, RY, RD1, RD2, RCC, R1B, RZX = 0, 4, 8, 12, 16, 17, 18, 19, 20, 21, 25
+
+
+class Group:
+    def __init__(self, grad, out, base, k):
+        self.grad, self.out, self.base, self.k = grad, out, base, k
+
+
+def reduce_steps(place, groups, acc, stage, first_in, second_in, line_in, line_extra, load_sem, store_sem, send_sem, recv_sem):
+    x, y, z, c, across, beside, twin, up, down = place
+    p = x * 2 + y
+    units = [(g, d) for g in range(len(groups)) for d in ORDER]
+
+    def move(source, target, g, kind, device):
+        return pltpu.make_async_remote_copy(
+            src_ref=source, dst_ref=target, send_sem=send_sem.at[g, kind], recv_sem=recv_sem.at[g, kind],
+            device_id=device, device_id_type=MESH,
+        )
+
+    def half_of(g, d, core):
+        group = groups[g]
+        return group.grad.at[d, pl.ds(group.base + core * 4 * group.k, 4 * group.k)]
+
+    def to_twin(g, d):
+        return move(half_of(g, d, 1 - c), acc[g].at[d], g, RC + d, twin)
+
+    def slot(d):
+        return ORDER.index(d) % 2
+
+    def load(g, d):
+        return pltpu.make_async_copy(half_of(g, d, c), stage[g].at[slot(d)], load_sem.at[g, slot(d)])
+
+    def add(g, d, at, extra, lead, extra_at, n):
+        def step(i, carry):
+            acc[g][d, at + i] = acc[g][d, at + i] + extra[lead, extra_at + i]
+            return carry
+
+        lax.fori_loop(0, n, step, 0)
+
+    def first_moves(g, d):
+        k = groups[g].k
+        if d in (0, 3):
+            return [move(acc[g].at[d, pl.ds((1 - x) * 2 * k, 2 * k)], first_in[g].at[d], g, R1 + d, across)]
+        return [
+            move(acc[g].at[d, pl.ds((1 - y) * k, k)], first_in[g].at[d, pl.ds(0, k)], g, R1 + d, beside),
+            move(acc[g].at[d, pl.ds((3 - y) * k, k)], first_in[g].at[d, pl.ds(k, k)], g, R1B + d, beside),
+        ]
+
+    def second_move(g, d):
+        k = groups[g].k
+        if d in (0, 3):
+            return move(acc[g].at[d, pl.ds((x * 2 + 1 - y) * k, k)], second_in[g].at[d], g, R2 + d, beside)
+        return move(acc[g].at[d, pl.ds(((1 - x) * 2 + y) * k, k)], second_in[g].at[d], g, R2 + d, across)
+
+    def twin_step(g, d):
+        to_twin(g, d).wait_recv()
+        load(g, d).wait()
+        add(g, d, 0, stage[g], slot(d), 0, 4 * groups[g].k)
+        for copy in first_moves(g, d):
+            copy.start()
+        later = ORDER.index(d) + 2
+        if later < len(ORDER):
+            load(g, ORDER[later]).start()
+
+    def first_step(g, d):
+        k = groups[g].k
+        for copy in first_moves(g, d):
+            copy.wait_recv()
+        if d in (0, 3):
+            add(g, d, x * 2 * k, first_in[g], d, 0, 2 * k)
+        else:
+            add(g, d, y * k, first_in[g], d, 0, k)
+            add(g, d, (2 + y) * k, first_in[g], d, k, k)
+        second_move(g, d).start()
+
+    def second_step(g, d):
+        second_move(g, d).wait_recv()
+        add(g, d, p * groups[g].k, second_in[g], d, 0, groups[g].k)
+
+    def piece(g, d):
+        return acc[g].at[d, pl.ds(p * groups[g].k, groups[g].k)]
+
+    def to_down(g, d, zz):
+        if d == zz - 1:
+            return move(piece(g, d), line_extra[g].at[0], g, RZX, down)
+        return move(piece(g, d), line_in[g].at[d], g, RZ + d, down)
+
+    def to_up(g, d, zz):
+        return move(piece(g, d), line_in[g].at[d], g, RZ + d, up)
+
+    def rows_of(g, px, py, low=0, n=None):
+        group = groups[g]
+        return group.out.at[pl.ds(group.base + (c * 4 + px * 2 + py) * group.k + low, group.k if n is None else n)]
+
+    def share_across(g):
+        return move(piece(g, z), rows_of(g, x, y), g, RX, across)
+
+    def share_beside(g):
+        return move(piece(g, z), rows_of(g, x, y), g, RY, beside)
+
+    def store(g):
+        return pltpu.make_async_copy(piece(g, z), rows_of(g, x, y), store_sem.at[g])
+
+    def arrived(g, px, py, kind):
+        return move(rows_of(g, px, py), rows_of(g, px, py), g, kind, across)
+
+    def corner(g, px, py, part):
+        k = groups[g].k
+        low, n = (0, max(k // 2, 1)) if part == 0 else (k // 2, k - k // 2)
+        rows = rows_of(g, px, py, low, n)
+        return move(rows, rows, g, RD1 if part == 0 else RD2, beside if part == 0 else across)
+
+    def to_core(g, core):
+        group = groups[g]
+        rows = group.out.at[pl.ds(group.base + core * 4 * group.k, 4 * group.k)]
+        return move(rows, rows, g, RCC, twin)
+
+    def line_step(g, d, s):
+        k = groups[g].k
+        for zz in range(ZN):
+            downward = d < zz and zz == ZN - 1 - s
+            upward = d > zz and zz == s
+            last = d == zz and s == ZN - 1
+            if not (downward or upward or last):
+                continue
+
+            @pl.when(z == zz)
+            def _():
+                if downward:
+                    if zz < ZN - 1:
+                        to_down(g, d, zz + 1).wait_recv()
+                        add(g, d, p * k, line_in[g], d, 0, k)
+                    to_down(g, d, zz).start()
+                if upward:
+                    if zz > 0:
+                        to_up(g, d, zz - 1).wait_recv()
+                        add(g, d, p * k, line_in[g], d, 0, k)
+                    to_up(g, d, zz).start()
+                if last:
+                    if zz > 0:
+                        to_up(g, d, zz - 1).wait_recv()
+                        add(g, d, p * k, line_in[g], d, 0, k)
+                    if zz < ZN - 1:
+                        to_down(g, d, zz + 1).wait_recv()
+                        add(g, d, p * k, line_extra[g], 0, 0, k)
+                    share_across(g).start()
+                    share_beside(g).start()
+                    store(g).start()
+
+    def corner_step(g, d):
+        @pl.when(z == d)
+        def _():
+            arrived(g, 1 - x, y, RX).wait_recv()
+            corner(g, 1 - x, y, 0).start()
+            arrived(g, x, 1 - y, RY).wait_recv()
+            if groups[g].k > 1:
+                corner(g, x, 1 - y, 1).start()
+
+    def core_step(g, d):
+        @pl.when(z == d)
+        def _():
+            store(g).wait()
+            corner(g, 1 - x, 1 - y, 0).wait_recv()
+            if groups[g].k > 1:
+                corner(g, 1 - x, 1 - y, 1).wait_recv()
+            to_core(g, c).start()
+
+    def finish():
+        for g, d in units:
+            to_twin(g, d).wait_send()
+            for copy in first_moves(g, d) + [second_move(g, d)]:
+                copy.wait_send()
+            for zz in range(ZN):
+                if d == zz:
+                    continue
+
+                @pl.when(z == zz)
+                def _():
+                    (to_down(g, d, zz) if d < zz else to_up(g, d, zz)).wait_send()
+
+            @pl.when(z == d)
+            def _():
+                to_core(g, 1 - c).wait_recv()
+                share_across(g).wait_send()
+                share_beside(g).wait_send()
+                corner(g, 1 - x, y, 0).wait_send()
+                if groups[g].k > 1:
+                    corner(g, x, 1 - y, 1).wait_send()
+                to_core(g, c).wait_send()
+
+    count = len(units)
+    stages = [(0, twin_step), (SKEW, first_step), (2 * SKEW, second_step)]
+    stages += [((2 + s) * SKEW, functools.partial(line_step, s=s)) for s in range(ZN)]
+    stages += [((2 + ZN) * SKEW, corner_step), ((3 + ZN) * SKEW, core_step)]
+
+    def steps():
+        for g, d in units:
+            to_twin(g, d).start()
+            if ORDER.index(d) < 2:
+                load(g, d).start()
+        yield True
+        for t in range(count + stages[-1][0]):
+            for delay, step in stages:
+                if 0 <= t - delay < count:
+                    step(*units[t - delay])
+                    yield True
+
+    return steps(), finish
+
+
+def reduce_scratch(groups):
+    low = jnp.bfloat16
+    buffers = []
+    for lead, rows in ((ZN, 4), (2, 4), (ZN, 2), (ZN, 1), (ZN, 1), (1, 1)):
+        buffers += [pltpu.VMEM((lead, rows * k) + shape, low) for k, shape in groups]
+    dma = pltpu.SemaphoreType.DMA
+    n = len(groups)
+    return buffers + [dma((n, 2)), dma((n,)), dma((n, 26)), dma((n, 26))]
+
+
+def take_reduce(place, spec, grads, outs, refs):
+    n = len(spec)
+    groups = [Group(grads[m], outs[m], base, k) for m, base, k in spec]
+    lists = [refs[i * n : (i + 1) * n] for i in range(6)]
+    return reduce_steps(place, groups, *lists, *refs[6 * n : 6 * n + 4])
+
+
+def spread_steps(work, comm, finish):
+    for _ in work:
+        if comm is not None:
+            advance(comm, REDUCE_PACE)
+    if comm is not None:
+        for _ in comm:
+            pass
+        finish()
+
+
+def spec_of(shapes, split):
+    spec = []
+    for m, shape in enumerate(shapes):
+        k = shape[1] // 8
+        for base in range(0, k // min(k, split)):
+            spec.append((m, base * 8 * min(k, split), min(k, split)))
+    return spec
+
+
+def stream(source, buffer, sems, width_rows, act):
+    chunks = source.shape[0]
+    per = buffer.shape[1]
+    whole, left = chunks // per, chunks % per
+
+    def fetch(i, n):
+        return pltpu.make_async_copy(
+            source.at[pl.ds(i * per, n)], buffer.at[i % 2, pl.ds(0, n)], sems.at[i % 2]
+        )
+
+    def begin():
+        fetch(0, per).start()
+
+    def run(low, high):
+        def step(i, carry):
+            fetch(i, per).wait()
+
+            @pl.when(i + 1 < whole)
+            def _():
+                fetch(i + 1, per).start()
+
+            if left:
+
+                @pl.when(i + 1 == whole)
+                def _():
+                    fetch(whole, left).start()
+
+            act(pl.multiple_of(i * per * 16, per * 16), per * 16, buffer[i % 2].reshape(per * 16, -1))
+            return carry
+
+        if low < min(high, whole):
+            lax.fori_loop(low, min(high, whole), step, 0)
+        if high > whole and left:
+            fetch(whole, left).wait()
+            act(whole * per * 16, left * 16, buffer[whole % 2, :left].reshape(left * 16, -1))
+
+    return begin, run, whole + (1 if left else 0)
+
+
+def each(low, high, size):
+    return [(at, min(at + size, high)) for at in range(low, high, size)]
+
+
+def mlp_work(layer, ins, outs, refs):
+    grad_in, middle_in, slope_in, normed_in, activated_in, gain, w_out, w_up, w_down = ins
+    g_middle_out, g_branch_out, g_attended_out, dw_up, dw_down, gb_down, gb_up, g_gain, g_shift, gb_out = outs
+    (
+        grad, middle, g_norm, slope, g_mlp, g_branch, g_att, nm, turned,
+        narrow, broad, act_tiles, down_tiles, up_tiles, load_sem, narrow_sem, broad_sem, act_sem, down_sem, up_sem,
+    ) = refs
+    width = grad.shape[1]
+    ff = slope.shape[1]
+    loads = [
+        pltpu.make_async_copy(a, b, load_sem.at[i])
+        for i, (a, b) in enumerate(((grad_in, grad), (middle_in, middle), (slope_in, slope), (normed_in, nm)))
     ]
-    for copy in copies:
-        begin(copy)
-    g_mlp[...] = dx[...].astype(jnp.bfloat16)
+    begin(loads)
+
+    def down_act(start, size, rows):
+        cols = pl.ds(start, size)
+        g = (dot_nt(g_mlp[...], rows) * slope[:, cols].astype(jnp.float32)).astype(jnp.bfloat16)
+        slope[:, cols] = g
+        gb_up[:, cols] = jnp.sum(g.astype(jnp.float32), axis=0, keepdims=True)
+
+    def up_act(start, size, rows):
+        g_norm[:, pl.ds(start, size)] = dot_nt(slope[...], rows)
+
+    def out_act(start, size, rows):
+        g_att[:, pl.ds(start, size)] = dot_nt(g_branch[...], rows).astype(jnp.bfloat16)
+
+    down_begin, down_run, down_n = stream(w_down.at[layer], narrow, narrow_sem, 0, down_act)
+    up_begin, up_run, up_n = stream(w_up.at[layer], broad, broad_sem, 0, up_act)
+    out_begin, out_run, out_n = stream(w_out.at[layer], narrow, narrow_sem, 0, out_act)
+    down_begin()
+    up_begin()
+    loads[0].wait()
+    g_mlp[...] = grad[...].astype(jnp.bfloat16)
     gb_down[...] = jnp.sum(g_mlp[...].astype(jnp.float32), axis=0, keepdims=True)
-    end(copies[0])
-
-    def down_step(start, size):
-        cols = pl.ds(start, size)
-        g = (dot_nt(g_mlp[...], some_rows(w_down, start, size)) * slope[:, cols].astype(jnp.float32)).astype(jnp.bfloat16)
-        g_pre[:, cols] = g
-        gb_up[:, cols] = jnp.sum(g.astype(jnp.float32), axis=0, keepdims=True)
-
-    tiles(g_pre.shape[1], BLOCK, down_step)
-    end(copies[1])
-
-    def up_step(start, size):
-        cols = pl.ds(start, size)
-        g_norm[:, cols] = dot_nt(g_pre[...], some_rows(w_up, start, size))
-
-    tiles(dx.shape[1], BLOCK, up_step)
-    norm_back(middle, g_norm, dx, gain[...], g_middle, g_gain, g_shift, g_branch)
+    loads[2].wait()
+    yield
+    for low, high in each(0, down_n, 4):
+        down_run(low, high)
+        yield
+    out_begin()
+    for low, high in each(0, up_n, 2):
+        up_run(low, high)
+        yield
+    loads[1].wait()
+    norm_back(middle, g_norm, grad, gain[...], grad, g_gain, g_shift, g_branch)
+    saves = [pltpu.make_async_copy(grad, g_middle_out, load_sem.at[0]), pltpu.make_async_copy(g_branch, g_branch_out, load_sem.at[1])]
+    begin(saves)
     gb_out[...] = jnp.sum(g_branch[...].astype(jnp.float32), axis=0, keepdims=True)
-    end(copies[2])
-
-    def out_step(start, size):
-        cols = pl.ds(start, size)
-        g_attended[:, cols] = dot_nt(g_branch[...], some_rows(w_out, start, size)).astype(jnp.bfloat16)
-
-    tiles(dx.shape[1], BLOCK, out_step)
-
-
-def mlp_back(layer, dx, middle, slope, gain, owns, fulls):
-    rows, width = dx.shape
-    ff = slope.shape[1]
+    yield
+    out_run(0, out_n)
+    saves.append(pltpu.make_async_copy(g_att, g_attended_out, load_sem.at[2]))
+    begin(saves[2:])
+    loads[3].wait()
+    turned[...] = nm[...].T
+    yield
+
+    tile = act_tiles.shape[2]
+
+    def bring_act(i, n):
+        return pltpu.make_async_copy(
+            activated_in.at[:, pl.ds(pl.multiple_of(i * tile, tile), n)], act_tiles.at[i % 2, :, pl.ds(0, n)], act_sem.at[i % 2]
+        )
+
+    def send_down(i, n):
+        return pltpu.make_async_copy(
+            down_tiles.at[i % 2, pl.ds(0, n // 16)], dw_down.at[pl.ds(i * (tile // 16), n // 16)], down_sem.at[i % 2]
+        )
+
+    whole, left = ff // tile, ff % tile
+    bring_act(0, tile).start()
+
+    def down_grad(i, carry):
+        bring_act(i, tile).wait()
+
+        @pl.when(i + 1 < whole)
+        def _():
+            bring_act(i + 1, tile).start()
+
+        if left:
+
+            @pl.when(i + 1 == whole)
+            def _():
+                bring_act(whole, left).start()
+
+        @pl.when(i >= 2)
+        def _():
+            send_down(i - 2, tile).wait()
+
+        out = dot_tn(act_tiles[i % 2], g_mlp[...]).astype(jnp.bfloat16)
+        down_tiles[i % 2] = out.reshape(tile // 16, 16, width)
+        send_down(i, tile).start()
+        return carry
+
+    for low, high in each(0, whole, 2):
+        lax.fori_loop(low, high, down_grad, 0)
+        yield
+    if left:
+        bring_act(whole, left).wait()
+        send_down(whole - 2, tile).wait()
+        out = dot_tn(act_tiles[whole % 2, :, :left], g_mlp[...]).astype(jnp.bfloat16)
+        down_tiles[whole % 2, : left // 16] = out.reshape(left // 16, 16, width)
+        send_down(whole, left).start()
+        yield
+
+    step = up_tiles.shape[3]
+
+    def send_up(i):
+        return pltpu.make_async_copy(
+            up_tiles.at[i % 2], dw_up.at[:, :, pl.ds(pl.multiple_of(i * step, step), step)], up_sem.at[i % 2]
+        )
+
+    def up_grad(i, carry):
+        @pl.when(i >= 2)
+        def _():
+            send_up(i - 2).wait()
+
+        out = product(turned[...], slope[:, pl.ds(pl.multiple_of(i * step, step), step)]).astype(jnp.bfloat16)
+        up_tiles[i % 2] = out.reshape(width // 16, 16, step)
+        send_up(i).start()
+        return carry
+
+    for low, high in each(0, ff // step, 4):
+        lax.fori_loop(low, high, up_grad, 0)
+        yield
+    send_up(ff // step - 2).wait()
+    send_up(ff // step - 1).wait()
+    send_down(whole - 1, tile).wait()
+    if left:
+        send_down(whole, left).wait()
+    else:
+        send_down(whole - 2, tile).wait()
+    end(saves)
+
+
+def mlp_refs(rows, width, ff):
     low = jnp.bfloat16
-    return pl.pallas_call(
-        functools.partial(mlp_back_body, layer),
-        out_shape=[
-            shaped((rows, width), low),
-            shaped((rows, ff), low),
-            shaped((rows, width)),
-            shaped((rows, width), low),
-            shaped((rows, width), low),
-            shaped((1, width)),
-            shaped((1, ff)),
-            shaped((1, width)),
-            shaped((1, width)),
-            shaped((1, width)),
-        ],
-        in_specs=whole(4) + anywhere(6),
-        out_specs=whole(10),
-        scratch_shapes=[
-            pltpu.VMEM((ff // 16, 16, width), low),
-            pltpu.VMEM((width // 16, 16, ff), low),
-            pltpu.VMEM((width // 16, 16, width), low),
-            pltpu.VMEM((rows, width), jnp.float32),
-            pltpu.SemaphoreType.DMA((3, ZN)),
-        ],
-        compiler_params=params(),
-        name="mlp_back",
-    )(dx, middle, gain, slope, owns[3], fulls[3], owns[2], fulls[2], owns[1], fulls[1])
-
-
-def attend_back_body(
-    q, g_attended, attended, lse, mask, keys, values, g_q, g_own, g_other, inner, g_k, g_v
-):
-    core = lax.rem(lax.axis_index("rep"), 2)
-    width = q.shape[1]
-    head = lax.broadcasted_iota(jnp.int32, (HEAD_ROWS, width), 0)
-    lane = lax.broadcasted_iota(jnp.int32, (HEAD_ROWS, width), 1)
-    pick = (lane // HEAD_DIM == head).astype(jnp.float32).astype(jnp.bfloat16)
-    both = g_attended[...].astype(jnp.float32) * attended[...].astype(jnp.float32)
-    high = both.astype(jnp.bfloat16)
-    rest = (both - high.astype(jnp.float32)).astype(jnp.bfloat16)
-    inner[...] = dot_nt(pick, high) + dot_nt(pick, rest)
-    def act(start, size, head):
+    dma = pltpu.SemaphoreType.DMA
+    return (
+        [pltpu.VMEM((rows, width), jnp.float32)] * 3
+        + [pltpu.VMEM((rows, ff), low)]
+        + [pltpu.VMEM((rows, width), low)] * 4
+        + [
+            pltpu.VMEM((width, rows), low),
+            pltpu.VMEM((2, 16, 16, width), low),
+            pltpu.VMEM((2, 16, 16, ff), low),
+            pltpu.VMEM((2, rows, 512), low),
+            pltpu.VMEM((2, 32, 16, width), low),
+            pltpu.VMEM((2, width // 16, 16, BLOCK), low),
+            dma((4,)), dma((2,)), dma((2,)), dma((2,)), dma((2,)), dma((2,)),
+        ]
+    )
+
+
+def attend_work(layer, place, ins, outs, refs):
+    q_in, g_att_in, lse_in, mask_in, keys_in, values_in, x_in, g_middle_in, normed_in, attended_in, g_branch_in, gain, w_qkv = ins
+    g_x_out, dw_qkv, dw_out, gb_q, gb_v, g_gain, g_shift = outs
+    (
+        q, g_att, lse, mask, keys, values, g_q, g_k, g_v, g_nat, got, xs, grad, g_norm, g_proj, turned,
+        tall, tiles_qkv, tiles_out, load_sem, tall_sem, qkv_sem, out_sem, swap_send, swap_recv,
+    ) = refs
+    c, twin = place[3], place[6]
+    width = xs.shape[1]
+    pairs = (
+        (q_in, q), (g_att_in, g_att), (lse_in, lse), (mask_in, mask), (keys_in, keys), (values_in, values),
+        (x_in, xs), (g_middle_in, grad),
+    )
+    loads = [pltpu.make_async_copy(a, b, load_sem.at[i]) for i, (a, b) in enumerate(pairs)]
+    begin(loads)
+
+    def norm_act(start, size, rows):
+        g_norm[:, pl.ds(start, size)] = dot_nt(g_proj[...], rows)
+
+    tall_begin, tall_run, tall_n = stream(w_qkv.at[layer], tall, tall_sem, 0, norm_act)
+    tall_begin()
+    end(loads[:6])
+    yield
+
+    def slab(start, size, head):
         cols = pl.ds(start, size)
         g_k[...] = jnp.zeros_like(g_k)
         g_v[...] = jnp.zeros_like(g_v)
         lanes = slice(0, size)
         for variant in range(2):
 
-            @pl.when(core == variant)
+            @pl.when(c == variant)
             def _():
                 for row, high in RANGES[variant]:
                     rows = slice(row, row + BLOCK)
-                    qs, gs = q[rows, cols], g_attended[rows, cols]
+                    qs, gs = q[rows, cols], g_att[rows, cols]
                     ks, vs = keys[:high, cols], values[:high, cols]
                     parts = []
                     for j in range(size // HEAD_DIM):
                         q_j, g_j = of_head(qs, j), of_head(gs, j)
                         s = dot_nt(ks, q_j) + mask[:high, rows]
                         p = jnp.exp(s - lse[pl.ds(head + j, 1), rows])
-                        g_p = dot_nt(vs, g_j)
-                        g_s = (p * (g_p - inner[pl.ds(head + j, 1), rows])).astype(jnp.bfloat16)
+                        g_p = p * dot_nt(vs, g_j)
+                        inner = jnp.sum(g_p, axis=0, keepdims=True)
+                        g_s = (g_p - p * inner).astype(jnp.bfloat16)
                         g_v[:high, lanes] += product(p.astype(jnp.bfloat16), g_j)
                         g_k[:high, lanes] += product(g_s, q_j)
                         parts.append(dot_tn(ks, g_s)[j * HEAD_DIM : (j + 1) * HEAD_DIM])
                     out = jnp.concatenate(parts, axis=0) if len(parts) > 1 else parts[0]
                     g_q[rows, cols] = out.T.astype(jnp.bfloat16) * QUERY_SCALE
 
-        for block in range(2):
-            rows = slice(block * BLOCK, (block + 1) * BLOCK)
-            for target, who in ((g_own, core), (g_other, 1 - core)):
-                at = ((2 * who) if block == 0 else (3 - 2 * who)) * BLOCK
-                spot = pl.ds(pl.multiple_of(at, BLOCK), BLOCK)
-                target[0, rows, cols] = g_k[spot, lanes].astype(jnp.bfloat16)
-                target[1, rows, cols] = g_v[spot, lanes].astype(jnp.bfloat16)
-
-    over_slabs(width, act, 0, width // (2 * HEAD_DIM) + 1)
-
-
-def attend_back(q, g_attended, attended, lse, mask, keys, values):
-    rows, width = q.shape
+        g_nat[0, :, cols] = g_k[:, lanes].astype(jnp.bfloat16)
+        g_nat[1, :, cols] = g_v[:, lanes].astype(jnp.bfloat16)
+
+    slab_count = width // (2 * HEAD_DIM) + 1
+    for first, last in each(0, slab_count, 2):
+        over_slabs(width, slab, first, last)
+        yield
+
+    def spot(who, block):
+        at = ((2 * who) if block == 0 else (3 - 2 * who)) * BLOCK
+        return pl.ds(pl.multiple_of(at, BLOCK), BLOCK)
+
+    swaps = [
+        pltpu.make_async_remote_copy(
+            src_ref=g_nat.at[i, spot(1 - c, block)], dst_ref=got.at[i, pl.ds(block * BLOCK, BLOCK)],
+            send_sem=swap_send.at[i, block], recv_sem=swap_recv.at[i, block], device_id=twin, device_id_type=MESH,
+        )
+        for i in range(2)
+        for block in range(2)
+    ]
+    begin(swaps)
+    more = [
+        pltpu.make_async_copy(attended_in, q, load_sem.at[0]),
+        pltpu.make_async_copy(g_branch_in, g_att, load_sem.at[1]),
+    ]
+    begin(more)
+    g_proj[:, :width] = g_q[...]
+    gb_q[...] = jnp.sum(g_q[...].astype(jnp.float32), axis=0, keepdims=True)
+    yield
+    end(more)
+    turned[...] = q[...].T
+    rows = tiles_out.shape[1] * 16
+
+    def row_grad(right, tiles_ref, sem, target, i):
+        def act(start, size):
+            cols = pl.ds(start, size)
+            out = product(turned[pl.ds(i * rows, rows), :], right[:, cols]).astype(jnp.bfloat16)
+            tiles_ref[i % 2, :, :, cols] = out.reshape(rows // 16, 16, size)
+
+        if i >= 2:
+            row_send(tiles_ref, sem, target, i - 2).wait()
+        tiles_between(0, right.shape[1], BLOCK, act)
+        row_send(tiles_ref, sem, target, i).start()
+
+    def row_send(tiles_ref, sem, target, i):
+        return pltpu.make_async_copy(tiles_ref.at[i % 2], target.at[pl.ds(i * (rows // 16), rows // 16)], sem.at[i % 2])
+
+    for i in range(ZN):
+        row_grad(g_att, tiles_out, out_sem, dw_out, i)
+    yield
+    after = pltpu.make_async_copy(normed_in, q, load_sem.at[0])
+    after.start()
+    for copy in swaps:
+        copy.wait_recv()
+    for block in range(2):
+        part = slice(block * BLOCK, (block + 1) * BLOCK)
+        g_proj[part, width : 2 * width] = g_nat[0, spot(c, block), :] + got[0, part, :]
+        values_part = g_nat[1, spot(c, block), :] + got[1, part, :]
+        g_proj[part, 2 * width :] = values_part
+        total = jnp.sum(values_part.astype(jnp.float32), axis=0, keepdims=True)
+        gb_v[...] = total if block == 0 else gb_v[...] + total
+    yield
+    for low, high in each(0, tall_n, 2):
+        tall_run(low, high)
+        yield
+    end(loads[6:])
+    norm_back(xs, g_norm, grad, gain[...], grad, g_gain, g_shift)
+    save = pltpu.make_async_copy(grad, g_x_out, load_sem.at[1])
+    save.start()
+    after.wait()
+    turned[...] = q[...].T
+    yield
+    for i in range(ZN):
+        row_grad(g_proj, tiles_qkv, qkv_sem, dw_qkv, i)
+        yield
+    for i in (ZN - 2, ZN - 1):
+        row_send(tiles_out, out_sem, dw_out, i).wait()
+        row_send(tiles_qkv, qkv_sem, dw_qkv, i).wait()
+    for copy in swaps:
+        copy.wait_send()
+    save.wait()
+
+
+def attend_refs(rows, width):
     low = jnp.bfloat16
-    return pl.pallas_call(
-        attend_back_body,
-        out_shape=[shaped((rows, width), low), shaped((2, rows, width), low), shaped((2, rows, width), low)],
-        in_specs=whole(7),
-        out_specs=whole(3),
-        scratch_shapes=[
-            pltpu.VMEM((HEAD_ROWS, rows), jnp.float32),
-            pltpu.VMEM((2 * rows, 2 * HEAD_DIM), jnp.float32),
-            pltpu.VMEM((2 * rows, 2 * HEAD_DIM), jnp.float32),
-        ],
-        compiler_params=params(),
+    dma = pltpu.SemaphoreType.DMA
+    share = width // 16 // ZN
+    return [
+        pltpu.VMEM((rows, width), low),
+        pltpu.VMEM((rows, width), low),
+        pltpu.VMEM((HEAD_ROWS, rows), jnp.float32),
+        pltpu.VMEM((2 * rows, rows), jnp.float32),
+        pltpu.VMEM((2 * rows, width), low),
+        pltpu.VMEM((2 * rows, width), low),
+        pltpu.VMEM((rows, width), low),
+        pltpu.VMEM((2 * rows, 2 * HEAD_DIM), jnp.float32),
+        pltpu.VMEM((2 * rows, 2 * HEAD_DIM), jnp.float32),
+        pltpu.VMEM((2, 2 * rows, width), low),
+        pltpu.VMEM((2, rows, width), low),
+        pltpu.VMEM((rows, width), jnp.float32),
+        pltpu.VMEM((rows, width), jnp.float32),
+        pltpu.VMEM((rows, width), jnp.float32),
+        pltpu.VMEM((rows, 3 * width), low),
+        pltpu.VMEM((width, rows), low),
+        pltpu.VMEM((2, 16, 16, 3 * width), low),
+        pltpu.VMEM((2, share, 16, 3 * width), low),
+        pltpu.VMEM((2, share, 16, width), low),
+        dma((8,)), dma((2,)), dma((2,)), dma((2,)), dma((2, 2)), dma((2, 2)),
+    ]
+
+
+def mlp_kernel(layer, grad, kept, gain, fulls, grads, spec):
+    rows, width = grad.shape
+    ff = kept["slope"].shape[1]
+    low = jnp.bfloat16
+    ins = [grad, kept["middle"], kept["slope"], kept["normed_mlp"], kept["activated"], gain, fulls[1], fulls[2], fulls[3]]
+    work_out = [
+        shaped((rows, width)),
+        shaped((rows, width), low),
+        shaped((rows, width), low),
+        shaped((width // 16, 16, ff), low),
+        shaped((ff // 16, 16, width), low),
+    ] + [shaped((1, n)) for n in (width, ff, width, width, width)]
+    work_refs = mlp_refs(rows, width, ff)
+    n, extra = len(work_out), len(grads)
+    in_specs = anywhere(5) + whole(1) + anywhere(3 + extra)
+
+    def body(*refs):
+        i = len(ins) + extra
+        outs, more = refs[i : i + n], refs[i + n : i + n + extra]
+        rest = refs[i + n + extra :]
+        comm = finish = None
+        if extra:
+            place = neighbours()
+            greet(*[place[j] for j in (2, 3, 0, 4, 5, 6)], None, *place[7:])
+            comm, finish = take_reduce(place, spec, refs[len(ins) : i], more, rest[len(work_refs) :])
+        work = mlp_work(layer, refs[: len(ins)], outs, rest[: len(work_refs)])
+        spread_steps(work, comm, finish)
+
+    settings = dict(collective_id=100 + layer, has_side_effects=True) if extra else {}
+    outs = pl.pallas_call(
+        body,
+        out_shape=work_out + [shaped(g.shape[1:], low) for g in grads],
+        in_specs=in_specs,
+        out_specs=anywhere(5) + whole(5) + anywhere(extra),
+        scratch_shapes=work_refs + (reduce_scratch([(k, grads[m].shape[2:]) for m, _, k in spec]) if extra else []),
+        compiler_params=pltpu.CompilerParams(vmem_limit_bytes=VMEM_LIMIT, **settings),
+        name="mlp_back",
+    )(*ins, *grads)
+    return outs[:n], outs[n:]
+
+
+def attend_kernel(layer, kept, mask, g_att, g_middle, g_branch, gain, fulls, grads, spec):
+    rows, width = g_middle.shape
+    low = jnp.bfloat16
+    ins = [
+        kept["q"], g_att, kept["lse"], mask, kept["keys"], kept["values"], kept["x"], g_middle,
+        kept["normed_attn"], kept["attended"], g_branch, gain, fulls[0],
+    ]
+    work_out = [
+        shaped((rows, width)),
+        shaped((width // 16, 16, 3 * width), low),
+        shaped((width // 16, 16, width), low),
+    ] + [shaped((1, width))] * 4
+    work_refs = attend_refs(rows, width)
+    n, extra = len(work_out), len(grads)
+
+    def body(*refs):
+        i = len(ins) + extra
+        outs, more = refs[i : i + n], refs[i + n : i + n + extra]
+        rest = refs[i + n + extra :]
+        place = neighbours()
+        greet(*[place[j] for j in (2, 3, 0, 4, 5, 6)], None, *place[7:])
+        comm, finish = take_reduce(place, spec, refs[len(ins) : i], more, rest[len(work_refs) :])
+        work = attend_work(layer, place, refs[: len(ins)], outs, rest[: len(work_refs)])
+        spread_steps(work, comm, finish)
+
+    outs = pl.pallas_call(
+        body,
+        out_shape=work_out + [shaped(g.shape[1:], low) for g in grads],
+        in_specs=anywhere(11) + whole(1) + anywhere(1 + extra),
+        out_specs=anywhere(3) + whole(4) + anywhere(extra),
+        scratch_shapes=work_refs + reduce_scratch([(k, grads[m].shape[2:]) for m, _, k in spec]),
+        compiler_params=pltpu.CompilerParams(collective_id=200 + layer, has_side_effects=True, vmem_limit_bytes=VMEM_LIMIT),
         name="attend_back",
-    )(q, g_attended, attended, lse, mask, keys, values)
-
-
-def project_back_body(
-    layer, x, g_middle, gain, g_q, g_own, g_got, w_own, w_full, g_x, g_proj, gb_q, gb_v, g_gain, g_shift, w, g_norm, sem
-):
-    width = x.shape[1]
-    load = bring(layer, w_own, w_full, w, sem, 0)
-    begin(load)
-    g_k = g_own[0] + g_got[0]
-    g_v = g_own[1] + g_got[1]
-    gb_q[...] = jnp.sum(g_q[...].astype(jnp.float32), axis=0, keepdims=True)
-    gb_v[...] = jnp.sum(g_v.astype(jnp.float32), axis=0, keepdims=True)
-    g_proj[:, :width] = g_q[...]
-    g_proj[:, width : 2 * width] = g_k
-    g_proj[:, 2 * width :] = g_v
-    end(load)
-
-    def step(start, size):
-        cols = pl.ds(start, size)
-        g_norm[:, cols] = dot_nt(g_proj[...], some_rows(w, start, size))
-
-    tiles(width, BLOCK, step)
-    norm_back(x, g_norm, g_middle, gain[...], g_x, g_gain, g_shift)
-
-
-def project_back(layer, x, g_middle, g_q, g_own, g_got, gain, own, full):
-    rows, width = x.shape
-    low = jnp.bfloat16
-    return pl.pallas_call(
-        functools.partial(project_back_body, layer),
-        out_shape=[
-            shaped((rows, width)),
-            shaped((rows, 3 * width), low),
-            shaped((1, width)),
-            shaped((1, width)),
-            shaped((1, width)),
-            shaped((1, width)),
-        ],
-        in_specs=whole(6) + anywhere(2),
-        out_specs=whole(6),
-        scratch_shapes=[
-            pltpu.VMEM((width // 16, 16, 3 * width), low),
-            pltpu.VMEM((rows, width), jnp.float32),
-            pltpu.SemaphoreType.DMA((1, ZN)),
-        ],
-        compiler_params=params(),
-        name="project_back",
-    )(x, g_middle, gain, g_q, g_own, g_got, own, full)
-
-
-PAIRS = ((0, 1), (3, 2))
-RC, R1, R2, RL, RR, RX, RY, RD1, RD2, RCC, R1B = 0, 4, 8, 12, 16, 20, 21, 22, 23, 24, 25
-
-
-def reduce_body(ks, grads, outs, own, twin_in, first_in, second_in, low_in, high_in, load_sem, store_sem, send_sem, recv_sem):
-    x, y, z, c, across, beside, twin, up, down = neighbours()
-    greet(z, c, x, across, beside, twin, None, up, down)
-    units = [(m, h) for h in range(2) for m in range(len(grads))]
-    p = x * 2 + y
-
-    def move(source, target, m, kind, device):
-        return pltpu.make_async_remote_copy(
-            src_ref=source,
-            dst_ref=target,
-            send_sem=send_sem.at[m, kind],
-            recv_sem=recv_sem.at[m, kind],
-            device_id=device,
-            device_id_type=MESH,
-        )
-
-    def to_twin(m, d):
-        k = ks[m]
-        return move(grads[m].at[d, pl.ds((1 - c) * 4 * k, 4 * k)], twin_in[m].at[d], m, RC + d, twin)
-
-    def load(m, d):
-        k = ks[m]
-        return pltpu.make_async_copy(grads[m].at[d, pl.ds(c * 4 * k, 4 * k)], own[m].at[d], load_sem.at[m, d])
-
-    def add(m, d, at, extra, extra_at, n):
-        def step(i, carry):
-            own[m][d, at + i] = own[m][d, at + i] + extra[d, extra_at + i]
-            return carry
-
-        lax.fori_loop(0, n, step, 0)
-
-    def first_moves(u):
-        m, h = units[u]
-        k = ks[m]
-        a, b = PAIRS[h]
-        return [
-            move(own[m].at[a, pl.ds((1 - x) * 2 * k, 2 * k)], first_in[m].at[a], m, R1 + a, across),
-            move(own[m].at[b, pl.ds((1 - y) * k, k)], first_in[m].at[b, pl.ds(0, k)], m, R1 + b, beside),
-            move(own[m].at[b, pl.ds((3 - y) * k, k)], first_in[m].at[b, pl.ds(k, k)], m, R1B + h, beside),
-        ]
-
-    def second_moves(u):
-        m, h = units[u]
-        k = ks[m]
-        a, b = PAIRS[h]
-        return [
-            move(own[m].at[a, pl.ds((x * 2 + 1 - y) * k, k)], second_in[m].at[a], m, R2 + a, beside),
-            move(own[m].at[b, pl.ds(((1 - x) * 2 + y) * k, k)], second_in[m].at[b], m, R2 + b, across),
-        ]
-
-    def with_twin(u):
-        m, h = units[u]
-        for d in PAIRS[h]:
-            to_twin(m, d).wait_recv()
-            load(m, d).wait()
-            add(m, d, 0, twin_in[m], 0, 4 * ks[m])
-        for copy in first_moves(u):
-            copy.start()
-
-    def with_first(u):
-        m, h = units[u]
-        k = ks[m]
-        a, b = PAIRS[h]
-        for copy in first_moves(u):
-            copy.wait_recv()
-        add(m, a, x * 2 * k, first_in[m], 0, 2 * k)
-        add(m, b, y * k, first_in[m], 0, k)
-        add(m, b, (2 + y) * k, first_in[m], k, k)
-        for copy in second_moves(u):
-            copy.start()
-
-    def with_second(u):
-        m, h = units[u]
-        for copy in second_moves(u):
-            copy.wait_recv()
-        for d in PAIRS[h]:
-            add(m, d, p * ks[m], second_in[m], 0, ks[m])
-
-    def piece(m, d):
-        return own[m].at[d, pl.ds(p * ks[m], ks[m])]
-
-    def to_down(m, d):
-        return move(piece(m, d), high_in[m].at[d], m, RR + d, down)
-
-    def to_up(m, d):
-        return move(piece(m, d), low_in[m].at[d], m, RL + d, up)
-
-    def rows_of(m, px, py, low=0, n=None):
-        k = ks[m]
-        return outs[m].at[pl.ds((c * 4 + px * 2 + py) * k + low, k if n is None else n)]
-
-    def share_across(m):
-        return move(piece(m, z), rows_of(m, x, y), m, RX, across)
-
-    def share_beside(m):
-        return move(piece(m, z), rows_of(m, x, y), m, RY, beside)
-
-    def store(m):
-        return pltpu.make_async_copy(piece(m, z), rows_of(m, x, y), store_sem.at[m])
-
-    def arrived_across(m):
-        return move(rows_of(m, 1 - x, y), rows_of(m, 1 - x, y), m, RX, across)
-
-    def arrived_beside(m):
-        return move(rows_of(m, x, 1 - y), rows_of(m, x, 1 - y), m, RY, beside)
-
-    def corner(m, px, py, part):
-        k = ks[m]
-        low, n = (0, max(k // 2, 1)) if part == 0 else (k // 2, k - k // 2)
-        rows = rows_of(m, px, py, low, n)
-        return move(rows, rows, m, RD1 if part == 0 else RD2, beside if part == 0 else across)
-
-    def to_core(m, core):
-        rows = outs[m].at[pl.ds(core * 4 * ks[m], 4 * ks[m])]
-        return move(rows, rows, m, RCC, twin)
-
-    def line_step(u, s):
-        m, h = units[u]
-        for zz in range(ZN):
-            downward = [d for d in PAIRS[h] if d < zz] if zz == ZN - 1 - s else []
-            upward = [d for d in PAIRS[h] if d > zz] if zz == s else []
-            last = [d for d in PAIRS[h] if d == zz] if s == ZN - 1 else []
-            if not (downward or upward or last):
-                continue
-
-            @pl.when(z == zz)
-            def _():
-                for d in downward:
-                    if zz < ZN - 1:
-                        to_down(m, d).wait_recv()
-                        add(m, d, p * ks[m], high_in[m], 0, ks[m])
-                    to_down(m, d).start()
-                for d in upward:
-                    if zz > 0:
-                        to_up(m, d).wait_recv()
-                        add(m, d, p * ks[m], low_in[m], 0, ks[m])
-                    to_up(m, d).start()
-                for d in last:
-                    if zz > 0:
-                        to_up(m, d).wait_recv()
-                        add(m, d, p * ks[m], low_in[m], 0, ks[m])
-                    if zz < ZN - 1:
-                        to_down(m, d).wait_recv()
-                        add(m, d, p * ks[m], high_in[m], 0, ks[m])
-                    share_across(m).start()
-                    share_beside(m).start()
-                    store(m).start()
-
-    def where_mine(u, act):
-        m, h = units[u]
-
-        @pl.when((z >= min(PAIRS[h])) & (z <= max(PAIRS[h])))
-        def _():
-            act(m)
-
-    def corner_step(u):
-        def act(m):
-            arrived_across(m).wait_recv()
-            corner(m, 1 - x, y, 0).start()
-            arrived_beside(m).wait_recv()
-            if ks[m] > 1:
-                corner(m, x, 1 - y, 1).start()
-
-        where_mine(u, act)
-
-    def core_step(u):
-        def act(m):
-            store(m).wait()
-            corner(m, 1 - x, 1 - y, 0).wait_recv()
-            if ks[m] > 1:
-                corner(m, 1 - x, 1 - y, 1).wait_recv()
-            to_core(m, c).start()
-
-        where_mine(u, act)
-
-    def finish(u):
-        m, h = units[u]
-        for d in PAIRS[h]:
-            to_twin(m, d).wait_send()
-        for copy in first_moves(u) + second_moves(u):
-            copy.wait_send()
-        for zz in range(ZN):
-
-            @pl.when(z == zz)
-            def _():
-                for d in PAIRS[h]:
-                    if d < zz:
-                        to_down(m, d).wait_send()
-                    if d > zz:
-                        to_up(m, d).wait_send()
-
-        def act(m):
-            to_core(m, 1 - c).wait_recv()
-            share_across(m).wait_send()
-            share_beside(m).wait_send()
-            corner(m, 1 - x, y, 0).wait_send()
-            if ks[m] > 1:
-                corner(m, x, 1 - y, 1).wait_send()
-            to_core(m, c).wait_send()
-
-        where_mine(u, act)
-
-    count = len(units)
-
-    def at(step, u, *s):
-        if 0 <= u < count:
-            step(u, *s)
-
-    for u in range(count):
-        m, h = units[u]
-        for d in PAIRS[h]:
-            to_twin(m, d).start()
-            load(m, d).start()
-    for t in range(count + 8):
-        at(with_twin, t)
-        at(with_first, t - 1)
-        at(with_second, t - 2)
-        for s in range(ZN):
-            at(line_step, t - 2 - s, s)
-        at(corner_step, t - 6)
-        at(core_step, t - 7)
-    for u in range(count):
-        finish(u)
-
-
-def reduce_pieces(grads, ks):
-    m_count = len(grads)
+    )(*ins, *grads)
+    return outs[:n], outs[n:]
+
+
+def reduce_kernel(grads, spec):
+    extra = len(grads)
 
     def body(*refs):
-        groups = [refs[i * m_count : (i + 1) * m_count] for i in range(8)]
-        reduce_body(ks, *groups, *refs[8 * m_count :])
-
-    def buffers(rows):
-        return [pltpu.VMEM((ZN, rows * k) + g.shape[2:], g.dtype) for g, k in zip(grads, ks)]
+        place = neighbours()
+        greet(*[place[j] for j in (2, 3, 0, 4, 5, 6)], None, *place[7:])
+        comm, finish = take_reduce(place, spec, refs[:extra], refs[extra : 2 * extra], refs[2 * extra :])
+        spread_steps((), comm, finish)
 
     return pl.pallas_call(
         body,
-        out_shape=[jax.ShapeDtypeStruct((8 * k,) + g.shape[2:], g.dtype) for g, k in zip(grads, ks)],
-        in_specs=[pl.BlockSpec(memory_space=pl.ANY)] * m_count,
-        out_specs=[pl.BlockSpec(memory_space=pl.ANY)] * m_count,
-        scratch_shapes=buffers(4)
-        + buffers(4)
-        + buffers(2)
-        + buffers(1)
-        + buffers(1)
-        + buffers(1)
-        + [
-            pltpu.SemaphoreType.DMA((m_count, ZN)),
-            pltpu.SemaphoreType.DMA((m_count,)),
-            pltpu.SemaphoreType.DMA((m_count, 27)),
-            pltpu.SemaphoreType.DMA((m_count, 27)),
-        ],
-        compiler_params=pltpu.CompilerParams(
-            collective_id=1, has_side_effects=True, vmem_limit_bytes=60 << 20
-        ),
+        out_shape=[shaped(g.shape[1:], g.dtype) for g in grads],
+        in_specs=anywhere(extra),
+        out_specs=anywhere(extra),
+        scratch_shapes=reduce_scratch([(k, grads[m].shape[2:]) for m, _, k in spec]),
+        compiler_params=pltpu.CompilerParams(collective_id=2, has_side_effects=True, vmem_limit_bytes=VMEM_LIMIT),
         name="reduce_grads",
     )(*grads)
 
 
 VECTORS = (0, 1, 3, 4, 6, 7, 8, 12, 10)
 MATRICES = (2, 5, 9, 11)
-WIDE = 13312
-
-
-def reduce_layer(gradients):
-    low = [g.astype(jnp.bfloat16) for g in gradients]
-    mats = [low[i].reshape(ZN, -1, 16, low[i].shape[1]) for i in MATRICES]
-    rest = [jnp.swapaxes(g[:, g.shape[1] // 8 * 8 :], 1, 2).reshape(ZN, 16, -1) for g in mats]
-    vectors = jnp.concatenate([low[i].reshape(ZN, -1) for i in VECTORS], axis=1)
-    width = WIDE - sum(r.shape[2] for r in rest)
-    vectors = jnp.pad(vectors, ((0, 0), (0, 16 * width - vectors.shape[1]))).reshape(ZN, 16, width)
-    wide = jnp.concatenate(rest + [vectors], axis=2)
-    wide = jnp.swapaxes(wide.reshape(ZN, 16, 8, WIDE // 8), 1, 2)
-    ks = [g.shape[1] // 8 for g in mats] + [1]
-    sums = reduce_pieces(mats + [wide], ks)
-    tail = jnp.swapaxes(sums[-1], 0, 1).reshape(16, WIDE)
-    result = [None] * 13
-    col = 0
-    for at, i in enumerate(MATRICES):
-        columns = low[i].shape[1]
-        n = mats[at].shape[1] % 8
-        extra = jnp.swapaxes(tail[:, col : col + n * columns].reshape(16, n, columns), 0, 1)
-        col += n * columns
-        result[i] = jnp.concatenate([sums[at].reshape(-1, columns), extra.reshape(-1, columns)], axis=0)
-    flat = tail[:, col:].reshape(-1)
-    col = 0
-    for i in VECTORS:
-        n = low[i].shape[0] // ZN
-        result[i] = flat[col : col + n]
-        col += n
-    return tuple(r.astype(jnp.float32) for r in result)
-
-
-def swap_cores(rows):
-    return lax.ppermute(rows, "rep", [(0, 1), (1, 0), (2, 3), (3, 2)])
+
+
+def wide_of(weight_grads, vector_grads):
+    width = weight_grads[0].shape[3]
+
+    def pieces(g):
+        left = g[:, g.shape[1] // 8 * 8 :]
+        parts = left.shape[3] // width
+        return jnp.swapaxes(left.reshape(ZN, left.shape[1], 16, parts, width), 2, 3).reshape(ZN, -1, 16, width)
+
+    vectors = jnp.concatenate([g.reshape(ZN, -1) for g in vector_grads], axis=1).astype(jnp.bfloat16)
+    vectors = vectors.reshape(ZN, 1, -1, width)
+    vectors = jnp.pad(vectors, ((0, 0), (0, 0), (0, 16 - vectors.shape[2]), (0, 0)))
+    wide = jnp.concatenate([pieces(g) for g in weight_grads] + [vectors], axis=1)
+    return jnp.pad(wide, ((0, 0), (0, -wide.shape[1] % 8), (0, 0), (0, 0)))
+
+
+def rows_from(sums, wide, at):
+    n, _, columns = sums.shape
+    left = n % 8
+    parts = columns // wide.shape[2]
+    tail = wide[at : at + left * parts].reshape(left, parts, 16, -1)
+    tail = jnp.swapaxes(tail, 1, 2).reshape(left * 16, columns)
+    rows = jnp.concatenate([sums[: n - left].reshape(-1, columns), tail], axis=0)
+    return rows.astype(jnp.float32), at + left * parts
 
 
 def on_cores(tokens, segments, grad_out, *params):
@@ -1695,39 +1937,45 @@
     fulls, result, grads_here, mask, vector_rows, saved = forward(
         tokens[0], grad_out[0], segments, vectors, weights
     )
+    fulls = [full.reshape(layers, -1, 16, full.shape[4]) for full in fulls]
     result = from_cores(result)[None]
     grad = grads_here.astype(jnp.float32)
     reduced = [None] * layers
+    waiting, waiting_spec = [], []
     for layer in reversed(range(layers)):
         kept = saved[layer]
         attn_gain, mlp_gain = vector_rows[layer, 0:1], vector_rows[layer, 5:6]
-        g_mlp, g_pre, g_middle, g_branch, g_attended, gb_down, gb_up, gm_gain, gm_shift, gb_out = mlp_back(
-            layer, grad, kept["middle"], kept["slope"], mlp_gain, weights, fulls
+        (g_middle, g_branch, g_att, dw_up, dw_down, gb_down, gb_up, gm_gain, gm_shift, gb_out), sums = mlp_kernel(
+            layer, grad, kept, mlp_gain, fulls, waiting, waiting_spec
         )
-        g_q, g_own, g_other = attend_back(
-            kept["q"], g_attended, kept["attended"], kept["lse"], mask, kept["keys"], kept["values"]
+        if waiting:
+            reduced[layer + 1].extend(sums)
+        dw_down = dw_down.reshape(ZN, -1, 16, width)
+        down_spec = spec_of([dw_down.shape], 2)
+        (grad, dw_qkv, dw_out, gb_q, gb_v, ga_gain, ga_shift), sums = attend_kernel(
+            layer, kept, mask, g_att, g_middle, g_branch, attn_gain, fulls, [dw_down], down_spec
         )
-        g_got = swap_cores(g_other)
-        grad, g_proj, gb_q, gb_v, ga_gain, ga_shift = project_back(
-            layer, kept["x"], g_middle, g_q, g_own, g_got, attn_gain, weights[0], fulls[0]
-        )
-        gradients = (
-            ga_gain[0],
-            ga_shift[0],
-            inner_rows(kept["normed_attn"], g_proj),
-            gb_q[0],
-            gb_v[0],
-            inner_rows(kept["attended"], g_branch),
-            gb_out[0],
-            gm_gain[0],
-            gm_shift[0],
-            inner_rows(kept["normed_mlp"], g_pre),
-            gb_up[0],
-            inner_rows(kept["activated"], g_mlp),
-            gb_down[0],
-        )
-        reduced[layer] = reduce_layer(gradients)
-    stacked = tuple((jnp.stack([entry[member] for entry in reduced]) for member in range(13)))
+        reduced[layer] = list(sums)
+        waiting = [dw.reshape(ZN, -1, 16, dw.shape[2]) for dw in (dw_up, dw_out, dw_qkv)]
+        vector_grads = (ga_gain, ga_shift, gb_q, gb_v, gb_out, gm_gain, gm_shift, gb_down, gb_up)
+        waiting.append(wide_of([dw_down] + waiting, vector_grads))
+        waiting_spec = spec_of([w.shape for w in waiting], 2)
+    reduced[0].extend(reduce_kernel(waiting, waiting_spec))
+    final = []
+    for layer in range(layers):
+        down, up, out, qkv, wide = reduced[layer]
+        entry = [None] * 13
+        at = 0
+        for i, sums in ((11, down), (9, up), (5, out), (2, qkv)):
+            entry[i], at = rows_from(sums, wide, at)
+        flat = wide[at].reshape(-1).astype(jnp.float32)
+        at = 0
+        for i in VECTORS:
+            n = params[i].shape[1]
+            entry[i] = flat[at : at + n]
+            at += n
+        final.append(entry)
+    stacked = tuple((jnp.stack([entry[member] for entry in final]) for member in range(13)))
     return (result, from_cores(grad.astype(jnp.bfloat16))[None]) + stacked
 
 

time: 1060 us -> 904 us (0.85)
  matrix products: 53.8 us -> 0 us
  local copies, waits for them, and re-layouts: 111 us -> 60.9 us
  Pallas kernels: 820 us -> 790 us
    dot_general x8 -> x0, matrix products: 53.8 us -> none  [inner_rows(): lax.dot_general(left, right, (((0,), (0,)), ((), ())), preferred_element_...]
    pallas_call x8 -> x5, Pallas kernels: 541 us -> 511 us  [the longest x2 195 us: mlp_kernel(): pl.pallas_call(body, out_shape=work_out + [shaped(g.shape[1:], low) for g...]
    convert_element_type x20 -> x4, local copies, waits for them, and re-layouts: 30 us -> 1.64 us  [the longest x2 1.43 us: on_cores(): flat = wide[at].reshape(-1).astype(jnp.float32)]
    another operation x13 -> x30, other arithmetic: 25.7 us -> 20.5 us  [the longest x13 18.5 us: on_cores(): jnp.stack([entry[member] for entry in final])]
  transfers between devices with their start and end apart: 6 -> 4, of which waited for: 0 -> 0; matrix products, arithmetic and copies ran while one was open for 12% -> 8% of each run, Pallas kernels for 6% -> 57%
where the time goes in v3:
time: 904 us; the launch traced here: 890 us
  Pallas kernels  790 us (87%)
  local copies, waits for them, and re-layouts  60.9 us (7%)
  other arithmetic  31.2 us (3%)
    pallas_call x1, Pallas kernels, forward(): pl.pallas_call(forward_body, out_shape=out_shape, in_specs=anywhere(4 + l...  279 us
    pallas_call x2, Pallas kernels, mlp_kernel(): pl.pallas_call(body, out_shape=work_out + [shaped(g.shape[1:], low) for g...  195 us
    pallas_call x2, Pallas kernels, attend_kernel(): pl.pallas_call(body, out_shape=work_out + [shaped(g.shape[1:], low) for g...  187 us
    pallas_call x1, Pallas kernels, reduce_kernel(): pl.pallas_call(body, out_shape=[shaped(g.shape[1:], g.dtype) for g in gra...  128 us
    another operation x13, other arithmetic, on_cores(): jnp.stack([entry[member] for entry in final])  18.5 us
  transfers between devices with their start and end apart: 4, of which 0 were waited for; matrix products, arithmetic and copies ran while one was open for 8% of the time, Pallas kernels for 57%

profile of v3, /device:TPU:25, one launch (start us, length us, event | category | flops | bytes accessed | tf_op | source)
XLA Modules:
  0.0 889.8 jit_solution(3859640648760942692)
XLA Ops:
  7.7 2.4 copy.53
  11.5 279.1 %forward.1 = (bf16[2,4,17,16,3264]{4,3,2,1,0:T(8,128)(2,1)}, bf16[2,4,17,16,1088]{4,3,2,1,0:T(8,128)(2,1)}, bf16[2,4,17,16,4352]{4,3,2,1,0:T(8,128)(2,1)}, bf16[...) custom-call(bf16[512,1088]{1,0:T(8,128)(2,1)} %bitcast.104, ...), custom_call_target="tpu_custom_call" | custom-call | tf_op jit(solution)/shard_map/forward/pallas_call | solution.py:1172
  294.8 2.0 collective-permute-start
  298.2 1.6 convert_element_type.112.refs_0_
  299.8 61.3 %mlp_back.2 = (f32[512,1088]{1,0:T(8,128)}, bf16[512,1088]{1,0:T(8,128)(2,1)}, bf16[512,1088]{1,0:T(8,128)(2,1)}, bf16[68,16,4352]{2,1,0:T(8,128)(2,1)}, bf16[27...) custom-call(f32[512,1088]{1,0:T(8,128)} %convert_element_type.112.re, ...), custom_call_target="tpu_custom_call" | custom-call | tf_op jit(solution)/shard_map/mlp_back/pallas_call | solution.py:1833
  362.2 96.6 %attend_back.2 = (f32[512,1088]{1,0:T(8,128)}, bf16[68,16,3264]{2,1,0:T(8,128)(2,1)}, bf16[68,16,1088]{2,1,0:T(8,128)(2,1)}, f32[1,1088]{1,0:T(1,128)}, f32[1,10...) custom-call(bf16[512,1088]{1,0:T(8,128)(2,1)} %get-tuple-element.91.refs_0_, ...), custom_call_target="tpu_custom_call" | custom-call | tf_op jit(solution)/shard_map/attend_back/pallas_call | solution.py:1870
  465.2 1.6 pad.20.refs_12_
  466.8 134.0 %mlp_back.3 = (f32[512,1088]{1,0:T(8,128)}, bf16[512,1088]{1,0:T(8,128)(2,1)}, bf16[512,1088]{1,0:T(8,128)(2,1)}, bf16[68,16,4352]{2,1,0:T(8,128)(2,1)}, bf16[27...) custom-call(f32[512,1088]{1,0:T(8,128)} %get-tuple-element.113.refs_, ...), custom_call_target="tpu_custom_call" | custom-call | tf_op jit(solution)/shard_map/mlp_back/pallas_call | solution.py:1833
  600.8 90.9 %attend_back.3 = (f32[512,1088]{1,0:T(8,128)}, bf16[68,16,3264]{2,1,0:T(8,128)(2,1)}, bf16[68,16,1088]{2,1,0:T(8,128)(2,1)}, f32[1,1088]{1,0:T(1,128)}, f32[1,10...) custom-call(bf16[512,1088]{1,0:T(8,128)(2,1)} %get-tuple-element.90.refs_0_, ...), custom_call_target="tpu_custom_call" | custom-call | tf_op jit(solution)/shard_map/attend_back/pallas_call | solution.py:1870
  691.7 1.8 convert_element_type.114
  695.9 2.9 collective-permute-start.2
  709.6 1.6 pad.22.refs_3_
  711.2 128.5 %reduce_grads.1 = (bf16[17,16,4352]{2,1,0:T(8,128)(2,1)}, bf16[17,16,1088]{2,1,0:T(8,128)(2,1)}, bf16[17,16,3264]{2,1,0:T(8,128)(2,1)}, bf16[16,16,1088]{2,1,0:T(8,128)(2,1)}) custom-call(bf16[4,17,16,4352]{3,2,1,0:T(8,128)(2,1)} %bitcast.89, bf16[4,17,16,1088]{3,2,1,0:T(8,128)(2,1)} %bitcast.110, bf16[4,17,16,3264]{3,2,1,0:T(8,128)(2,1)} %bitcast.97, ...), custom_call_target="tpu_custom_call" | custom-call | tf_op jit(solution)/shard_map/reduce_grads/pallas_call | solution.py:1891
  839.7 1.6 slice_bitcast_fusion.3
  850.6 1.6 slice.238
  860.0 1.6 slice.240
  861.7 1.5 copy-done.2
  864.2 1.5 copy-done
  869.4 1.6 maximum_convert_fusion.3
  871.0 3.3 maximum_convert_fusion.2
  874.3 4.1 maximum_convert_fusion.1
  878.4 4.2 maximum_convert_fusion
  885.0 2.1 maximum_bitcast_fusion
  887.1 2.3 maximum_bitcast_fusion.1
  (211 shorter events, 58.7 us)
Async XLA Ops:
  0.6 9.4 %copy-start.5 = (bf16[1,512,1088]{1,2,0:T(8,128)(2,1)S(1)}, bf16[1,512,1088]{1,2,0:T(8,128)(2,1)}, u32[]{:S(2)}) copy-start(bf16[1,512,1088]{1,2,0:T(8,128)(2,1)} %param.18) | copy-start | bytes 3342340
  290.6 7.7 copy-start.4
  293.0 591.9 %collective-permute-start.1 = (bf16[256,1088]{0,1:T(8,128)(2,1)}, bf16[256,1088]{0,1:T(8,128)(2,1)S(1)}, u32[]{:S(2)}, u32[]{:S(2)}) collective-permute-start(bf16[256,1088]{0,1:T(8,128)(2,1)} %copy.64), channel_id=1, source_target_pairs={{1,0},{17,1},{3,2},{19,3},{0,16},{16,17},{2,18},{18,19},{5,4},{21,... | collective-permute-start | bytes 1671176 | tf_op jit(solution)/shard_map/ppermute | solution.py:387
  294.8 590.2 %collective-permute-start = (bf16[256,1088]{0,1:T(8,128)(2,1)}, bf16[256,1088]{0,1:T(8,128)(2,1)}, u32[]{:S(2)}, u32[]{:S(2)}) collective-permute-start(bf16[256,1088]{0,1:T(8,128)(2,1)} %copy.63), channel_id=1, source_target_pairs={{0,0},{16,1},{2,2},{18,3},{1,16},{17,17},{3,18},{19,19},{4,4},{20,... | collective-permute-start | bytes 1671176 | tf_op jit(solution)/shard_map/ppermute | solution.py:386
  362.2 98.5 %copy-start.40 = (f32[1,1088]{1,0:T(1,128)S(1)}, f32[1,1088]{1,0:T(1,128)}, u32[]{:S(2)}) copy-start(f32[1,1088]{1,0:T(1,128)} %get-tuple-element.126) | copy-start | bytes 13060
  362.2 98.5 %copy-start.41 = (f32[1,1088]{1,0:T(1,128)S(1)}, f32[1,1088]{1,0:T(1,128)}, u32[]{:S(2)}) copy-start(f32[1,1088]{1,0:T(1,128)} %get-tuple-element.125) | copy-start | bytes 13060
  362.2 98.7 %copy-start.38 = (f32[1,1088]{1,0:T(1,128)S(1)}, f32[1,1088]{1,0:T(1,128)}, u32[]{:S(2)}) copy-start(f32[1,1088]{1,0:T(1,128)} %get-tuple-element.128) | copy-start | bytes 13060
  362.2 98.7 %copy-start.39 = (f32[1,1088]{1,0:T(1,128)S(1)}, f32[1,1088]{1,0:T(1,128)}, u32[]{:S(2)}) copy-start(f32[1,1088]{1,0:T(1,128)} %get-tuple-element.127) | copy-start | bytes 13060
  362.2 99.0 %copy-start.15 = (f32[1,4352]{1,0:T(1,128)S(1)}, f32[1,4352]{1,0:T(1,128)}, u32[]{:S(2)}) copy-start(f32[1,4352]{1,0:T(1,128)} %get-tuple-element.129) | copy-start | bytes 52228
  693.6 11.0 %copy-start.37 = (f32[1,1088]{1,0:T(1,128)S(1)}, f32[1,1088]{1,0:T(1,128)}, u32[]{:S(2)}) copy-start(f32[1,1088]{1,0:T(1,128)} %get-tuple-element.144) | copy-start | bytes 13060
  693.6 11.1 %copy-start.36 = (f32[1,1088]{1,0:T(1,128)S(1)}, f32[1,1088]{1,0:T(1,128)}, u32[]{:S(2)}) copy-start(f32[1,1088]{1,0:T(1,128)} %get-tuple-element.145) | copy-start | bytes 13060
  693.6 11.2 %copy-start.35 = (f32[1,1088]{1,0:T(1,128)S(1)}, f32[1,1088]{1,0:T(1,128)}, u32[]{:S(2)}) copy-start(f32[1,1088]{1,0:T(1,128)} %get-tuple-element.146) | copy-start | bytes 13060
  693.6 11.3 %copy-start.34 = (f32[1,1088]{1,0:T(1,128)S(1)}, f32[1,1088]{1,0:T(1,128)}, u32[]{:S(2)}) copy-start(f32[1,1088]{1,0:T(1,128)} %get-tuple-element.147) | copy-start | bytes 13060
  693.6 11.5 %copy-start.33 = (f32[1,1088]{1,0:T(1,128)S(1)}, f32[1,1088]{1,0:T(1,128)}, u32[]{:S(2)}) copy-start(f32[1,1088]{1,0:T(1,128)} %get-tuple-element.148) | copy-start | bytes 13060
  693.6 11.6 %copy-start.32 = (f32[1,1088]{1,0:T(1,128)S(1)}, f32[1,1088]{1,0:T(1,128)}, u32[]{:S(2)}) copy-start(f32[1,1088]{1,0:T(1,128)} %get-tuple-element.149) | copy-start | bytes 13060
  693.6 11.7 %copy-start.31 = (f32[1,1088]{1,0:T(1,128)S(1)}, f32[1,1088]{1,0:T(1,128)}, u32[]{:S(2)}) copy-start(f32[1,1088]{1,0:T(1,128)} %get-tuple-element.150) | copy-start | bytes 13060
  693.6 11.8 %copy-start.30 = (f32[1,1088]{1,0:T(1,128)S(1)}, f32[1,1088]{1,0:T(1,128)}, u32[]{:S(2)}) copy-start(f32[1,1088]{1,0:T(1,128)} %get-tuple-element.151) | copy-start | bytes 13060
  693.6 11.9 %copy-start.14 = (f32[1,4352]{1,0:T(1,128)S(1)}, f32[1,4352]{1,0:T(1,128)}, u32[]{:S(2)}) copy-start(f32[1,4352]{1,0:T(1,128)} %get-tuple-element.152) | copy-start | bytes 52228
  694.7 192.4 %collective-permute-start.3 = (bf16[256,1088]{0,1:T(8,128)(2,1)}, bf16[256,1088]{0,1:T(8,128)(2,1)}, u32[]{:S(2)}, u32[]{:S(2)}) collective-permute-start(bf16[256,1088]{0,1:T(8,128)(2,1)} %copy.67), channel_id=1, source_target_pairs={{1,0},{17,1},{3,2},{19,3},{0,16},{16,17},{2,18},{18,19},{5,4},{21,... | collective-permute-start | bytes 1671176 | tf_op jit(solution)/shard_map/ppermute | solution.py:387
  695.9 191.2 %collective-permute-start.2 = (bf16[256,1088]{0,1:T(8,128)(2,1)}, bf16[256,1088]{0,1:T(8,128)(2,1)}, u32[]{:S(2)}, u32[]{:S(2)}) collective-permute-start(bf16[256,1088]{0,1:T(8,128)(2,1)} %copy.66), channel_id=1, source_target_pairs={{0,0},{16,1},{2,2},{18,3},{1,16},{17,17},{3,18},{19,19},{4,4},{20,... | collective-permute-start | bytes 1671176 | tf_op jit(solution)/shard_map/ppermute | solution.py:386
  839.7 10.8 %copy-start.7 = (bf16[17,16,1088]{2,1,0:T(8,128)(2,1)S(1)}, bf16[17,16,1088]{2,1,0:T(8,128)(2,1)}, u32[]{:S(2)}) copy-start(bf16[17,16,1088]{2,1,0:T(8,128)(2,1)} %get-tuple-element.158) | copy-start | bytes 1775620
  878.4 5.4 copy-start.23
  878.4 6.0 copy-start.12
  878.4 6.0 copy-start.13
  (22 other events, 56.8 us)

commit v4 on v3

--- a/solution.py
+++ b/solution.py
@@ -376,20 +376,6 @@
         return lax.psum_scatter(rows, "seq", scatter_dimension=0, tiled=True)
 
 
-def from_cores(rows):
-    half = rows.shape[0] // 2
-    spots = [(x, y, c) for x in range(2) for y in range(2) for c in range(2)]
-    first = [(c * 4 + y * 2 + x, x * 4 + y * 2 + c) for x, y, c in spots]
-    second = [(c * 4 + y * 2 + 1 - x, x * 4 + y * 2 + c) for x, y, c in spots]
-    return jnp.concatenate(
-        [
-            lax.ppermute(rows[:half], ("seq", "rep"), first),
-            lax.ppermute(rows[half:], ("seq", "rep"), second),
-        ],
-        axis=0,
-    )
-
-
 ZN = 4
 
 
@@ -437,6 +423,7 @@
 PACE = 2
 REDUCE_PACE = 6
 SKEW = 2
+AHEAD = 6
 
 
 NT = (((1,), (1,)), ((), ()))
@@ -1200,8 +1187,8 @@
 
 
 class Group:
-    def __init__(self, grad, out, base, k):
-        self.grad, self.out, self.base, self.k = grad, out, base, k
+    def __init__(self, grad, out, base, k, ready):
+        self.grad, self.out, self.base, self.k, self.ready = grad, out, base, k, ready
 
 
 def reduce_steps(place, groups, acc, stage, first_in, second_in, line_in, line_extra, load_sem, store_sem, send_sem, recv_sem):
@@ -1392,12 +1379,12 @@
     stages += [((2 + ZN) * SKEW, corner_step), ((3 + ZN) * SKEW, core_step)]
 
     def steps():
-        for g, d in units:
-            to_twin(g, d).start()
-            if ORDER.index(d) < 2:
-                load(g, d).start()
-        yield True
         for t in range(count + stages[-1][0]):
+            for g, d in units[AHEAD + t - 1 : AHEAD + t] if t else units[:AHEAD]:
+                yield groups[g].ready
+                to_twin(g, d).start()
+                if ORDER.index(d) < 2:
+                    load(g, d).start()
             for delay, step in stages:
                 if 0 <= t - delay < count:
                     step(*units[t - delay])
@@ -1416,29 +1403,85 @@
     return buffers + [dma((n, 2)), dma((n,)), dma((n, 26)), dma((n, 26))]
 
 
-def take_reduce(place, spec, grads, outs, refs):
+def take_reduce(place, spec, grads, outs, refs, made_here=()):
     n = len(spec)
-    groups = [Group(grads[m], outs[m], base, k) for m, base, k in spec]
+    groups = [Group(grads[m], outs[m], base, k, m if m in made_here else True) for m, base, k in spec]
     lists = [refs[i * n : (i + 1) * n] for i in range(6)]
     return reduce_steps(place, groups, *lists, *refs[6 * n : 6 * n + 4])
 
 
 def spread_steps(work, comm, finish):
-    for _ in work:
-        if comm is not None:
-            advance(comm, REDUCE_PACE)
-    if comm is not None:
-        for _ in comm:
-            pass
-        finish()
-
-
-def spec_of(shapes, split):
+    done = {True}
+    blocked = None
+    for made in work:
+        done.add(made)
+        for _ in range(REDUCE_PACE):
+            if blocked is not None and blocked not in done:
+                break
+            blocked = next(comm, True)
+    for _ in comm:
+        pass
+    finish()
+
+
+def ship_moves(place, source, target, local_sem, send_sem, recv_sem):
+    x, y, z, c, across, beside, twin, up, down = place
+    diag = (1 - x, z, y * 2 + (1 - c))
+    top, low = pl.ds(0, BLOCK), pl.ds(BLOCK, BLOCK)
+
+    def move(i, rows, device):
+        return pltpu.make_async_remote_copy(
+            src_ref=source.at[rows], dst_ref=target.at[rows], send_sem=send_sem.at[i], recv_sem=recv_sem.at[i],
+            device_id=device, device_id_type=MESH,
+        )
+
+    stay = pltpu.make_async_copy(source.at[top], target.at[top], local_sem.at[0])
+
+    def start():
+        @pl.when(c == x)
+        def _():
+            stay.start()
+            move(1, low, across).start()
+
+        @pl.when(c != x)
+        def _():
+            move(0, top, diag).start()
+            move(1, low, twin).start()
+
+    def wait():
+        @pl.when(c == x)
+        def _():
+            stay.wait()
+            move(1, low, across).wait()
+
+        @pl.when(c != x)
+        def _():
+            move(0, top, diag).wait()
+            move(1, low, twin).wait()
+
+    return start, wait
+
+
+def ship_scratch():
+    dma = pltpu.SemaphoreType.DMA
+    return [dma((1,)), dma((2,)), dma((2,))]
+
+
+def meet(ship):
+    place = neighbours()
+    x, y, z, c, across, beside, twin, up, down = place
+    diag = (1 - x, z, y * 2 + (1 - c)) if ship else None
+    greet(z, c, x, across, beside, twin, diag, up, down)
+    return place
+
+
+def spec_of(shapes):
     spec = []
     for m, shape in enumerate(shapes):
         k = shape[1] // 8
-        for base in range(0, k // min(k, split)):
-            spec.append((m, base * 8 * min(k, split), min(k, split)))
+        split = min(k, 1 if shape[3] > 2048 else 2)
+        for base in range(0, k, split):
+            spec.append((m, base * 8, split))
     return spec
 
 
@@ -1485,7 +1528,7 @@
     return [(at, min(at + size, high)) for at in range(low, high, size)]
 
 
-def mlp_work(layer, ins, outs, refs):
+def mlp_work(layer, ins, outs, refs, made_down):
     grad_in, middle_in, slope_in, normed_in, activated_in, gain, w_out, w_up, w_down = ins
     g_middle_out, g_branch_out, g_attended_out, dw_up, dw_down, gb_down, gb_up, g_gain, g_shift, gb_out = outs
     (
@@ -1496,7 +1539,7 @@
     ff = slope.shape[1]
     loads = [
         pltpu.make_async_copy(a, b, load_sem.at[i])
-        for i, (a, b) in enumerate(((grad_in, grad), (middle_in, middle), (slope_in, slope), (normed_in, nm)))
+        for i, (a, b) in enumerate(((grad_in, g_mlp if grad_in.dtype == jnp.bfloat16 else grad), (middle_in, middle), (slope_in, slope), (normed_in, nm)))
     ]
     begin(loads)
 
@@ -1518,10 +1561,66 @@
     down_begin()
     up_begin()
     loads[0].wait()
-    g_mlp[...] = grad[...].astype(jnp.bfloat16)
+    if grad_in.dtype == jnp.bfloat16:
+        grad[...] = g_mlp[...].astype(jnp.float32)
+    else:
+        g_mlp[...] = grad[...].astype(jnp.bfloat16)
     gb_down[...] = jnp.sum(g_mlp[...].astype(jnp.float32), axis=0, keepdims=True)
+    yield
+    tile = act_tiles.shape[2]
+
+    def bring_act(i, n):
+        return pltpu.make_async_copy(
+            activated_in.at[:, pl.ds(pl.multiple_of(i * tile, tile), n)], act_tiles.at[i % 2, :, pl.ds(0, n)], act_sem.at[i % 2]
+        )
+
+    def send_down(i, n):
+        return pltpu.make_async_copy(
+            down_tiles.at[i % 2, pl.ds(0, n // 16)], dw_down.at[pl.ds(i * (tile // 16), n // 16)], down_sem.at[i % 2]
+        )
+
+    whole, left = ff // tile, ff % tile
+    bring_act(0, tile).start()
+
+    def down_grad(i, carry):
+        bring_act(i, tile).wait()
+
+        @pl.when(i + 1 < whole)
+        def _():
+            bring_act(i + 1, tile).start()
+
+        if left:
+
+            @pl.when(i + 1 == whole)
+            def _():
+                bring_act(whole, left).start()
+
+        @pl.when(i >= 2)
+        def _():
+            send_down(i - 2, tile).wait()
+
+        out = dot_tn(act_tiles[i % 2], g_mlp[...]).astype(jnp.bfloat16)
+        down_tiles[i % 2] = out.reshape(tile // 16, 16, width)
+        send_down(i, tile).start()
+        return carry
+
+    for low, high in each(0, whole, 4):
+        lax.fori_loop(low, high, down_grad, 0)
+        yield
+    if left:
+        bring_act(whole, left).wait()
+        send_down(whole - 2, tile).wait()
+        out = dot_tn(act_tiles[whole % 2, :, :left], g_mlp[...]).astype(jnp.bfloat16)
+        down_tiles[whole % 2, : left // 16] = out.reshape(left // 16, 16, width)
+        send_down(whole, left).start()
+    send_down(whole - 1, tile).wait()
+    if left:
+        send_down(whole, left).wait()
+    else:
+        send_down(whole - 2, tile).wait()
+    yield made_down
+
     loads[2].wait()
-    yield
     for low, high in each(0, down_n, 4):
         down_run(low, high)
         yield
@@ -1542,54 +1641,6 @@
     turned[...] = nm[...].T
     yield
 
-    tile = act_tiles.shape[2]
-
-    def bring_act(i, n):
-        return pltpu.make_async_copy(
-            activated_in.at[:, pl.ds(pl.multiple_of(i * tile, tile), n)], act_tiles.at[i % 2, :, pl.ds(0, n)], act_sem.at[i % 2]
-        )
-
-    def send_down(i, n):
-        return pltpu.make_async_copy(
-            down_tiles.at[i % 2, pl.ds(0, n // 16)], dw_down.at[pl.ds(i * (tile // 16), n // 16)], down_sem.at[i % 2]
-        )
-
-    whole, left = ff // tile, ff % tile
-    bring_act(0, tile).start()
-
-    def down_grad(i, carry):
-        bring_act(i, tile).wait()
-
-        @pl.when(i + 1 < whole)
-        def _():
-            bring_act(i + 1, tile).start()
-
-        if left:
-
-            @pl.when(i + 1 == whole)
-            def _():
-                bring_act(whole, left).start()
-
-        @pl.when(i >= 2)
-        def _():
-            send_down(i - 2, tile).wait()
-
-        out = dot_tn(act_tiles[i % 2], g_mlp[...]).astype(jnp.bfloat16)
-        down_tiles[i % 2] = out.reshape(tile // 16, 16, width)
-        send_down(i, tile).start()
-        return carry
-
-    for low, high in each(0, whole, 2):
-        lax.fori_loop(low, high, down_grad, 0)
-        yield
-    if left:
-        bring_act(whole, left).wait()
-        send_down(whole - 2, tile).wait()
-        out = dot_tn(act_tiles[whole % 2, :, :left], g_mlp[...]).astype(jnp.bfloat16)
-        down_tiles[whole % 2, : left // 16] = out.reshape(left // 16, 16, width)
-        send_down(whole, left).start()
-        yield
-
     step = up_tiles.shape[3]
 
     def send_up(i):
@@ -1612,11 +1663,6 @@
         yield
     send_up(ff // step - 2).wait()
     send_up(ff // step - 1).wait()
-    send_down(whole - 1, tile).wait()
-    if left:
-        send_down(whole, left).wait()
-    else:
-        send_down(whole - 2, tile).wait()
     end(saves)
 
 
@@ -1757,7 +1803,11 @@
         yield
     end(loads[6:])
     norm_back(xs, g_norm, grad, gain[...], grad, g_gain, g_shift)
-    save = pltpu.make_async_copy(grad, g_x_out, load_sem.at[1])
+    if g_x_out.dtype == jnp.bfloat16:
+        g_att[...] = grad[...].astype(jnp.bfloat16)
+        save = pltpu.make_async_copy(g_att, g_x_out, load_sem.at[1])
+    else:
+        save = pltpu.make_async_copy(grad, g_x_out, load_sem.at[1])
     save.start()
     after.wait()
     turned[...] = q[...].T
@@ -1801,11 +1851,12 @@
     ]
 
 
-def mlp_kernel(layer, grad, kept, gain, fulls, grads, spec):
+def mlp_kernel(layer, grad, kept, gain, fulls, grads):
     rows, width = grad.shape
     ff = kept["slope"].shape[1]
     low = jnp.bfloat16
     ins = [grad, kept["middle"], kept["slope"], kept["normed_mlp"], kept["activated"], gain, fulls[1], fulls[2], fulls[3]]
+    down_shape = (ZN, ff // 16 // ZN, 16, width)
     work_out = [
         shaped((rows, width)),
         shaped((rows, width), low),
@@ -1815,34 +1866,45 @@
     ] + [shaped((1, n)) for n in (width, ff, width, width, width)]
     work_refs = mlp_refs(rows, width, ff)
     n, extra = len(work_out), len(grads)
-    in_specs = anywhere(5) + whole(1) + anywhere(3 + extra)
+    shapes = [g.shape for g in grads] + [down_shape]
+    spec = spec_of(shapes)
 
     def body(*refs):
         i = len(ins) + extra
-        outs, more = refs[i : i + n], refs[i + n : i + n + extra]
-        rest = refs[i + n + extra :]
-        comm = finish = None
-        if extra:
-            place = neighbours()
-            greet(*[place[j] for j in (2, 3, 0, 4, 5, 6)], None, *place[7:])
-            comm, finish = take_reduce(place, spec, refs[len(ins) : i], more, rest[len(work_refs) :])
-        work = mlp_work(layer, refs[: len(ins)], outs, rest[: len(work_refs)])
+        outs, more = refs[i : i + n], refs[i + n : i + n + extra + 1]
+        rest = refs[i + n + extra + 1 :]
+        place = meet(False)
+        down_rows = Rows(outs[4], down_shape[1])
+        comm, finish = take_reduce(
+            place, spec, list(refs[len(ins) : i]) + [down_rows], more, rest[len(work_refs) :], (extra,)
+        )
+        work = mlp_work(layer, refs[: len(ins)], outs, rest[: len(work_refs)], extra)
         spread_steps(work, comm, finish)
 
-    settings = dict(collective_id=100 + layer, has_side_effects=True) if extra else {}
     outs = pl.pallas_call(
         body,
-        out_shape=work_out + [shaped(g.shape[1:], low) for g in grads],
-        in_specs=in_specs,
-        out_specs=anywhere(5) + whole(5) + anywhere(extra),
-        scratch_shapes=work_refs + (reduce_scratch([(k, grads[m].shape[2:]) for m, _, k in spec]) if extra else []),
-        compiler_params=pltpu.CompilerParams(vmem_limit_bytes=VMEM_LIMIT, **settings),
+        out_shape=work_out + [shaped(shape[1:], low) for shape in shapes],
+        in_specs=anywhere(5) + whole(1) + anywhere(3 + extra),
+        out_specs=anywhere(5) + whole(5) + anywhere(extra + 1),
+        scratch_shapes=work_refs + reduce_scratch([(k, shapes[m][2:]) for m, _, k in spec]),
+        compiler_params=pltpu.CompilerParams(
+            collective_id=100 + layer, has_side_effects=True, vmem_limit_bytes=VMEM_LIMIT
+        ),
         name="mlp_back",
     )(*ins, *grads)
     return outs[:n], outs[n:]
 
 
-def attend_kernel(layer, kept, mask, g_att, g_middle, g_branch, gain, fulls, grads, spec):
+class Rows:
+    def __init__(self, ref, n):
+        self.ref, self.n, self.at = ref, n, self
+
+    def __getitem__(self, where):
+        d, chunks = where
+        return self.ref.at[pl.ds(d * self.n + chunks.start, chunks.size)]
+
+
+def attend_kernel(layer, kept, mask, g_att, g_middle, g_branch, gain, fulls, grads, ship):
     rows, width = g_middle.shape
     low = jnp.bfloat16
     ins = [
@@ -1850,53 +1912,135 @@
         kept["normed_attn"], kept["attended"], g_branch, gain, fulls[0],
     ]
     work_out = [
-        shaped((rows, width)),
+        shaped((rows, width), jnp.float32 if layer else low),
         shaped((width // 16, 16, 3 * width), low),
         shaped((width // 16, 16, width), low),
     ] + [shaped((1, width))] * 4
     work_refs = attend_refs(rows, width)
-    n, extra = len(work_out), len(grads)
+    ships = [ship] if ship is not None else []
+    n, extra, k = len(work_out), len(grads), len(ships)
+    spec = spec_of([g.shape for g in grads])
+    buffers = reduce_scratch([(depth, grads[m].shape[2:]) for m, _, depth in spec])
 
     def body(*refs):
-        i = len(ins) + extra
+        i = len(ins) + extra + k
         outs, more = refs[i : i + n], refs[i + n : i + n + extra]
-        rest = refs[i + n + extra :]
-        place = neighbours()
-        greet(*[place[j] for j in (2, 3, 0, 4, 5, 6)], None, *place[7:])
-        comm, finish = take_reduce(place, spec, refs[len(ins) : i], more, rest[len(work_refs) :])
+        rest = refs[i + n + extra + k :]
+        place = meet(bool(k))
+        if k:
+            start, wait = ship_moves(place, refs[i - 1], refs[i + n + extra], *rest[-3:])
+            start()
+        comm, finish = take_reduce(place, spec, refs[len(ins) : i - k], more, rest[len(work_refs) :])
         work = attend_work(layer, place, refs[: len(ins)], outs, rest[: len(work_refs)])
         spread_steps(work, comm, finish)
+        if k:
+            wait()
 
     outs = pl.pallas_call(
         body,
-        out_shape=work_out + [shaped(g.shape[1:], low) for g in grads],
-        in_specs=anywhere(11) + whole(1) + anywhere(1 + extra),
-        out_specs=anywhere(3) + whole(4) + anywhere(extra),
-        scratch_shapes=work_refs + reduce_scratch([(k, grads[m].shape[2:]) for m, _, k in spec]),
-        compiler_params=pltpu.CompilerParams(collective_id=200 + layer, has_side_effects=True, vmem_limit_bytes=VMEM_LIMIT),
+        out_shape=work_out + [shaped(g.shape[1:], low) for g in grads] + [shaped(v.shape, v.dtype) for v in ships],
+        in_specs=anywhere(11) + whole(1) + anywhere(1 + extra + k),
+        out_specs=anywhere(3) + whole(4) + anywhere(extra + k),
+        scratch_shapes=work_refs + buffers + (ship_scratch() if k else []),
+        compiler_params=pltpu.CompilerParams(
+            collective_id=200 + layer, has_side_effects=True, vmem_limit_bytes=VMEM_LIMIT
+        ),
         name="attend_back",
-    )(*ins, *grads)
-    return outs[:n], outs[n:]
-
-
-def reduce_kernel(grads, spec):
+    )(*ins, *grads, *ships)
+    return outs[:n], outs[n : n + extra], outs[n + extra :]
+
+
+def reduce_kernel(grads, ship):
     extra = len(grads)
+    spec = spec_of([g.shape for g in grads])
 
     def body(*refs):
-        place = neighbours()
-        greet(*[place[j] for j in (2, 3, 0, 4, 5, 6)], None, *place[7:])
-        comm, finish = take_reduce(place, spec, refs[:extra], refs[extra : 2 * extra], refs[2 * extra :])
+        place = meet(True)
+        rest = refs[2 * extra + 2 :]
+        start, wait = ship_moves(place, refs[extra], refs[2 * extra + 1], *rest[-3:])
+        start()
+        comm, finish = take_reduce(place, spec, refs[:extra], refs[extra + 1 : 2 * extra + 1], rest)
         spread_steps((), comm, finish)
-
-    return pl.pallas_call(
+        wait()
+
+    outs = pl.pallas_call(
         body,
-        out_shape=[shaped(g.shape[1:], g.dtype) for g in grads],
-        in_specs=anywhere(extra),
-        out_specs=anywhere(extra),
-        scratch_shapes=reduce_scratch([(k, grads[m].shape[2:]) for m, _, k in spec]),
+        out_shape=[shaped(g.shape[1:], g.dtype) for g in grads] + [shaped(ship.shape, ship.dtype)],
+        in_specs=anywhere(extra + 1),
+        out_specs=anywhere(extra + 1),
+        scratch_shapes=reduce_scratch([(k, grads[m].shape[2:]) for m, _, k in spec]) + ship_scratch(),
         compiler_params=pltpu.CompilerParams(collective_id=2, has_side_effects=True, vmem_limit_bytes=VMEM_LIMIT),
         name="reduce_grads",
-    )(*grads)
+    )(*grads, ship)
+    return outs[:extra], outs[extra]
+
+
+def assemble_body(layers, *refs):
+    ins = [refs[layer * 5 : (layer + 1) * 5] for layer in range(layers)]
+    outs = refs[layers * 5 : layers * 5 + 4]
+    vectors = refs[layers * 5 + 4 : layers * 5 + 13]
+    rest = refs[layers * 5 + 13 :]
+    held, made = rest[:5], rest[5:9]
+    in_sem, out_sem = rest[9:]
+    width = held[4].shape[3]
+    loads, stores = [], []
+    for layer in range(layers):
+        loads.append(
+            [pltpu.make_async_copy(ins[layer][m], held[m].at[layer], in_sem.at[layer, m]) for m in range(5)]
+        )
+        begin(loads[-1])
+    for layer in range(layers):
+        loads[layer][4].wait()
+        piece = 0
+        for m in range(4):
+            loads[layer][m].wait()
+            n = held[m].shape[1]
+            whole_n = n // 8 * 8
+            if layer:
+                stores[m].wait()
+
+            def widen(i, carry, m=m):
+                made[m][i] = held[m][layer, i].astype(jnp.float32)
+                return carry
+
+            lax.fori_loop(0, whole_n, widen, 0)
+            for i in range(whole_n, n):
+                for at in range(0, held[m].shape[3], width):
+                    made[m][i, :, at : at + width] = held[4][layer, piece].astype(jnp.float32)
+                    piece += 1
+            copy = pltpu.make_async_copy(made[m], outs[m].at[layer], out_sem.at[layer, m])
+            copy.start()
+            if layer:
+                stores[m] = copy
+            else:
+                stores.append(copy)
+        flat = held[4][layer, piece].astype(jnp.float32)
+        at = 0
+        for ref in vectors:
+            n = ref.shape[1]
+            ref[layer : layer + 1, :] = flat[at // width : at // width + 1, at % width : at % width + n]
+            at += n
+    for copy in stores:
+        copy.wait()
+
+
+def assemble(reduced, vector_sizes):
+    layers = len(reduced)
+    low = jnp.bfloat16
+    shapes = [r.shape for r in reduced[0]]
+    dma = pltpu.SemaphoreType.DMA
+    outs = pl.pallas_call(
+        functools.partial(assemble_body, layers),
+        out_shape=[shaped((layers,) + shape) for shape in shapes[:4]] + [shaped((layers, n)) for n in vector_sizes],
+        in_specs=anywhere(5 * layers),
+        out_specs=anywhere(4) + whole(len(vector_sizes)),
+        scratch_shapes=[pltpu.VMEM((layers,) + shape, low) for shape in shapes]
+        + [pltpu.VMEM(shape, jnp.float32) for shape in shapes[:4]]
+        + [dma((layers, 5)), dma((layers, 4))],
+        compiler_params=params(),
+        name="assemble",
+    )(*[r for entry in reduced for r in entry])
+    return outs[:4], outs[4:]
 
 
 VECTORS = (0, 1, 3, 4, 6, 7, 8, 12, 10)
@@ -1916,16 +2060,6 @@
     vectors = jnp.pad(vectors, ((0, 0), (0, 0), (0, 16 - vectors.shape[2]), (0, 0)))
     wide = jnp.concatenate([pieces(g) for g in weight_grads] + [vectors], axis=1)
     return jnp.pad(wide, ((0, 0), (0, -wide.shape[1] % 8), (0, 0), (0, 0)))
-
-
-def rows_from(sums, wide, at):
-    n, _, columns = sums.shape
-    left = n % 8
-    parts = columns // wide.shape[2]
-    tail = wide[at : at + left * parts].reshape(left, parts, 16, -1)
-    tail = jnp.swapaxes(tail, 1, 2).reshape(left * 16, columns)
-    rows = jnp.concatenate([sums[: n - left].reshape(-1, columns), tail], axis=0)
-    return rows.astype(jnp.float32), at + left * parts
 
 
 def on_cores(tokens, segments, grad_out, *params):
@@ -1934,49 +2068,39 @@
     weights = [params[i].reshape(layers, -1, 16, params[i].shape[2]) for i in MATRICES]
     vectors = jnp.concatenate([params[i].reshape(layers, -1, params[0].shape[1]) for i in VECTORS], axis=1)
     vectors = jnp.pad(vectors, ((0, 0), (0, 16 - vectors.shape[1]), (0, 0)))[:, None]
-    fulls, result, grads_here, mask, vector_rows, saved = forward(
-        tokens[0], grad_out[0], segments, vectors, weights
-    )
+    fulls, result, grad, mask, vector_rows, saved = forward(tokens[0], grad_out[0], segments, vectors, weights)
     fulls = [full.reshape(layers, -1, 16, full.shape[4]) for full in fulls]
-    result = from_cores(result)[None]
-    grad = grads_here.astype(jnp.float32)
     reduced = [None] * layers
-    waiting, waiting_spec = [], []
+    waiting = []
+    ship = result
     for layer in reversed(range(layers)):
         kept = saved[layer]
         attn_gain, mlp_gain = vector_rows[layer, 0:1], vector_rows[layer, 5:6]
         (g_middle, g_branch, g_att, dw_up, dw_down, gb_down, gb_up, gm_gain, gm_shift, gb_out), sums = mlp_kernel(
-            layer, grad, kept, mlp_gain, fulls, waiting, waiting_spec
+            layer, grad, kept, mlp_gain, fulls, waiting
         )
         if waiting:
-            reduced[layer + 1].extend(sums)
-        dw_down = dw_down.reshape(ZN, -1, 16, width)
-        down_spec = spec_of([dw_down.shape], 2)
-        (grad, dw_qkv, dw_out, gb_q, gb_v, ga_gain, ga_shift), sums = attend_kernel(
-            layer, kept, mask, g_att, g_middle, g_branch, attn_gain, fulls, [dw_down], down_spec
+            reduced[layer + 1].extend(sums[:-1])
+        reduced[layer] = [sums[-1]]
+        dw_up, dw_down = dw_up.reshape(ZN, -1, 16, dw_up.shape[2]), dw_down.reshape(ZN, -1, 16, width)
+        (grad, dw_qkv, dw_out, gb_q, gb_v, ga_gain, ga_shift), sums, shipped = attend_kernel(
+            layer, kept, mask, g_att, g_middle, g_branch, attn_gain, fulls, [dw_up], ship
         )
-        reduced[layer] = list(sums)
-        waiting = [dw.reshape(ZN, -1, 16, dw.shape[2]) for dw in (dw_up, dw_out, dw_qkv)]
+        if ship is not None:
+            result, ship = shipped[0], None
+        reduced[layer].extend(sums)
+        waiting = [dw.reshape(ZN, -1, 16, dw.shape[2]) for dw in (dw_out, dw_qkv)]
         vector_grads = (ga_gain, ga_shift, gb_q, gb_v, gb_out, gm_gain, gm_shift, gb_down, gb_up)
-        waiting.append(wide_of([dw_down] + waiting, vector_grads))
-        waiting_spec = spec_of([w.shape for w in waiting], 2)
-    reduced[0].extend(reduce_kernel(waiting, waiting_spec))
-    final = []
-    for layer in range(layers):
-        down, up, out, qkv, wide = reduced[layer]
-        entry = [None] * 13
-        at = 0
-        for i, sums in ((11, down), (9, up), (5, out), (2, qkv)):
-            entry[i], at = rows_from(sums, wide, at)
-        flat = wide[at].reshape(-1).astype(jnp.float32)
-        at = 0
-        for i in VECTORS:
-            n = params[i].shape[1]
-            entry[i] = flat[at : at + n]
-            at += n
-        final.append(entry)
-    stacked = tuple((jnp.stack([entry[member] for entry in final]) for member in range(13)))
-    return (result, from_cores(grad.astype(jnp.bfloat16))[None]) + stacked
+        waiting.append(wide_of([dw_down, dw_up] + waiting, vector_grads))
+    sums, grad = reduce_kernel(waiting, grad)
+    reduced[0].extend(sums)
+    (down, up, out, qkv), vector_outs = assemble(reduced, [params[i].shape[1] for i in VECTORS])
+    final = [None] * 13
+    for i, value in ((11, down), (9, up), (5, out), (2, qkv)):
+        final[i] = value.reshape(layers, -1, value.shape[3])
+    for i, value in zip(VECTORS, vector_outs):
+        final[i] = value
+    return (result[None], grad[None], *final)
 
 
 def on_device(

time: 904 us -> 858 us (0.949)
  local copies, waits for them, and re-layouts: 60.9 us -> 23.6 us
  other arithmetic: 31.2 us -> 6.23 us
  Pallas kernels: 790 us -> 813 us
    pallas_call x2 -> x3, Pallas kernels: 195 us -> 268 us  [the longest x2 253 us: mlp_kernel(): pl.pallas_call(body, out_shape=work_out + [shaped(shape[1:], low) for sha...]
    pallas_call x1, Pallas kernels: 128 us -> 94.8 us  [reduce_kernel(): pl.pallas_call(body, out_shape=[shaped(g.shape[1:], g.dtype) for g in gra...]
    pallas_call x2, Pallas kernels: 187 us -> 172 us  [attend_kernel(): pl.pallas_call(body, out_shape=work_out + [shaped(g.shape[1:], low) for g...]
    slice x19 -> x1, local copies, waits for them, and re-layouts: 16 us -> 1.29 us  [the longest x8 5.09 us: rows_from(): rows = jnp.concatenate([sums[:n - left].reshape(-1, columns), tail], axis=0)]
    another operation x30 -> x17, other arithmetic: 20.5 us -> 6.18 us  [the longest x13 18.5 us: on_cores(): jnp.stack([entry[member] for entry in final])]
    another operation x21 -> x3, local copies, waits for them, and re-layouts: 12.7 us -> 3.64 us  [the longest x18 9.11 us: on_cores(): jnp.stack([entry[member] for entry in final])]
  transfers between devices with their start and end apart: 4 -> 0, of which waited for: 0 -> 0; matrix products, arithmetic and copies ran while one was open for 8% -> 0% of each run, Pallas kernels for 57% -> 0%
where the time goes in v4:
time: 858 us; the launch traced here: 844 us
  Pallas kernels  813 us (95%)
  local copies, waits for them, and re-layouts  23.6 us (3%)
    pallas_call x1, Pallas kernels, forward(): pl.pallas_call(forward_body, out_shape=out_shape, in_specs=anywhere(4 + l...  279 us
    pallas_call x2, Pallas kernels, mlp_kernel(): pl.pallas_call(body, out_shape=work_out + [shaped(shape[1:], low) for sha...  253 us
    pallas_call x2, Pallas kernels, attend_kernel(): pl.pallas_call(body, out_shape=work_out + [shaped(g.shape[1:], low) for g...  172 us
    pallas_call x1, Pallas kernels, reduce_kernel(): pl.pallas_call(body, out_shape=[shaped(g.shape[1:], g.dtype) for g in gra...  94.8 us

profile of v4, /device:TPU:25, one launch (start us, length us, event | category | flops | bytes accessed | tf_op | source)
XLA Modules:
  0.0 844.4 jit_solution(3084050780142345087)
XLA Ops:
  0.7 2.4 copy.35
  3.2 1.4 copy.36
  5.6 279.1 %forward.1 = (bf16[2,4,17,16,3264]{4,3,2,1,0:T(8,128)(2,1)}, bf16[2,4,17,16,1088]{4,3,2,1,0:T(8,128)(2,1)}, bf16[2,4,17,16,4352]{4,3,2,1,0:T(8,128)(2,1)}, bf16[...) custom-call(bf16[512,1088]{1,0:T(8,128)(2,1)} %bitcast.66, ...), custom_call_target="tpu_custom_call" | custom-call | tf_op jit(solution)/shard_map/forward/pallas_call | solution.py:1159
  284.7 1.5 slice_bitcast_fusion
  286.2 96.5 %mlp_back.2 = (f32[512,1088]{1,0:T(8,128)}, bf16[512,1088]{1,0:T(8,128)(2,1)}, bf16[512,1088]{1,0:T(8,128)(2,1)}, bf16[68,16,4352]{2,1,0:T(8,128)(2,1)}, bf16[27...) custom-call(bf16[512,1088]{1,0:T(8,128)(2,1)} %get-tuple-element.105, ...), custom_call_target="tpu_custom_call" | custom-call | tf_op jit(solution)/shard_map/mlp_back/pallas_call | solution.py:1884
  382.7 0.7 convert_reduce_fusion.10
  383.6 0.7 convert_reduce_fusion.12
  384.5 87.9 %attend_back.2 = (f32[512,1088]{1,0:T(8,128)}, bf16[68,16,3264]{2,1,0:T(8,128)(2,1)}, bf16[68,16,1088]{2,1,0:T(8,128)(2,1)}, f32[1,1088]{1,0:T(1,128)}, f32[1,10...) custom-call(bf16[512,1088]{1,0:T(8,128)(2,1)} %get-tuple-element.104, ...), custom_call_target="tpu_custom_call" | custom-call | tf_op jit(solution)/shard_map/attend_back/pallas_call | solution.py:1939
  474.7 1.2 fusion.3
  475.9 1.3 fusion.1
  477.2 1.1 slice_dynamic-update-slice_fusion.1
  478.4 0.9 slice_dynamic-update-slice_fusion.3
  479.4 1.6 pad.20.refs_11_
  481.0 156.2 %mlp_back.3 = (f32[512,1088]{1,0:T(8,128)}, bf16[512,1088]{1,0:T(8,128)(2,1)}, bf16[512,1088]{1,0:T(8,128)(2,1)}, bf16[68,16,4352]{2,1,0:T(8,128)(2,1)}, bf16[27...) custom-call(f32[512,1088]{1,0:T(8,128)} %get-tuple-element.129.refs_, ...), custom_call_target="tpu_custom_call" | custom-call | tf_op jit(solution)/shard_map/mlp_back/pallas_call | solution.py:1884
  637.3 83.6 %attend_back.3 = (bf16[512,1088]{1,0:T(8,128)(2,1)}, bf16[68,16,3264]{2,1,0:T(8,128)(2,1)}, bf16[68,16,1088]{2,1,0:T(8,128)(2,1)}, f32[1,1088]{1,0:T(1,128)}, f3...) custom-call(bf16[512,1088]{1,0:T(8,128)(2,1)} %get-tuple-element.128.refs_0_, ...), custom_call_target="tpu_custom_call" | custom-call | tf_op jit(solution)/shard_map/attend_back/pallas_call | solution.py:1939
  725.1 1.2 fusion.2
  726.3 1.3 fusion
  727.6 1.1 slice_dynamic-update-slice_fusion
  728.8 0.9 slice_dynamic-update-slice_fusion.2
  729.9 1.6 pad.22.refs_2_
  731.4 94.8 %reduce_grads.1 = (bf16[17,16,1088]{2,1,0:T(8,128)(2,1)}, bf16[17,16,3264]{2,1,0:T(8,128)(2,1)}, bf16[16,16,1088]{2,1,0:T(8,128)(2,1)}, bf16[512,1088]{1,0:T(8,128)(2,1)}) custom-call(bf16[4,17,16,1088]{3,2,1,0:T(8,128)(2,1)} %bitcast.72, bf16[4,17,16,3264]{3,2,1,0:T(8,128)(2,1)} %bitcast.61, bf16[4,16,16,1088]{3,2,1,0:T(8,128)(2,1)} %pad.22.refs_2_, ...), custom_call_target="tpu_custom_call" | custom-call | tf_op jit(solution)/shard_map/reduce_grads/pallas_call | solution.py:1966
  826.3 14.9 %assemble.1 = (f32[2,68,16,1088]{3,2,1,0:T(8,128)}, f32[2,17,16,4352]{3,2,1,0:T(8,128)}, f32[2,17,16,1088]{3,2,1,0:T(8,128)}, f32[2,17,16,3264]{3,2,1,0:T(8,128)...) custom-call(bf16[68,16,1088]{2,1,0:T(8,128)(2,1)} %get-tuple-element, ...), custom_call_target="tpu_custom_call" | custom-call | tf_op jit(solution)/shard_map/assemble/pallas_call | solution.py:2032
  841.2 1.4 copy.48
  842.6 1.4 copy.47
  (91 shorter events, 8.0 us)
Async XLA Ops:
  0.6 2.5 copy-start.2
  0.7 3.9 copy-start.9
  0.7 4.0 copy-start.10
  0.7 4.0 copy-start.11
  0.7 4.0 copy-start.12
  0.7 4.1 copy-start.13
  0.7 4.1 copy-start.14
  0.7 4.1 copy-start.15
  0.7 4.1 copy-start.16
  0.7 4.1 copy-start.17
  384.5 89.7 %copy-start.3 = (f32[1,4352]{1,0:T(1,128)S(1)}, f32[1,4352]{1,0:T(1,128)}, u32[]{:S(2)}) copy-start(f32[1,4352]{1,0:T(1,128)} %get-tuple-element.145) | copy-start | bytes 52228
  637.2 86.9 %copy-start.4 = (f32[1,4352]{1,0:T(1,128)S(1)}, f32[1,4352]{1,0:T(1,128)}, u32[]{:S(2)}) copy-start(f32[1,4352]{1,0:T(1,128)} %get-tuple-element.167) | copy-start | bytes 52228
  637.2 87.1 %copy-start.8 = (f32[1,1088]{1,0:T(1,128)S(1)}, f32[1,1088]{1,0:T(1,128)}, u32[]{:S(2)}) copy-start(f32[1,1088]{1,0:T(1,128)} %get-tuple-element.163) | copy-start | bytes 13060
  637.3 87.2 %copy-start.7 = (f32[1,1088]{1,0:T(1,128)S(1)}, f32[1,1088]{1,0:T(1,128)}, u32[]{:S(2)}) copy-start(f32[1,1088]{1,0:T(1,128)} %get-tuple-element.164) | copy-start | bytes 13060
  637.3 87.3 %copy-start.6 = (f32[1,1088]{1,0:T(1,128)S(1)}, f32[1,1088]{1,0:T(1,128)}, u32[]{:S(2)}) copy-start(f32[1,1088]{1,0:T(1,128)} %get-tuple-element.165) | copy-start | bytes 13060
  637.3 87.4 %copy-start.5 = (f32[1,1088]{1,0:T(1,128)S(1)}, f32[1,1088]{1,0:T(1,128)}, u32[]{:S(2)}) copy-start(f32[1,1088]{1,0:T(1,128)} %get-tuple-element.166) | copy-start | bytes 13060
  826.3 14.9 %copy-start.1 = (bf16[512,1088]{1,0:T(8,128)(2,1)S(1)}, bf16[512,1088]{1,0:T(8,128)(2,1)}, u32[]{:S(2)}) copy-start(bf16[512,1088]{1,0:T(8,128)(2,1)} %get-tuple-element.169) | copy-start | bytes 3342340
  841.2 1.4 copy-start

commit v5 on v4

--- a/solution.py
+++ b/solution.py
@@ -420,7 +420,10 @@
 GELU_B = 0.044715
 QUERY_SCALE = 1.0 / math.sqrt(HEAD_DIM)
 HEAD_ROWS = 24
-PACE = 2
+PACE = 4
+LEAD = 3
+GAP = 2
+TILE = 512
 REDUCE_PACE = 6
 SKEW = 2
 AHEAD = 6
@@ -534,19 +537,36 @@
             return
 
 
+def gather_units(layers, shapes):
+    units = []
+    for layer in range(layers):
+        for m, shape in enumerate(shapes):
+            n = shape[1] // 8
+            k = min(n, 1 if shape[3] > 2048 else 2)
+            bases = range(0, max(n, 1), max(k, 1))
+            units += [(layer, m, base * 8, k, base + k >= n) for base in bases]
+    return units
+
+
 def weight_moves(ins, outs, send_sem, recv_sem, place):
     x, y, z, c, across, beside, twin, up, down = place
     m_count = len(ins) - 1
     layers = ins[0].shape[0]
-    units = [(layer, m) for layer in range(layers) for m in range(m_count + 1)]
+    units = gather_units(layers, [w.shape for w in ins])
     index = {unit: i for i, unit in enumerate(units)}
 
     def depth(u):
-        return ins[u[1]].shape[1] // 8
+        return u[3]
+
+    def corners(u, px, py, act):
+        k = depth(u)
+        for half, device, kind in ((0, beside, GD1), (1, across, GD2)):
+            if k > 1 or half == index[u] % 2:
+                act(half if k > 1 else None, device, kind)
 
     def owned(u, px, py, half=None):
         k = depth(u)
-        base = (c * 4 + px * 2 + py) * k
+        base = u[2] + (c * 4 + px * 2 + py) * k
         if half is None:
             return pl.ds(base, k)
         return pl.ds(base + half * (k // 2), k // 2)
@@ -556,7 +576,7 @@
         return pl.ds(n // 8 * 8, n % 8)
 
     def slab(u, core):
-        return pl.ds(core * 4 * depth(u), 4 * depth(u))
+        return pl.ds(u[2] + core * 4 * depth(u), 4 * depth(u))
 
     def move(u, zz, rows, device, kind, source=None, send_kind=None):
         target = outs[u[1]].at[u[0], zz, rows]
@@ -575,7 +595,8 @@
         def along(device, first):
             if depth(u):
                 act(move(u, z, owned(u, x, y), device, ZA, source.at[owned(u, x, y)], first))
-            act(move(u, z, rest(u), device, ZR, source.at[rest(u)], first + 1))
+            if u[4]:
+                act(move(u, z, rest(u), device, ZR, source.at[rest(u)], first + 1))
 
         @pl.when(z < ZN - 1)
         def _():
@@ -598,7 +619,8 @@
         def along(device):
             if depth(u):
                 act(move(u, zz, owned(u, x, y), device, ZA))
-            act(move(u, zz, rest(u), device, ZR))
+            if u[4]:
+                act(move(u, zz, rest(u), device, ZR))
 
         if d == 0:
 
@@ -616,7 +638,8 @@
         def act(zz, d):
             if depth(u):
                 move(u, zz, owned(u, x, y), across, ZA).wait_recv()
-            move(u, zz, rest(u), across, ZR).wait_recv()
+            if u[4]:
+                move(u, zz, rest(u), across, ZR).wait_recv()
             onward(u, zz, d, lambda copy: copy.start())
             if depth(u):
                 move(u, zz, owned(u, x, y), across, GX).start()
@@ -626,24 +649,32 @@
 
     def plane_step(u, s):
         def act(zz, d):
+            def pass_on(half, device, kind):
+                if kind == GD1:
+                    move(u, zz, owned(u, 1 - x, y, half), device, kind).start()
+                else:
+                    move(u, zz, owned(u, x, 1 - y, half), device, kind).start()
+
             move(u, zz, owned(u, 1 - x, y), across, GX).wait_recv()
-            move(u, zz, owned(u, 1 - x, y, 0), beside, GD1).start()
             move(u, zz, owned(u, x, 1 - y), beside, GY).wait_recv()
-            move(u, zz, owned(u, x, 1 - y, 1), across, GD2).start()
+            corners(u, x, y, pass_on)
 
         both(s, act)
 
     def corner_step(u, s):
         def act(zz, d):
-            move(u, zz, owned(u, 1 - x, 1 - y, 0), beside, GD1).wait_recv()
-            move(u, zz, owned(u, 1 - x, 1 - y, 1), across, GD2).wait_recv()
+            corners(
+                u, x, y, lambda half, device, kind: move(u, zz, owned(u, 1 - x, 1 - y, half), device, kind).wait_recv()
+            )
             move(u, zz, slab(u, c), twin, GC).start()
 
         both(s, act)
 
-    def arrive(u):
-        for s in range(1, ZN):
-            both(s, lambda zz, d: move(u, zz, slab(u, 1 - c), twin, GC).wait_recv())
+    def arrive(whole):
+        for u in units:
+            if u[:2] == whole:
+                for s in range(1, ZN):
+                    both(s, lambda zz, d: move(u, zz, slab(u, 1 - c), twin, GC).wait_recv())
 
     def finish(u):
         own_sends(u, lambda copy: copy.wait_send())
@@ -654,38 +685,50 @@
                 if depth(u):
                     move(u, zz, owned(u, x, y), across, GX).wait_send()
                     move(u, zz, owned(u, x, y), beside, GY).wait_send()
-                    move(u, zz, owned(u, 1 - x, y, 0), beside, GD1).wait_send()
-                    move(u, zz, owned(u, x, 1 - y, 1), across, GD2).wait_send()
+                    corners(
+                        u, x, y, lambda half, device, kind: move(u, zz, owned(u, x, y, half), device, kind).wait_send()
+                    )
                     move(u, zz, slab(u, c), twin, GC).wait_send()
 
             both(s, act)
 
     matrices = [u for u in units if u[1] < m_count]
     vectors = [u for u in units if u[1] == m_count]
-    count = len(matrices)
-
     def steps():
-        for u in vectors + matrices[:2]:
+        first = [u for u in matrices if u[:2] == matrices[0][:2]]
+        rest_units = [u for u in matrices if u not in first]
+        count = len(rest_units)
+        for u in vectors + first:
             own_sends(u, lambda copy: copy.start())
         for s in range(1, ZN):
             for u in vectors:
                 line_step(u, s)
         yield ("vectors",)
-        for t in range(count + 4):
-            if t + 2 < count:
-                own_sends(matrices[t + 2], lambda copy: copy.start())
-            for s in range(1, ZN):
-                if 0 <= t + 1 - s < count:
-                    line_step(matrices[t + 1 - s], s)
-                    yield ("line",)
-            for s in range(1, ZN):
-                if 0 <= t - s < count:
-                    plane_step(matrices[t - s], s)
-                    yield ("plane",)
-            for s in range(1, ZN):
-                if 0 <= t - 1 - s < count:
-                    corner_step(matrices[t - 1 - s], s)
-                    yield ("here", matrices[t - 1 - s]) if s == ZN - 1 else ("corner",)
+        for s in range(1, ZN):
+            for u in first:
+                line_step(u, s)
+                yield ("line",)
+            if s == 1:
+                for u in rest_units[:LEAD]:
+                    own_sends(u, lambda copy: copy.start())
+        early = [[(plane_step, u, s) for u in first] for s in range(1, ZN)]
+        early += [[(corner_step, u, s) for u in first] for s in range(1, ZN)]
+        for t in range(count + 4 * GAP):
+            if t + LEAD < count:
+                own_sends(rest_units[t + LEAD], lambda copy: copy.start())
+            for step, u, s in sum(early[t * 2 : t * 2 + 2], []):
+                step(u, s)
+                here = step is corner_step and s == ZN - 1 and u[4]
+                yield ("here", u[:2]) if here else ("early",)
+            for delay, step in ((0, line_step), (1, plane_step), (2, corner_step)):
+                for s in range(1, ZN):
+                    i = t - (s - 1 + delay) * GAP
+                    if not 0 <= i < count:
+                        continue
+                    u = rest_units[i]
+                    step(u, s)
+                    here = step is corner_step and s == ZN - 1 and u[4]
+                    yield ("here", u[:2]) if here else ("step",)
 
     return steps, arrive, lambda: [finish(u) for u in units]
 
@@ -970,15 +1013,17 @@
 
     def compute(layer):
         if layer == 0:
-            make_rows(0)
-            make_rows(1)
+            for i in range(layers):
+                make_rows(i)
+                yield
             for i in range(layers):
                 copy = pltpu.make_async_copy(rows.at[i], rows_out.at[i], save_sem.at[i, len(SAVED) + 1])
                 copy.start()
                 pending.append(copy)
+            make_mask()
+            yield
             wait_in(tok_copies)
             xs[...] = tok[...].astype(jnp.float32)
-            make_mask()
         else:
             settle()
         save(layer, "x", xs)
@@ -990,7 +1035,7 @@
 
         for low_at in range(0, total, 4 * BLOCK):
             high_at = min(low_at + 4 * BLOCK, total)
-            tiles_between(low_at, high_at, BLOCK, lambda start, size: project_tile(layer, start, size))
+            tiles_between(low_at, high_at, TILE, lambda start, size: project_tile(layer, start, size))
             yield
         done_with.add((layer, 0))
         q[...] = slope[:, :width]
@@ -1049,7 +1094,7 @@
 
         ff = wu.shape[2]
         for low_at in range(0, ff, 6 * BLOCK):
-            tiles_between(low_at, min(low_at + 6 * BLOCK, ff), BLOCK, up_step)
+            tiles_between(low_at, min(low_at + 6 * BLOCK, ff), TILE, up_step)
             yield
         done_with.add((layer, 2))
         save(layer, "slope", slope)
@@ -1098,7 +1143,7 @@
     low = jnp.bfloat16
     layers = vectors.shape[0]
     ff = weights[2].shape[3]
-    units = layers * (len(weights) + 1)
+    units = len(gather_units(layers, [w.shape for w in weights] + [vectors.shape]))
     shapes = dict(
         x=((rows, width), jnp.float32),
         normed_attn=((rows, width), low),

time: 858 us -> 833 us (0.971)
  Pallas kernels: 813 us -> 796 us
    pallas_call x1, Pallas kernels: 279 us -> 259 us  [forward(): pl.pallas_call(forward_body, out_shape=out_shape, in_specs=anywhere(4 + l...]
where the time goes in v5:
time: 833 us; the launch traced here: 827 us
  Pallas kernels  796 us (96%)
  local copies, waits for them, and re-layouts  23.6 us (3%)
    pallas_call x1, Pallas kernels, forward(): pl.pallas_call(forward_body, out_shape=out_shape, in_specs=anywhere(4 + l...  259 us
    pallas_call x2, Pallas kernels, mlp_kernel(): pl.pallas_call(body, out_shape=work_out + [shaped(shape[1:], low) for sha...  255 us
    pallas_call x2, Pallas kernels, attend_kernel(): pl.pallas_call(body, out_shape=work_out + [shaped(g.shape[1:], low) for g...  172 us
    pallas_call x1, Pallas kernels, reduce_kernel(): pl.pallas_call(body, out_shape=[shaped(g.shape[1:], g.dtype) for g in gra...  94.7 us

profile of v5, /device:TPU:25, one launch (start us, length us, event | category | flops | bytes accessed | tf_op | source)
XLA Modules:
  0.0 826.9 jit_solution(11424770426668854241)
XLA Ops:
  0.7 2.4 copy.35
  3.2 1.4 copy.36
  5.6 259.4 %forward.1 = (bf16[2,4,17,16,3264]{4,3,2,1,0:T(8,128)(2,1)}, bf16[2,4,17,16,1088]{4,3,2,1,0:T(8,128)(2,1)}, bf16[2,4,17,16,4352]{4,3,2,1,0:T(8,128)(2,1)}, bf16[...) custom-call(bf16[512,1088]{1,0:T(8,128)(2,1)} %bitcast.66, ...), custom_call_target="tpu_custom_call" | custom-call | tf_op jit(solution)/shard_map/forward/pallas_call | solution.py:1204
  265.0 1.5 slice_bitcast_fusion
  266.5 98.6 %mlp_back.2 = (f32[512,1088]{1,0:T(8,128)}, bf16[512,1088]{1,0:T(8,128)(2,1)}, bf16[512,1088]{1,0:T(8,128)(2,1)}, bf16[68,16,4352]{2,1,0:T(8,128)(2,1)}, bf16[27...) custom-call(bf16[512,1088]{1,0:T(8,128)(2,1)} %get-tuple-element.105, ...), custom_call_target="tpu_custom_call" | custom-call | tf_op jit(solution)/shard_map/mlp_back/pallas_call | solution.py:1929
  365.1 0.7 convert_reduce_fusion.10
  366.0 0.7 convert_reduce_fusion.12
  366.9 87.9 %attend_back.2 = (f32[512,1088]{1,0:T(8,128)}, bf16[68,16,3264]{2,1,0:T(8,128)(2,1)}, bf16[68,16,1088]{2,1,0:T(8,128)(2,1)}, f32[1,1088]{1,0:T(1,128)}, f32[1,10...) custom-call(bf16[512,1088]{1,0:T(8,128)(2,1)} %get-tuple-element.104, ...), custom_call_target="tpu_custom_call" | custom-call | tf_op jit(solution)/shard_map/attend_back/pallas_call | solution.py:1984
  457.1 1.2 fusion.3
  458.3 1.3 fusion.1
  459.6 1.1 slice_dynamic-update-slice_fusion.1
  460.8 0.9 slice_dynamic-update-slice_fusion.3
  461.9 1.6 pad.20.refs_11_
  463.4 156.2 %mlp_back.3 = (f32[512,1088]{1,0:T(8,128)}, bf16[512,1088]{1,0:T(8,128)(2,1)}, bf16[512,1088]{1,0:T(8,128)(2,1)}, bf16[68,16,4352]{2,1,0:T(8,128)(2,1)}, bf16[27...) custom-call(f32[512,1088]{1,0:T(8,128)} %get-tuple-element.129.refs_, ...), custom_call_target="tpu_custom_call" | custom-call | tf_op jit(solution)/shard_map/mlp_back/pallas_call | solution.py:1929
  619.7 83.9 %attend_back.3 = (bf16[512,1088]{1,0:T(8,128)(2,1)}, bf16[68,16,3264]{2,1,0:T(8,128)(2,1)}, bf16[68,16,1088]{2,1,0:T(8,128)(2,1)}, f32[1,1088]{1,0:T(1,128)}, f3...) custom-call(bf16[512,1088]{1,0:T(8,128)(2,1)} %get-tuple-element.128.refs_0_, ...), custom_call_target="tpu_custom_call" | custom-call | tf_op jit(solution)/shard_map/attend_back/pallas_call | solution.py:1984
  707.7 1.2 fusion.2
  708.9 1.3 fusion
  710.3 1.1 slice_dynamic-update-slice_fusion
  711.5 0.9 slice_dynamic-update-slice_fusion.2
  712.5 1.6 pad.22.refs_2_
  714.1 94.7 %reduce_grads.1 = (bf16[17,16,1088]{2,1,0:T(8,128)(2,1)}, bf16[17,16,3264]{2,1,0:T(8,128)(2,1)}, bf16[16,16,1088]{2,1,0:T(8,128)(2,1)}, bf16[512,1088]{1,0:T(8,128)(2,1)}) custom-call(bf16[4,17,16,1088]{3,2,1,0:T(8,128)(2,1)} %bitcast.72, bf16[4,17,16,3264]{3,2,1,0:T(8,128)(2,1)} %bitcast.61, bf16[4,16,16,1088]{3,2,1,0:T(8,128)(2,1)} %pad.22.refs_2_, ...), custom_call_target="tpu_custom_call" | custom-call | tf_op jit(solution)/shard_map/reduce_grads/pallas_call | solution.py:2011
  808.8 14.9 %assemble.1 = (f32[2,68,16,1088]{3,2,1,0:T(8,128)}, f32[2,17,16,4352]{3,2,1,0:T(8,128)}, f32[2,17,16,1088]{3,2,1,0:T(8,128)}, f32[2,17,16,3264]{3,2,1,0:T(8,128)...) custom-call(bf16[68,16,1088]{2,1,0:T(8,128)(2,1)} %get-tuple-element, ...), custom_call_target="tpu_custom_call" | custom-call | tf_op jit(solution)/shard_map/assemble/pallas_call | solution.py:2077
  823.7 1.4 copy.48
  825.1 1.4 copy.47
  (91 shorter events, 8.0 us)
Async XLA Ops:
  0.6 2.5 copy-start.2
  0.7 3.9 copy-start.9
  0.7 4.0 copy-start.10
  0.7 4.0 copy-start.11
  0.7 4.0 copy-start.12
  0.7 4.1 copy-start.13
  0.7 4.1 copy-start.14
  0.7 4.1 copy-start.15
  0.7 4.1 copy-start.16
  0.7 4.1 copy-start.17
  366.9 89.7 %copy-start.3 = (f32[1,4352]{1,0:T(1,128)S(1)}, f32[1,4352]{1,0:T(1,128)}, u32[]{:S(2)}) copy-start(f32[1,4352]{1,0:T(1,128)} %get-tuple-element.145) | copy-start | bytes 52228
  619.6 87.2 %copy-start.4 = (f32[1,4352]{1,0:T(1,128)S(1)}, f32[1,4352]{1,0:T(1,128)}, u32[]{:S(2)}) copy-start(f32[1,4352]{1,0:T(1,128)} %get-tuple-element.167) | copy-start | bytes 52228
  619.6 87.3 %copy-start.8 = (f32[1,1088]{1,0:T(1,128)S(1)}, f32[1,1088]{1,0:T(1,128)}, u32[]{:S(2)}) copy-start(f32[1,1088]{1,0:T(1,128)} %get-tuple-element.163) | copy-start | bytes 13060
  619.6 87.5 %copy-start.7 = (f32[1,1088]{1,0:T(1,128)S(1)}, f32[1,1088]{1,0:T(1,128)}, u32[]{:S(2)}) copy-start(f32[1,1088]{1,0:T(1,128)} %get-tuple-element.164) | copy-start | bytes 13060
  619.6 87.6 %copy-start.6 = (f32[1,1088]{1,0:T(1,128)S(1)}, f32[1,1088]{1,0:T(1,128)}, u32[]{:S(2)}) copy-start(f32[1,1088]{1,0:T(1,128)} %get-tuple-element.165) | copy-start | bytes 13060
  619.7 87.7 %copy-start.5 = (f32[1,1088]{1,0:T(1,128)S(1)}, f32[1,1088]{1,0:T(1,128)}, u32[]{:S(2)}) copy-start(f32[1,1088]{1,0:T(1,128)} %get-tuple-element.166) | copy-start | bytes 13060
  808.8 14.9 %copy-start.1 = (bf16[512,1088]{1,0:T(8,128)(2,1)S(1)}, bf16[512,1088]{1,0:T(8,128)(2,1)}, u32[]{:S(2)}) copy-start(bf16[512,1088]{1,0:T(8,128)(2,1)} %get-tuple-element.169) | copy-start | bytes 3342340
  823.7 1.4 copy-start

commit v6 on v5

--- a/solution.py
+++ b/solution.py
@@ -424,7 +424,6 @@
 LEAD = 3
 GAP = 2
 TILE = 512
-REDUCE_PACE = 6
 SKEW = 2
 AHEAD = 6
 
@@ -1455,12 +1454,12 @@
     return reduce_steps(place, groups, *lists, *refs[6 * n : 6 * n + 4])
 
 
-def spread_steps(work, comm, finish):
+def spread_steps(work, comm, finish, pace):
     done = {True}
     blocked = None
     for made in work:
         done.add(made)
-        for _ in range(REDUCE_PACE):
+        for _ in range(pace):
             if blocked is not None and blocked not in done:
                 break
             blocked = next(comm, True)
@@ -1520,11 +1519,11 @@
     return place
 
 
-def spec_of(shapes):
+def spec_of(shapes, narrow, wide):
     spec = []
     for m, shape in enumerate(shapes):
         k = shape[1] // 8
-        split = min(k, 1 if shape[3] > 2048 else 2)
+        split = min(k, wide if shape[3] > 2048 else narrow)
         for base in range(0, k, split):
             spec.append((m, base * 8, split))
     return spec
@@ -1666,7 +1665,7 @@
     yield made_down
 
     loads[2].wait()
-    for low, high in each(0, down_n, 4):
+    for low, high in each(0, down_n, 2):
         down_run(low, high)
         yield
     out_begin()
@@ -1720,7 +1719,7 @@
         + [pltpu.VMEM((rows, width), low)] * 4
         + [
             pltpu.VMEM((width, rows), low),
-            pltpu.VMEM((2, 16, 16, width), low),
+            pltpu.VMEM((2, 32, 16, width), low),
             pltpu.VMEM((2, 16, 16, ff), low),
             pltpu.VMEM((2, rows, 512), low),
             pltpu.VMEM((2, 32, 16, width), low),
@@ -1822,7 +1821,7 @@
 
         if i >= 2:
             row_send(tiles_ref, sem, target, i - 2).wait()
-        tiles_between(0, right.shape[1], BLOCK, act)
+        tiles_between(0, right.shape[1], TILE, act)
         row_send(tiles_ref, sem, target, i).start()
 
     def row_send(tiles_ref, sem, target, i):
@@ -1912,7 +1911,7 @@
     work_refs = mlp_refs(rows, width, ff)
     n, extra = len(work_out), len(grads)
     shapes = [g.shape for g in grads] + [down_shape]
-    spec = spec_of(shapes)
+    spec = spec_of(shapes, 4, 2)
 
     def body(*refs):
         i = len(ins) + extra
@@ -1924,7 +1923,7 @@
             place, spec, list(refs[len(ins) : i]) + [down_rows], more, rest[len(work_refs) :], (extra,)
         )
         work = mlp_work(layer, refs[: len(ins)], outs, rest[: len(work_refs)], extra)
-        spread_steps(work, comm, finish)
+        spread_steps(work, comm, finish, 6 if extra else 3)
 
     outs = pl.pallas_call(
         body,
@@ -1964,7 +1963,7 @@
     work_refs = attend_refs(rows, width)
     ships = [ship] if ship is not None else []
     n, extra, k = len(work_out), len(grads), len(ships)
-    spec = spec_of([g.shape for g in grads])
+    spec = spec_of([g.shape for g in grads], 2, 1)
     buffers = reduce_scratch([(depth, grads[m].shape[2:]) for m, _, depth in spec])
 
     def body(*refs):
@@ -1977,7 +1976,7 @@
             start()
         comm, finish = take_reduce(place, spec, refs[len(ins) : i - k], more, rest[len(work_refs) :])
         work = attend_work(layer, place, refs[: len(ins)], outs, rest[: len(work_refs)])
-        spread_steps(work, comm, finish)
+        spread_steps(work, comm, finish, 6)
         if k:
             wait()
 
@@ -1997,7 +1996,7 @@
 
 def reduce_kernel(grads, ship):
     extra = len(grads)
-    spec = spec_of([g.shape for g in grads])
+    spec = spec_of([g.shape for g in grads], 2, 1)
 
     def body(*refs):
         place = meet(True)
@@ -2005,7 +2004,7 @@
         start, wait = ship_moves(place, refs[extra], refs[2 * extra + 1], *rest[-3:])
         start()
         comm, finish = take_reduce(place, spec, refs[:extra], refs[extra + 1 : 2 * extra + 1], rest)
-        spread_steps((), comm, finish)
+        spread_steps((), comm, finish, 1)
         wait()
 
     outs = pl.pallas_call(

time: 833 us -> 802 us (0.963)
  Pallas kernels: 796 us -> 766 us
    pallas_call x2, Pallas kernels: 255 us -> 234 us  [mlp_kernel(): pl.pallas_call(body, out_shape=work_out + [shaped(shape[1:], low) for sha...]
where the time goes in v6:
time: 802 us; the launch traced here: 797 us
  Pallas kernels  766 us (96%)
  local copies, waits for them, and re-layouts  23.6 us (3%)
    pallas_call x1, Pallas kernels, forward(): pl.pallas_call(forward_body, out_shape=out_shape, in_specs=anywhere(4 + l...  259 us
    pallas_call x2, Pallas kernels, mlp_kernel(): pl.pallas_call(body, out_shape=work_out + [shaped(shape[1:], low) for sha...  234 us
    pallas_call x2, Pallas kernels, attend_kernel(): pl.pallas_call(body, out_shape=work_out + [shaped(g.shape[1:], low) for g...  164 us
    pallas_call x1, Pallas kernels, reduce_kernel(): pl.pallas_call(body, out_shape=[shaped(g.shape[1:], g.dtype) for g in gra...  93.4 us

profile of v6, /device:TPU:25, one launch (start us, length us, event | category | flops | bytes accessed | tf_op | source)
XLA Modules:
  0.0 797.1 jit_solution(2908539451248472846)
XLA Ops:
  0.7 2.4 copy.35
  3.2 1.4 copy.36
  5.6 259.4 %forward.1 = (bf16[2,4,17,16,3264]{4,3,2,1,0:T(8,128)(2,1)}, bf16[2,4,17,16,1088]{4,3,2,1,0:T(8,128)(2,1)}, bf16[2,4,17,16,4352]{4,3,2,1,0:T(8,128)(2,1)}, bf16[...) custom-call(bf16[512,1088]{1,0:T(8,128)(2,1)} %bitcast.66, ...), custom_call_target="tpu_custom_call" | custom-call | tf_op jit(solution)/shard_map/forward/pallas_call | solution.py:1203
  265.0 1.5 slice_bitcast_fusion
  266.5 92.2 %mlp_back.2 = (f32[512,1088]{1,0:T(8,128)}, bf16[512,1088]{1,0:T(8,128)(2,1)}, bf16[512,1088]{1,0:T(8,128)(2,1)}, bf16[68,16,4352]{2,1,0:T(8,128)(2,1)}, bf16[27...) custom-call(bf16[512,1088]{1,0:T(8,128)(2,1)} %get-tuple-element.105, ...), custom_call_target="tpu_custom_call" | custom-call | tf_op jit(solution)/shard_map/mlp_back/pallas_call | solution.py:1928
  358.7 0.7 convert_reduce_fusion.10
  359.6 0.7 convert_reduce_fusion.12
  360.5 83.8 %attend_back.2 = (f32[512,1088]{1,0:T(8,128)}, bf16[68,16,3264]{2,1,0:T(8,128)(2,1)}, bf16[68,16,1088]{2,1,0:T(8,128)(2,1)}, f32[1,1088]{1,0:T(1,128)}, f32[1,10...) custom-call(bf16[512,1088]{1,0:T(8,128)(2,1)} %get-tuple-element.104, ...), custom_call_target="tpu_custom_call" | custom-call | tf_op jit(solution)/shard_map/attend_back/pallas_call | solution.py:1983
  446.6 1.2 fusion.3
  447.8 1.3 fusion.1
  449.2 1.1 slice_dynamic-update-slice_fusion.1
  450.4 0.9 slice_dynamic-update-slice_fusion.3
  451.4 1.6 pad.20.refs_11_
  453.0 142.2 %mlp_back.3 = (f32[512,1088]{1,0:T(8,128)}, bf16[512,1088]{1,0:T(8,128)(2,1)}, bf16[512,1088]{1,0:T(8,128)(2,1)}, bf16[68,16,4352]{2,1,0:T(8,128)(2,1)}, bf16[27...) custom-call(f32[512,1088]{1,0:T(8,128)} %get-tuple-element.129.refs_, ...), custom_call_target="tpu_custom_call" | custom-call | tf_op jit(solution)/shard_map/mlp_back/pallas_call | solution.py:1928
  595.3 80.0 %attend_back.3 = (bf16[512,1088]{1,0:T(8,128)(2,1)}, bf16[68,16,3264]{2,1,0:T(8,128)(2,1)}, bf16[68,16,1088]{2,1,0:T(8,128)(2,1)}, f32[1,1088]{1,0:T(1,128)}, f3...) custom-call(bf16[512,1088]{1,0:T(8,128)(2,1)} %get-tuple-element.128.refs_0_, ...), custom_call_target="tpu_custom_call" | custom-call | tf_op jit(solution)/shard_map/attend_back/pallas_call | solution.py:1983
  679.4 1.2 fusion.2
  680.6 1.3 fusion
  682.0 1.1 slice_dynamic-update-slice_fusion
  683.2 0.9 slice_dynamic-update-slice_fusion.2
  684.2 1.6 pad.22.refs_2_
  685.8 93.4 %reduce_grads.1 = (bf16[17,16,1088]{2,1,0:T(8,128)(2,1)}, bf16[17,16,3264]{2,1,0:T(8,128)(2,1)}, bf16[16,16,1088]{2,1,0:T(8,128)(2,1)}, bf16[512,1088]{1,0:T(8,128)(2,1)}) custom-call(bf16[4,17,16,1088]{3,2,1,0:T(8,128)(2,1)} %bitcast.72, bf16[4,17,16,3264]{3,2,1,0:T(8,128)(2,1)} %bitcast.61, bf16[4,16,16,1088]{3,2,1,0:T(8,128)(2,1)} %pad.22.refs_2_, ...), custom_call_target="tpu_custom_call" | custom-call | tf_op jit(solution)/shard_map/reduce_grads/pallas_call | solution.py:2010
  779.2 14.9 %assemble.1 = (f32[2,68,16,1088]{3,2,1,0:T(8,128)}, f32[2,17,16,4352]{3,2,1,0:T(8,128)}, f32[2,17,16,1088]{3,2,1,0:T(8,128)}, f32[2,17,16,3264]{3,2,1,0:T(8,128)...) custom-call(bf16[68,16,1088]{2,1,0:T(8,128)(2,1)} %get-tuple-element, ...), custom_call_target="tpu_custom_call" | custom-call | tf_op jit(solution)/shard_map/assemble/pallas_call | solution.py:2076
  794.1 1.4 copy.48
  795.5 1.4 copy.47
  (91 shorter events, 8.0 us)
Async XLA Ops:
  0.6 2.5 copy-start.2
  0.7 3.9 copy-start.9
  0.7 4.0 copy-start.10
  0.7 4.0 copy-start.11
  0.7 4.0 copy-start.12
  0.7 4.1 copy-start.13
  0.7 4.1 copy-start.14
  0.7 4.1 copy-start.15
  0.7 4.1 copy-start.16
  0.7 4.1 copy-start.17
  360.5 85.7 %copy-start.3 = (f32[1,4352]{1,0:T(1,128)S(1)}, f32[1,4352]{1,0:T(1,128)}, u32[]{:S(2)}) copy-start(f32[1,4352]{1,0:T(1,128)} %get-tuple-element.145) | copy-start | bytes 52228
  595.2 83.3 %copy-start.4 = (f32[1,4352]{1,0:T(1,128)S(1)}, f32[1,4352]{1,0:T(1,128)}, u32[]{:S(2)}) copy-start(f32[1,4352]{1,0:T(1,128)} %get-tuple-element.167) | copy-start | bytes 52228
  595.2 83.4 %copy-start.8 = (f32[1,1088]{1,0:T(1,128)S(1)}, f32[1,1088]{1,0:T(1,128)}, u32[]{:S(2)}) copy-start(f32[1,1088]{1,0:T(1,128)} %get-tuple-element.163) | copy-start | bytes 13060
  595.2 83.6 %copy-start.7 = (f32[1,1088]{1,0:T(1,128)S(1)}, f32[1,1088]{1,0:T(1,128)}, u32[]{:S(2)}) copy-start(f32[1,1088]{1,0:T(1,128)} %get-tuple-element.164) | copy-start | bytes 13060
  595.3 83.7 %copy-start.6 = (f32[1,1088]{1,0:T(1,128)S(1)}, f32[1,1088]{1,0:T(1,128)}, u32[]{:S(2)}) copy-start(f32[1,1088]{1,0:T(1,128)} %get-tuple-element.165) | copy-start | bytes 13060
  595.3 83.8 %copy-start.5 = (f32[1,1088]{1,0:T(1,128)S(1)}, f32[1,1088]{1,0:T(1,128)}, u32[]{:S(2)}) copy-start(f32[1,1088]{1,0:T(1,128)} %get-tuple-element.166) | copy-start | bytes 13060
  779.2 14.9 %copy-start.1 = (bf16[512,1088]{1,0:T(8,128)(2,1)S(1)}, bf16[512,1088]{1,0:T(8,128)(2,1)}, u32[]{:S(2)}) copy-start(bf16[512,1088]{1,0:T(8,128)(2,1)} %get-tuple-element.169) | copy-start | bytes 3342340
  794.1 1.4 copy-start
